TPU v7x, 32 devices: a whole 2x2x4 slice. The times are simulated.
32 devices in a mesh: groups: 2 (over x), gz: 16 (over z, y, core).
Axes of the slice: x: 2, y: 2, z: 4, core: 2. Of those that a mesh axis runs over, the one named last changes fastest.
Arguments:
- e_field: float32 [3, 32, 384, 256], P(None, 'gz', 'groups'), parts along dimension 2, may hold values from -6 to 6
- h_field: float32 [3, 32, 384, 256], P(None, 'gz', 'groups'), parts along dimension 2, may hold values from -6 to 6
- forward_field: float32 [3, 32, 384, 256], P(None, 'gz', 'groups'), parts along dimension 2, may hold values from -6 to 6
- permittivity: float32 [32, 384, 256], P('gz', 'groups'), parts along dimension 1, may hold values from 1 to 4
- conductivity: float32 [32, 384, 256], P('gz', 'groups'), parts along dimension 1, may hold values from 0.05 to 1
- owners: int32 [4096, 2], P('gz', 'groups'), parts along dimension 1, may hold values from 0 to 15; in each aligned block of 256 rows (0 to 255, 256 to 511, ...) at most 32 rows name the same one
- cells: int32 [4096, 2], P('gz', 'groups'), parts along dimension 1, may hold values from 0 to 98303
- amplitude: float32 [6, 4096], P('groups', 'gz'), parts along dimension 0, may hold values from -24 to 24
- timing: float32 [4, 2], P('groups'), parts along dimension 0, may hold values from 0.5 to 1.5
- bounds: int32 [6, 2], P('groups'), parts along dimension 0, may hold values from 0 to 256, as said below
Outputs:
- e_out: float32 [3, 32, 384, 256], P(None, 'gz', 'groups'), parts along dimension 2
- h_out: float32 [3, 32, 384, 256], P(None, 'gz', 'groups'), parts along dimension 2
- gradient: float32 [32, 384, 256], P('gz', 'groups'), parts along dimension 1
There are 2 independent parts, one for each index of `groups`. A program takes and returns all parts, laid end to end along the dimension named above; each array names one. Nothing has to cross between parts.
Inputs may be any that keep to these rules, and one draw needn't show every extreme that they name: `owners`: in the rows of one device no slab is named by more than 32 entries, a bound that some block reaches. `cells`: entries may name the same cell; they add. `bounds`: along each dimension of n cells the lower bound lies in 0 .. n // 4 and the upper in n - n // 4 .. n.
All inputs are finite; a program needn't handle non-finite values.
Results may differ from a plain program's by a relative error of at most 0.0001.
Values sent between devices are 32-bit elements; how exact they have to be, the bound alone decides.
No kernel may reach another device: no remote copies, remote signals or barrier semaphores. Data moves between devices by JAX's collectives and lax.ppermute only.
A program may use at most 256 MiB of HBM per device.

v0:
```python
import jax
import jax.numpy as jnp
from jax import lax
from jax.sharding import PartitionSpec as P

STEPS = 2


def passed_along(x, axis, by):
    peers = lax.axis_size(axis)
    pairs = [(i, i + by) for i in range(peers) if 0 <= i + by < peers]
    return lax.ppermute(x, axis, pairs)


def ahead(field, axis, top):
    upper = lax.slice_in_dim(field, 1, field.shape[axis], axis=axis)
    return jnp.concatenate([upper, top], axis=axis) - field


def behind(field, axis, bottom):
    lower = lax.slice_in_dim(field, 0, field.shape[axis] - 1, axis=axis)
    return field - jnp.concatenate([bottom, lower], axis=axis)


def zero_layer(field, axis):
    return jnp.zeros_like(lax.slice_in_dim(field, 0, 1, axis=axis))


def curl_ahead(efield, top_x, top_y):
    ex, ey, ez = (efield[0], efield[1], efield[2])
    cx = ahead(ez, 2, zero_layer(ez, 2)) - ahead(ey, 0, top_y)
    cy = ahead(ex, 0, top_x) - ahead(ez, 1, zero_layer(ez, 1))
    cz = ahead(ey, 1, zero_layer(ey, 1)) - ahead(ex, 2, zero_layer(ex, 2))
    return jnp.stack([cx, cy, cz])


def curl_behind(hfield, bottom_x, bottom_y):
    hx, hy, hz = (hfield[0], hfield[1], hfield[2])
    cx = behind(hz, 2, zero_layer(hz, 2)) - behind(hy, 0, bottom_y)
    cy = behind(hx, 0, bottom_x) - behind(hz, 1, zero_layer(hz, 1))
    cz = behind(hy, 1, zero_layer(hy, 1)) - behind(hx, 2, zero_layer(hx, 2))
    return jnp.stack([cx, cy, cz])


def local(
    e_field,
    h_field,
    forward_field,
    permittivity,
    conductivity,
    owners,
    cells,
    amplitude,
    timing,
    bounds,
):
    slab_z, width_x, width_y = permittivity.shape
    owner_ids = owners[:, 0]
    cell_ids = cells[:, 0]
    payload = jnp.concatenate(
        [amplitude, owner_ids[None, :].astype(jnp.float32), cell_ids[None, :].astype(jnp.float32)],
        axis=0,
    )
    everything = lax.all_gather(payload, "gz", axis=1, tiled=True)
    mine = (everything[3].astype(jnp.int32) == lax.axis_index("gz")).astype(jnp.float32)
    values = everything[0:3] * mine[None, :]
    targets = everything[4].astype(jnp.int32)
    source = jnp.zeros((3, slab_z * width_x * width_y), jnp.float32).at[:, targets].add(values)
    source = source.reshape(3, slab_z, width_x, width_y)
    loss = conductivity / (2.0 * permittivity)
    coef_a = (1.0 - loss) / (1.0 + loss)
    coef_b = 0.5 / (permittivity * (1.0 + loss))
    zpos = (lax.axis_index("gz") * slab_z + jnp.arange(slab_z, dtype=jnp.int32))[:, None, None]
    xpos = jnp.arange(width_x, dtype=jnp.int32)[None, :, None]
    ypos = jnp.arange(width_y, dtype=jnp.int32)[None, None, :]
    inside = (
        (zpos >= bounds[0, 0])
        & (zpos < bounds[0, 1])
        & (xpos >= bounds[1, 0])
        & (xpos < bounds[1, 1])
        & (ypos >= bounds[2, 0])
        & (ypos < bounds[2, 1])
    )
    mask = inside.astype(jnp.float32)
    gradient = jnp.zeros((slab_z, width_x, width_y), jnp.float32)
    efield, hfield = (e_field, h_field)
    for step in range(STEPS):
        upper = passed_along(efield[0:2, 0:1], "gz", -1)
        hfield = hfield - 0.5 * curl_ahead(efield, upper[0], upper[1])
        lower = passed_along(hfield[0:2, slab_z - 1 : slab_z], "gz", 1)
        efield = coef_a * efield + coef_b * (
            curl_behind(hfield, lower[0], lower[1]) - timing[0, step] * source
        )
        gradient = gradient + timing[1, step] * mask * jnp.sum(efield * forward_field, axis=0)
    return (efield, hfield, gradient)


def solution(mesh):
    placed = (
        P(None, "gz", "groups", None),
        P(None, "gz", "groups", None),
        P(None, "gz", "groups", None),
        P("gz", "groups", None),
        P("gz", "groups", None),
        P("gz", "groups"),
        P("gz", "groups"),
        P("groups", "gz"),
        P("groups", None),
        P("groups", None),
    )
    return jax.shard_map(
        local,
        mesh=mesh,
        in_specs=placed,
        out_specs=(
            P(None, "gz", "groups", None),
            P(None, "gz", "groups", None),
            P("gz", "groups", None),
        ),
        check_vma=False,
    )
```

profile of v0, /device:TPU:1, one launch (start us, length us, event | category | flops | bytes accessed | tf_op | source)
XLA Modules:
  0.0 220.9 jit_solution(14392034642963617361)
XLA Ops:
  0.6 1.9 slice.219
  2.5 2.0 collective-permute-start
  4.5 1.8 slice_bitcast_fusion.27
  7.0 23.3 %all_gather.3 = f32[5,4096]{1,0:T(8,128)S(1)} all-gather(f32[5,256]{1,0:T(8,128)S(1)} %pad_maximum_fusion), channel_id=1, replica_groups=mesh['groups'=2,'gz'=16] {'gz'}, dimensions={1}, use_global_device_ids=true | all-gather | bytes 87040 | tf_op jit(solution)/shard_map/all_gather | solution.py:64
  30.4 2.0 copy.16
  33.7 1.2 iota_compare_fusion.2
  35.0 42.4 %scatter_custom_fusion = f32[3,98304]{0,1:T(8,128)} fusion(s32[4096]{0:T(1024)S(1)} %bitcast.171, f32[4096,3]{1,0:T(8,128)} %copy.16, f32[]{:T(128)} %constant.11.clone.1), kind=kCustom, calls=%fused_computation.2 | custom fusion | flops 12288 | bytes 1180160 | tf_op jit(solution)/shard_map/scatter-add | solution.py:68
  77.4 49.7 %broadcast_multiply_fusion = (f32[3,98304]{0,1:T(8,128)}, f32[3,98304]{0,1:T(8,128)}) fusion(f32[3,98304]{0,1:T(8,128)} %scatter_custom_fusion, f32[]{:T(128)} %bitcast.48, f32[]{:T(128)} %bitcast.20), kind=kLoop, calls=%fused_computation.1 | loop fusion | flops 589824 | bytes 3538952 | tf_op jit(solution)/shard_map/mul | solution.py:92
  127.2 1.2 compare_and_fusion
  130.1 27.1 %copy.17 = f32[3,2,192,256]{3,2,1,0:T(8,128)S(1)} copy(f32[3,2,192,256]{0,3,2,1:T(8,128)} %bitcast.161) | data formatting | bytes 2359296 | tf_op jit(solution)/shard_map/mul | solution.py:92
  157.2 0.9 slice.289
  158.9 27.1 %copy.18 = f32[3,2,192,256]{3,2,1,0:T(8,128)S(1)} copy(f32[3,2,192,256]{0,3,2,1:T(8,128)} %bitcast.160) | data formatting | bytes 2359296 | tf_op jit(solution)/shard_map/mul | solution.py:92
  186.0 1.2 iota_compare_fusion
  187.3 1.4 subtract_divide_fusion
  188.7 1.0 slice_bitcast_fusion.25
  190.1 1.0 copy-done.2
  191.3 1.9 collective-permute-start.1
  193.3 4.6 %collective-permute-done.1 = f32[2,1,192,256]{3,2,1,0:T(8,128)S(1)} collective-permute-done((f32[2,1,192,256]{3,2,1,0:T(8,128)S(1)}, f32[2,1,192,256]{3,2,1,0:T(8,128)S(1)}, u32[]{:S(2)}, u32[]{:S(2)}) %collective-permute-start.1) | collective-permute-done | bytes 393248 | tf_op jit(solution)/shard_map/ppermute | solution.py:12
  198.7 1.9 collective-permute-start.2
  201.2 7.4 %collective-permute-done.2 = f32[2,1,192,256]{3,2,1,0:T(8,128)S(1)} collective-permute-done((f32[2,1,192,256]{3,2,1,0:T(8,128)S(1)}, f32[2,1,192,256]{3,2,1,0:T(8,128)S(1)}, u32[]{:S(2)}, u32[]{:S(2)}) %collective-permute-start.2) | collective-permute-done | bytes 393248 | tf_op jit(solution)/shard_map/ppermute | solution.py:12
  209.2 1.9 collective-permute-start.3
  211.3 4.5 %collective-permute-done.3 = f32[2,1,192,256]{3,2,1,0:T(8,128)S(1)} collective-permute-done((f32[2,1,192,256]{3,2,1,0:T(8,128)S(1)}, f32[2,1,192,256]{3,2,1,0:T(8,128)S(1)}, u32[]{:S(2)}, u32[]{:S(2)}) %collective-permute-start.3) | collective-permute-done | bytes 393248 | tf_op jit(solution)/shard_map/ppermute | solution.py:12
  217.1 1.5 multiply_reduce_fusion.1
  218.6 2.3 %multiply_add_fusion = f32[2,192,256]{2,1,0:T(8,128)} fusion(f32[2,192,256]{2,1,0:T(8,128)S(1)} %get-tuple-element.4, f32[2,192,256]{2,1,0:T(8,128)S(1)} %get-tuple-element.3, f32[]{:T(128)} %bitcast.57, f32[]{:T(128)} %bitcast.56, pred[256]{0:T(512)(128)(4,1)S(1)} %get-tuple-element.64, pred[256]{0:T(512)(128)(4,1)S(1)} %get-tuple-element.65, ...), kind=kLoop, calls=%fused_computation.50 | loop fusion | flops 688128 | bytes 1180552 | tf_op jit(solution)/shard_map/add | solution.py:94
  (65 shorter events, 8.6 us)
Async XLA Ops:
  0.6 5.7 %copy-start = (f32[3,2,192,256]{3,2,1,0:T(8,128)S(1)}, f32[3,2,192,256]{3,2,1,0:T(8,128)}, u32[]{:S(2)}) copy-start(f32[3,2,192,256]{3,2,1,0:T(8,128)} %param.10) | copy-start | bytes 3538948
  2.5 186.2 %collective-permute-start = (f32[2,1,192,256]{3,2,1,0:T(8,128)}, f32[2,1,192,256]{3,2,1,0:T(8,128)}, u32[]{:S(2)}, u32[]{:S(2)}) collective-permute-start(f32[2,1,192,256]{3,2,1,0:T(8,128)} %slice.219), channel_id=1, source_target_pairs={{1,0},{2,1},{3,2},{4,3},{5,4},{6,5},{7,6},{8,7},{9,8},{10,9},{11,1... | collective-permute-start | bytes 1179656 | tf_op jit(solution)/shard_map/ppermute | solution.py:12
  6.3 0.7 copy-start.13
  6.3 0.7 copy-start.14
  6.3 0.7 copy-start.11
  30.3 2.1 copy-start.12
  30.3 2.7 %copy-start.10 = (s32[3,2]{0,1:T(2,128)S(1)}, s32[3,2]{0,1:T(2,128)}, u32[]{:S(2)}) copy-start(s32[3,2]{0,1:T(2,128)} %param.19) | copy-start | bytes 76
  187.2 2.5 %copy-start.3 = (f32[2,192,255]{2,1,0:T(8,128)S(1)}, f32[2,192,255]{2,1,0:T(8,128)}, u32[]{:S(2)}) copy-start(f32[2,192,255]{2,1,0:T(8,128)} %slice.284) | copy-start | bytes 1175044
  187.2 2.5 %copy-start.4 = (f32[2,191,256]{2,1,0:T(8,128)S(1)}, f32[2,191,256]{2,1,0:T(8,128)}, u32[]{:S(2)}) copy-start(f32[2,191,256]{2,1,0:T(8,128)} %slice.287) | copy-start | bytes 1173508
  187.2 2.5 %copy-start.5 = (f32[2,192,255]{2,1,0:T(8,128)S(1)}, f32[2,192,255]{2,1,0:T(8,128)}, u32[]{:S(2)}) copy-start(f32[2,192,255]{2,1,0:T(8,128)} %slice.289) | copy-start | bytes 1175044
  187.3 2.5 %copy-start.6 = (f32[2,191,256]{2,1,0:T(8,128)S(1)}, f32[2,191,256]{2,1,0:T(8,128)}, u32[]{:S(2)}) copy-start(f32[2,191,256]{2,1,0:T(8,128)} %slice.288) | copy-start | bytes 1173508
  187.3 2.5 %copy-start.8 = (f32[1,192,256]{2,1,0:T(8,128)S(1)}, f32[1,192,256]{2,1,0:T(8,128)}, u32[]{:S(2)}) copy-start(f32[1,192,256]{2,1,0:T(8,128)} %get-tuple-element.35) | copy-start | bytes 589828
  187.3 2.5 %copy-start.9 = (f32[1,192,256]{2,1,0:T(8,128)S(1)}, f32[1,192,256]{2,1,0:T(8,128)}, u32[]{:S(2)}) copy-start(f32[1,192,256]{2,1,0:T(8,128)} %get-tuple-element.36) | copy-start | bytes 589828
  189.8 1.3 copy-start.2
  191.3 6.6 %collective-permute-start.1 = (f32[2,1,192,256]{3,2,1,0:T(8,128)S(1)}, f32[2,1,192,256]{3,2,1,0:T(8,128)S(1)}, u32[]{:S(2)}, u32[]{:S(2)}) collective-permute-start(f32[2,1,192,256]{3,2,1,0:T(8,128)S(1)} %slice.293), channel_id=1, source_target_pairs={{0,1},{1,2},{2,3},{3,4},{4,5},{5,6},{6,7},{7,8},{8,9},{9,10},{10,1... | collective-permute-start | bytes 1179656 | tf_op jit(solution)/shard_map/ppermute | solution.py:12
  198.7 9.8 %collective-permute-start.2 = (f32[2,1,192,256]{3,2,1,0:T(8,128)S(1)}, f32[2,1,192,256]{3,2,1,0:T(8,128)S(1)}, u32[]{:S(2)}, u32[]{:S(2)}) collective-permute-start(f32[2,1,192,256]{3,2,1,0:T(8,128)S(1)} %slice.308), channel_id=1, source_target_pairs={{1,0},{2,1},{3,2},{4,3},{5,4},{6,5},{7,6},{8,7},{9,8},{10,9},{11,1... | collective-permute-start | bytes 1179656 | tf_op jit(solution)/shard_map/ppermute | solution.py:12
  209.1 6.7 %copy-start.1 = (f32[3,2,192,256]{3,2,1,0:T(8,128)}, f32[3,2,192,256]{3,2,1,0:T(8,128)S(1)}, u32[]{:S(2)}) copy-start(f32[3,2,192,256]{3,2,1,0:T(8,128)S(1)} %fusion.5) | copy-start | bytes 3538948
  209.2 6.6 %collective-permute-start.3 = (f32[2,1,192,256]{3,2,1,0:T(8,128)S(1)}, f32[2,1,192,256]{3,2,1,0:T(8,128)S(1)}, u32[]{:S(2)}, u32[]{:S(2)}) collective-permute-start(f32[2,1,192,256]{3,2,1,0:T(8,128)S(1)} %slice.320), channel_id=1, source_target_pairs={{0,1},{1,2},{2,3},{3,4},{4,5},{5,6},{6,7},{7,8},{8,9},{9,10},{10,1... | collective-permute-start | bytes 1179656 | tf_op jit(solution)/shard_map/ppermute | solution.py:12
  215.8 1.3 copy-start.7
where the time goes:
time: 222 us; the launch traced here: 221 us
  other arithmetic  103 us (46%)
  local copies, waits for them, and re-layouts  69.1 us (31%)
  blocking collectives  23.3 us (10%)
  waiting for transfers between devices  16.5 us (7%)
  starting transfers between devices  7.72 us (3%)
    mul x2, local copies, waits for them, and re-layouts, local(): timing[0, step] * source  54.2 us
    mul x1, other arithmetic, local(): timing[0, step] * source  49.7 us
    scatter-add x1, other arithmetic, local(): jnp.zeros((3, slab_z * width_x * width_y), jnp.float32).at[:, targets]  42.4 us
    all_gather x1, blocking collectives, local(): everything = lax.all_gather(payload, 'gz', axis=1, tiled=True)  23.3 us
    ppermute x4, waiting for transfers between devices, passed_along(): return lax.ppermute(x, axis, pairs)  16.5 us
    ppermute x4, starting transfers between devices, passed_along(): return lax.ppermute(x, axis, pairs)  7.72 us
    slice x10, local copies, waits for them, and re-layouts, ahead(): upper = lax.slice_in_dim(field, 1, field.shape[axis], axis=axis)  5.6 us
  transfers between devices with their start and end apart: 4, of which 3 were waited for; matrix products, arithmetic and copies ran while one was open for 73% of the time, Pallas kernels for 0%

commit v1 on v0

v1 whole, which is shorter than its diff:
```python
import functools

import jax
import jax.numpy as jnp
from jax import lax
from jax.experimental import pallas as pl
from jax.experimental.pallas import tpu as pltpu
from jax.sharding import PartitionSpec as P

STEPS = 2
ROWS = 24
LANES = 128
HALF = 0.5
F32 = jnp.float32
BF16 = jnp.bfloat16
VMEM = pltpu.VMEM
SMEM = pltpu.SMEM


def lanes_of(v):
    return lax.broadcasted_iota(jnp.int32, v.shape, 1)


def ahead_y(v):
    last = v.shape[1] - 1
    return jnp.where(lanes_of(v) < last, pltpu.roll(v, last, axis=1), 0.0) - v


def behind_y(v):
    return v - jnp.where(lanes_of(v) > 0, pltpu.roll(v, 1, axis=1), 0.0)


class Chunk:
    def __init__(self, at, size, width_x):
        self.at, self.size, self.width = at, size, width_x

    def get(self, ref, *index):
        return ref[(*index, pl.ds(self.at, self.size), slice(None))]

    def put(self, ref, *index_and_value):
        *index, value = index_and_value
        ref[(*index, pl.ds(self.at, self.size), slice(None))] = value

    def ahead_x(self, ref, *index):
        here = self.get(ref, *index)
        after = pl.multiple_of(jnp.minimum(self.at + self.size, self.width - 8), 8)
        more = ref[(*index, pl.ds(after, 8), slice(None))]
        more = jnp.where(self.at + self.size < self.width, more, 0.0)
        both = jnp.concatenate([here, more], axis=0)
        return pltpu.roll(both, self.size + 7, axis=0)[: self.size] - here

    def behind_x(self, ref, *index):
        here = self.get(ref, *index)
        before = pl.multiple_of(jnp.maximum(self.at - 8, 0), 8)
        more = ref[(*index, pl.ds(before, 8), slice(None))]
        more = jnp.where(self.at > 0, more, 0.0)
        both = jnp.concatenate([more, here], axis=0)
        return here - pltpu.roll(both, 1, axis=0)[8:]


def over_rows(width_x, body):
    size = ROWS if width_x % ROWS == 0 else 8

    def step(i, carry):
        body(Chunk(pl.multiple_of(i * size, 8), size, width_x))
        return carry

    lax.fori_loop(0, width_x // size, step, 0)


def coefficient(c, eps_ref, sigma_ref, z):
    eps, sigma = c.get(eps_ref, z), c.get(sigma_ref, z)
    return 1.0 / (2.0 * eps + sigma), eps, sigma


def odd_device():
    return lax.rem(lax.axis_index("gz"), 2) == 1


def halves_first(e_ref, h_ref, eps_ref, sigma_ref, chip_ref, far_ref):
    top, width_x = e_ref.shape[1] - 1, e_ref.shape[2]
    odd = odd_device()

    def body(c):
        ez = c.get(e_ref, 2, top)
        hx = c.get(h_ref, 0, top) - HALF * (ahead_y(ez) + c.get(e_ref, 1, top))
        hy = c.get(h_ref, 1, top) + HALF * (c.get(e_ref, 0, top) + c.ahead_x(e_ref, 2, top))
        cb_top = coefficient(c, eps_ref, sigma_ref, top)[0]
        cb_low = coefficient(c, eps_ref, sigma_ref, 0)[0]
        upward = (hx, hy, cb_top)
        downward = (c.get(e_ref, 0, 0), c.get(e_ref, 1, 0), cb_low)
        for k in range(3):
            c.put(chip_ref, k, jnp.where(odd, downward[k], upward[k]))
            c.put(far_ref, k, jnp.where(odd, upward[k], downward[k]))

    over_rows(width_x, body)


def split3(v):
    one = v.astype(BF16)
    rest = v - one.astype(F32)
    two = rest.astype(BF16)
    three = (rest - two.astype(F32)).astype(BF16)
    return one, two, three


def pack_entries(owners_ref, cells_ref, amplitude_ref, packed_ref, slab, top, width_x, width_y, cap):
    peers, _, lanes = packed_ref.shape
    owner, cell, amp = owners_ref[...], cells_ref[...], amplitude_ref[...]
    entries = owner.shape[1]
    named = lax.broadcasted_iota(jnp.int32, (peers, entries), 0) == owner
    hot = named.astype(F32).astype(BF16)
    first = lax.broadcasted_iota(jnp.int32, (entries, entries), 0)
    second = lax.broadcasted_iota(jnp.int32, (entries, entries), 1)
    ahead = (first < second).astype(F32).astype(BF16)
    before = jnp.dot(hot, ahead, preferred_element_type=F32)
    rank = jnp.sum(jnp.where(named, before, 0.0), axis=0, keepdims=True).astype(jnp.int32)
    layer = width_x * width_y
    own = owner * lanes + rank
    above = jnp.where((cell >= top * layer) & (owner + 1 < peers), own + (lanes + cap), -1)
    below = jnp.where((cell < layer) & (owner > 0), own + (2 * cap - lanes), -1)
    line = cell // width_y
    column = cell - line * width_y
    rows = jnp.concatenate(
        [amp, line.astype(F32), column.astype(F32), jnp.zeros((3, entries), F32)], axis=0
    )
    one, two, three = split3(rows)
    values = jnp.concatenate(
        [one.astype(F32), two.astype(F32), three.astype(F32), jnp.zeros((8, entries), F32)], axis=0
    ).astype(BF16)
    slot = lax.broadcasted_iota(jnp.int32, (lanes, entries), 0)

    def body(d, carry):
        want = slot + d * lanes
        hit = (want == own) | (want == above) | (want == below)
        place = hit.astype(F32).astype(BF16)
        out = lax.dot_general(values, place, (((1,), (1,)), ((), ())), preferred_element_type=F32)
        packed_ref[d] = out[0:8] + out[8:16] + out[16:24]
        return carry

    lax.fori_loop(0, peers, body, 0)


def halves_second(
    cap,
    e_ref,
    h_ref,
    eps_ref,
    sigma_ref,
    owners_ref,
    cells_ref,
    amplitude_ref,
    chip_ref,
    far_ref,
    packed_ref,
    h1_ref,
    e1_ref,
    ca_ref,
    cb_ref,
):
    slab, width_x, width_y = e_ref.shape[1], e_ref.shape[2], e_ref.shape[3]
    top = slab - 1
    odd = odd_device()
    pack_entries(
        owners_ref, cells_ref, amplitude_ref, packed_ref, slab, top, width_x, width_y, cap
    )

    def magnetic(c):
        for z in range(slab):
            ex, ey, ez = (c.get(e_ref, k, z) for k in range(3))
            up_x = c.get(e_ref, 0, z + 1) - ex if z < top else -ex
            up_y = c.get(e_ref, 1, z + 1) - ey if z < top else -ey
            c.put(h1_ref, 0, z, c.get(h_ref, 0, z) - HALF * (ahead_y(ez) - up_y))
            c.put(h1_ref, 1, z, c.get(h_ref, 1, z) - HALF * (up_x - c.ahead_x(e_ref, 2, z)))
            c.put(h1_ref, 2, z, c.get(h_ref, 2, z) - HALF * (c.ahead_x(e_ref, 1, z) - ahead_y(ex)))

    over_rows(width_x, magnetic)

    def electric(c):
        for z in range(slab):
            cb, eps, sigma = coefficient(c, eps_ref, sigma_ref, z)
            ca = (2.0 * eps - sigma) * cb
            c.put(ca_ref, z, ca)
            c.put(cb_ref, z, cb)
            hx, hy, hz = (c.get(h1_ref, k, z) for k in range(3))
            by_x, by_y = behind_y(hx), behind_y(hz)
            if z > 0:
                down_x, down_y = hx - c.get(h1_ref, 0, z - 1), hy - c.get(h1_ref, 1, z - 1)
            else:
                down_x, down_y = hx, hy
            ex = ca * c.get(e_ref, 0, z) + cb * (by_y - down_y)
            ey = ca * c.get(e_ref, 1, z) + cb * (down_x - c.behind_x(h1_ref, 2, z))
            ez = ca * c.get(e_ref, 2, z) + cb * (c.behind_x(h1_ref, 1, z) - by_x)
            c.put(e1_ref, 0, z, ex)
            c.put(e1_ref, 1, z, ey)
            c.put(e1_ref, 2, z, ez)

    over_rows(width_x, electric)

    def boundary(c):
        ex, ey, ez = (c.get(e1_ref, k, top) for k in range(3))
        hx = c.get(h1_ref, 0, top) - HALF * (ahead_y(ez) + ey)
        hy = c.get(h1_ref, 1, top) + HALF * (ex + c.ahead_x(e1_ref, 2, top))
        upward = (hx, hy)
        downward = (c.get(e1_ref, 0, 0), c.get(e1_ref, 1, 0))
        for k in range(2):
            c.put(chip_ref, k, jnp.where(odd, downward[k], upward[k]))
            c.put(far_ref, k, jnp.where(odd, upward[k], downward[k]))

    over_rows(width_x, boundary)


def place_entries(cap, slab, got_ref, own_ref, below_ref, above_ref):
    peers, _, lanes = got_ref.shape
    width_x, width_y = own_ref.shape[2], own_ref.shape[3]
    group = LANES // cap
    part = lax.broadcasted_iota(jnp.int32, (8, LANES), 1) // cap

    def row_of(segment):
        blocks = []
        for g in range(0, peers, group):
            block = jnp.zeros((8, LANES), F32)
            for p in range(min(group, peers - g)):
                shift = ((p - segment) * cap) % LANES
                there = got_ref[g + p]
                there = pltpu.roll(there, shift, axis=1) if shift else there
                block = jnp.where(part == p, there, block)
            blocks.append(block)
        return jnp.concatenate(blocks, axis=1)

    def fill(segment, first_line, lines, comps, store):
        row = row_of(segment)
        count = row.shape[1]
        line = row[3:4].astype(jnp.int32) - first_line
        column = row[4:5].astype(jnp.int32)
        where_line = lax.broadcasted_iota(jnp.int32, (lines, count), 0) == line
        left = where_line.astype(F32).astype(BF16)
        where_column = lax.broadcasted_iota(jnp.int32, (width_y, count), 0) == column
        for k in range(comps):
            total = None
            for term in split3(row[k : k + 1]):
                right = jnp.where(where_column, term.astype(F32), 0.0).astype(BF16)
                out = lax.dot_general(
                    left, right, (((1,), (1,)), ((), ())), preferred_element_type=F32
                )
                total = out if total is None else total + out
            store(k, total)

    def store_own(k, total):
        for z in range(slab):
            own_ref[k, z] = total[z * width_x : (z + 1) * width_x]

    def store_below(k, total):
        below_ref[k] = total

    def store_above(k, total):
        above_ref[k] = total

    fill(0, 0, slab * width_x, 3, store_own)
    fill(1, (slab - 1) * width_x, width_x, 3, store_below)
    fill(2, 0, width_x, 2, store_above)


def inside(c, bounds_ref, z, slab, shape):
    deep = lax.axis_index("gz") * slab + z
    in_z = (deep >= bounds_ref[0, 0]) & (deep < bounds_ref[0, 1])
    line = lax.broadcasted_iota(jnp.int32, shape, 0) + c.at
    column = lax.broadcasted_iota(jnp.int32, shape, 1)
    keep = (line >= bounds_ref[1, 0]) & (line < bounds_ref[1, 1])
    keep = keep & (column >= bounds_ref[2, 0]) & (column < bounds_ref[2, 1])
    return jnp.where(keep & in_z, 1.0, 0.0)


def middle(
    e_ref,
    forward_ref,
    h1_ref,
    e1_ref,
    ca_ref,
    cb_ref,
    own_ref,
    sbelow_ref,
    sabove_ref,
    chip_ref,
    far_ref,
    timing_ref,
    bounds_ref,
    h2_ref,
    e2_ref,
    grad_ref,
    e1s,
    h1s,
    fs,
    h2a,
    dza,
):
    slab, width_x = e_ref.shape[1], e_ref.shape[2]
    top = slab - 1
    odd = odd_device()
    has_below = jnp.where(lax.axis_index("gz") > 0, 1.0, 0.0).astype(F32)
    wave0, wave1 = timing_ref[0, 0], timing_ref[0, 1]
    weight0, weight1 = timing_ref[1, 0], timing_ref[1, 1]

    def first(c):
        chip = [c.get(chip_ref, k) for k in range(3)]
        far = [c.get(far_ref, k) for k in range(3)]
        low = [jnp.where(odd, a, b) for a, b in zip(chip, far)]
        high = [jnp.where(odd, b, a) for a, b in zip(chip, far)]
        ex, ey = c.get(e_ref, 0, 0), c.get(e_ref, 1, 0)
        hax = has_below * (low[0] + HALF * ey)
        hay = has_below * (low[1] - HALF * ex)
        cb_a, cb_b = low[2], high[2]
        cb = [c.get(cb_ref, z) for z in range(slab)]
        e1 = [
            [c.get(e1_ref, k, z) - wave0 * cb[z] * c.get(own_ref, k, z) for k in range(3)]
            for z in range(slab)
        ]
        e1[0][0] = e1[0][0] + cb[0] * hay
        e1[0][1] = e1[0][1] - cb[0] * hax
        hx = c.get(h1_ref, 0, top) + HALF * high[1]
        hy = c.get(h1_ref, 1, top) - HALF * high[0]
        c.put(h1s, 0, hx)
        c.put(h1s, 1, hy)
        bx_far, bx_chip = c.behind_x(far_ref, 0), c.behind_x(chip_ref, 0)
        bx = jnp.where(odd, bx_far, bx_chip)
        e1[top][0] = e1[top][0] + HALF * cb[top] * high[0]
        e1[top][1] = e1[top][1] + HALF * cb[top] * high[1]
        e1[top][2] = e1[top][2] - HALF * cb[top] * (bx + behind_y(high[1]))
        c.put(fs, 0, cb_b * (hy - wave0 * c.get(sabove_ref, 0)))
        c.put(fs, 1, -cb_b * (hx + wave0 * c.get(sabove_ref, 1)))
        for z in range(slab):
            for k in range(3):
                c.put(e1s, k, z, e1[z][k])
        dx = cb_a * (HALF * ex - wave0 * c.get(sbelow_ref, 0))
        dy = cb_a * (HALF * ey - wave0 * c.get(sbelow_ref, 1))
        dz = -cb_a * (
            HALF * (c.behind_x(e_ref, 0, 0) + behind_y(ey)) + wave0 * c.get(sbelow_ref, 2)
        )
        c.put(dza, dz)
        c.put(h2a, 0, has_below * HALF * (ey - dy + e1[0][1] - ahead_y(dz)))
        c.put(h2a, 1, has_below * HALF * (dx - ex - e1[0][0]))

    over_rows(width_x, first)

    def second(c):
        c.put(h2a, 1, c.get(h2a, 1) + has_below * HALF * c.ahead_x(dza))
        for z in range(slab):
            ex, ey, ez = (c.get(e1s, k, z) for k in range(3))
            if z < top:
                up_x, up_y = c.get(e1s, 0, z + 1) - ex, c.get(e1s, 1, z + 1) - ey
                hx, hy = c.get(h1_ref, 0, z), c.get(h1_ref, 1, z)
            else:
                up_x, up_y = c.get(fs, 0) - ex, c.get(fs, 1) - ey
                hx, hy = c.get(h1s, 0), c.get(h1s, 1)
            c.put(h2_ref, 0, z, hx - HALF * (ahead_y(ez) - up_y))
            c.put(h2_ref, 1, z, hy - HALF * (up_x - c.ahead_x(e1s, 2, z)))
            hz = c.get(h1_ref, 2, z)
            c.put(h2_ref, 2, z, hz - HALF * (c.ahead_x(e1s, 1, z) - ahead_y(ex)))

    over_rows(width_x, second)

    def third(c):
        for z in range(slab):
            ca, cb = c.get(ca_ref, z), c.get(cb_ref, z)
            hx, hy, hz = (c.get(h2_ref, k, z) for k in range(3))
            if z > 0:
                down_x, down_y = hx - c.get(h2_ref, 0, z - 1), hy - c.get(h2_ref, 1, z - 1)
            else:
                down_x, down_y = hx - c.get(h2a, 0), hy - c.get(h2a, 1)
            curl = (
                behind_y(hz) - down_y,
                down_x - c.behind_x(h2_ref, 2, z),
                c.behind_x(h2_ref, 1, z) - behind_y(hx),
            )
            dot1, dot2 = 0.0, 0.0
            for k in range(3):
                e1 = c.get(e1s, k, z)
                e2 = ca * e1 + cb * (curl[k] - wave1 * c.get(own_ref, k, z))
                c.put(e2_ref, k, z, e2)
                fwd = c.get(forward_ref, k, z)
                dot1 = dot1 + e1 * fwd
                dot2 = dot2 + e2 * fwd
            mask = inside(c, bounds_ref, z, slab, ca.shape)
            c.put(grad_ref, z, mask * (weight0 * dot1 + weight1 * dot2))

    over_rows(width_x, third)


def last(
    forward_ref,
    h2_ref,
    e2_ref,
    gradp_ref,
    cb_ref,
    chip_ref,
    far_ref,
    timing_ref,
    bounds_ref,
    eout_ref,
    hout_ref,
    grad_ref,
):
    slab, width_x = e2_ref.shape[1], e2_ref.shape[2]
    top = slab - 1
    odd = odd_device()
    weight1 = timing_ref[1, 1]

    def body(c):
        chip = [c.get(chip_ref, k) for k in range(2)]
        far = [c.get(far_ref, k) for k in range(2)]
        low = [jnp.where(odd, a, b) for a, b in zip(chip, far)]
        high = [jnp.where(odd, b, a) for a, b in zip(chip, far)]
        bx = jnp.where(odd, c.behind_x(far_ref, 0), c.behind_x(chip_ref, 0))
        more = [[None] * 3 for _ in range(slab)]
        cb_low, cb_top = c.get(cb_ref, 0), HALF * c.get(cb_ref, top)
        more[0][0] = cb_low * low[1]
        more[0][1] = -cb_low * low[0]
        more[top][0] = cb_top * high[0]
        more[top][1] = cb_top * high[1]
        more[top][2] = -cb_top * (bx + behind_y(high[1]))
        for z in range(slab):
            dot = 0.0
            for k in range(3):
                e2 = c.get(e2_ref, k, z)
                if more[z][k] is not None:
                    e2 = e2 + more[z][k]
                    dot = dot + more[z][k] * c.get(forward_ref, k, z)
                c.put(eout_ref, k, z, e2)
            mask = inside(c, bounds_ref, z, slab, cb_low.shape)
            c.put(grad_ref, z, c.get(gradp_ref, z) + (weight1 * mask) * dot)
            hx, hy = c.get(h2_ref, 0, z), c.get(h2_ref, 1, z)
            if z == top:
                hx, hy = hx + HALF * high[1], hy - HALF * high[0]
            c.put(hout_ref, 0, z, hx)
            c.put(hout_ref, 1, z, hy)
            c.put(hout_ref, 2, z, c.get(h2_ref, 2, z))

    over_rows(width_x, body)


def shape(*dims):
    return jax.ShapeDtypeStruct(dims, F32)


def call(body, outs, ins, flops, scratch=()):
    total = sum(8 * x.size for x in jax.tree.leaves((outs, list(ins))))
    return pl.pallas_call(
        body,
        out_shape=outs,
        in_specs=[
            pl.BlockSpec(memory_space=SMEM if x.size < 16 else VMEM) for x in ins
        ],
        out_specs=jax.tree.map(lambda _: pl.BlockSpec(memory_space=VMEM), outs),
        scratch_shapes=list(scratch),
        compiler_params=pltpu.CompilerParams(vmem_limit_bytes=40 * 1024 * 1024),
        cost_estimate=pl.CostEstimate(flops=flops, bytes_accessed=total, transcendentals=0),
    )(*ins)


def local(
    e_field,
    h_field,
    forward_field,
    permittivity,
    conductivity,
    owners,
    cells,
    amplitude,
    timing,
    bounds,
):
    slab, wx, wy = permittivity.shape
    peers = lax.axis_size("gz")
    rows = owners.shape[0]
    cap = 2 * rows // peers
    lanes = -(-3 * cap // LANES) * LANES
    cells_all = slab * wx * wy
    chip_pairs = [p for i in range(0, peers - 1, 2) for p in ((i, i + 1), (i + 1, i))]
    far_pairs = [p for i in range(1, peers - 1, 2) for p in ((i, i + 1), (i + 1, i))]

    chip1, far1 = call(
        halves_first,
        (shape(3, wx, wy), shape(3, wx, wy)),
        (e_field, h_field, permittivity, conductivity),
        cells_all * 20,
    )
    far1 = lax.ppermute(far1, "gz", far_pairs)
    chip1 = lax.ppermute(chip1, "gz", chip_pairs)
    chip2, far2, packed, h1, e1, ca, cb = call(
        functools.partial(halves_second, cap),
        (
            shape(2, wx, wy),
            shape(2, wx, wy),
            shape(peers, 8, lanes),
            shape(3, slab, wx, wy),
            shape(3, slab, wx, wy),
            shape(slab, wx, wy),
            shape(slab, wx, wy),
        ),
        (
            e_field,
            h_field,
            permittivity,
            conductivity,
            owners.reshape(1, rows),
            cells.reshape(1, rows),
            amplitude,
        ),
        cells_all * 60,
    )
    got = lax.all_to_all(packed, "gz", 0, 0, tiled=True)
    far2 = lax.ppermute(far2, "gz", far_pairs)
    chip2 = lax.ppermute(chip2, "gz", chip_pairs)
    own, sbelow, sabove = call(
        functools.partial(place_entries, cap, slab),
        (shape(3, slab, wx, wy), shape(3, wx, wy), shape(2, wx, wy)),
        (got,),
        cells_all * 60,
    )
    h2, e2, grad = call(
        middle,
        (shape(3, slab, wx, wy), shape(3, slab, wx, wy), shape(slab, wx, wy)),
        (
            e_field,
            forward_field,
            h1,
            e1,
            ca,
            cb,
            own,
            sbelow,
            sabove,
            chip1,
            far1,
            timing,
            bounds,
        ),
        cells_all * 100,
        scratch=(
            VMEM((3, slab, wx, wy), F32),
            VMEM((2, wx, wy), F32),
            VMEM((2, wx, wy), F32),
            VMEM((2, wx, wy), F32),
            VMEM((wx, wy), F32),
        ),
    )
    return call(
        last,
        (shape(3, slab, wx, wy), shape(3, slab, wx, wy), shape(slab, wx, wy)),
        (forward_field, h2, e2, grad, cb, chip2, far2, timing, bounds),
        cells_all * 20,
    )


def solution(mesh):
    placed = (
        P(None, "gz", "groups", None),
        P(None, "gz", "groups", None),
        P(None, "gz", "groups", None),
        P("gz", "groups", None),
        P("gz", "groups", None),
        P("gz", "groups"),
        P("gz", "groups"),
        P("groups", "gz"),
        P("groups", None),
        P("groups", None),
    )
    return jax.shard_map(
        local,
        mesh=mesh,
        in_specs=placed,
        out_specs=(
            P(None, "gz", "groups", None),
            P(None, "gz", "groups", None),
            P("gz", "groups", None),
        ),
        check_vma=False,
    )
```

time: 222 us -> 50.3 us (0.23)
  the two profiles are of different devices: /device:TPU:1 before, /device:TPU:0 now
where the time goes in v1:
time: 50.3 us; the launch traced here: 49.7 us
  Pallas kernels  17.8 us (35%)
  starting transfers between devices  13.4 us (27%)
  local copies, waits for them, and re-layouts  11 us (22%)
  waiting for transfers between devices  6.8 us (14%)
  between operations  0.78 us (2%)
    pallas_call x5, Pallas kernels, call(): pl.pallas_call(body, out_shape=outs, in_specs=[pl.BlockSpec(memory_space=...  17.8 us
    unnamed x35, local copies, waits for them, and re-layouts  11 us
    all_to_all x1, starting transfers between devices, local(): got = lax.all_to_all(packed, 'gz', 0, 0, tiled=True)  6.94 us
    all_to_all x1, waiting for transfers between devices, local(): got = lax.all_to_all(packed, 'gz', 0, 0, tiled=True)  6.79 us
    ppermute x1, starting transfers between devices, local(): chip2 = lax.ppermute(chip2, 'gz', chip_pairs)  3.05 us
    ppermute x1, starting transfers between devices, local(): far1 = lax.ppermute(far1, 'gz', far_pairs)  1.51 us
    ppermute x1, starting transfers between devices, local(): far2 = lax.ppermute(far2, 'gz', far_pairs)  1.42 us
  transfers between devices with their start and end apart: 5, of which 1 were waited for; matrix products, arithmetic and copies ran while one was open for 0% of the time, Pallas kernels for 25%

profile of v1, /device:TPU:0, one launch (start us, length us, event | category | flops | bytes accessed | tf_op | source)
XLA Modules:
  0.0 49.7 jit_solution(17425469171041522058)
XLA Ops:
  0.6 0.0 copy-start
  0.6 1.3 %copy-done = f32[3,2,192,256]{3,2,1,0:T(8,128)S(1)} copy-done((f32[3,2,192,256]{3,2,1,0:T(8,128)S(1)}, f32[3,2,192,256]{3,2,1,0:T(8,128)}, u32[]{:S(2)}) %copy-start) | copy-done | bytes 1179672
  1.9 1.3 %copy-done.3 = f32[3,2,192,256]{3,2,1,0:T(8,128)S(1)} copy-done((f32[3,2,192,256]{3,2,1,0:T(8,128)S(1)}, f32[3,2,192,256]{3,2,1,0:T(8,128)}, u32[]{:S(2)}) %copy-start.3) | copy-done | bytes 1179672
  3.2 1.0 %copy-done.4 = f32[2,192,256]{2,1,0:T(8,128)S(1)} copy-done((f32[2,192,256]{2,1,0:T(8,128)S(1)}, f32[2,192,256]{2,1,0:T(8,128)}, u32[]{:S(2)}) %copy-start.4) | copy-done | bytes 393240
  4.2 1.0 %copy-done.5 = f32[2,192,256]{2,1,0:T(8,128)S(1)} copy-done((f32[2,192,256]{2,1,0:T(8,128)S(1)}, f32[2,192,256]{2,1,0:T(8,128)}, u32[]{:S(2)}) %copy-start.5) | copy-done | bytes 393240
  5.2 1.7 %shard_map.123 = (f32[3,192,256]{2,1,0:T(8,128)}, f32[3,192,256]{2,1,0:T(8,128)}) custom-call(f32[3,2,192,256]{3,2,1,0:T(8,128)S(1)} %copy-done, f32[3,2,192,256]{3,2,1,0:T(8,128)S(1)} %copy-done.3, f32[2,192,256]{2,1,0:T(8,128)S(1)} %copy-done.4, f32[2,192,256]{2,1,0:T(8,128)S(1)} %copy-done.5), custom_call_target="tpu_custom_call" | custom-call | flops 1966080 | bytes 8650752 | tf_op jit(solution)/shard_map/pallas_call | solution.py:447
  6.9 0.5 collective-permute-start
  7.4 1.5 %collective-permute-start.1 = (f32[3,192,256]{2,1,0:T(8,128)}, f32[3,192,256]{2,1,0:T(8,128)}, u32[]{:S(2)}, u32[]{:S(2)}) collective-permute-start(f32[3,192,256]{2,1,0:T(8,128)} %get-tuple-element.27), channel_id=1, source_target_pairs={{1,2},{2,1},{3,4},{4,3},{5,6},{6,5},{7,8},{8,7},{9,10},{10,9},{11,... | collective-permute-start | bytes 1769480 | tf_op jit(solution)/shard_map/ppermute | solution.py:487
  8.9 0.0 copy-start.13
  8.9 6.0 %shard_map.121 = (f32[2,192,256]{2,1,0:T(8,128)}, f32[2,192,256]{2,1,0:T(8,128)}, f32[16,8,128]{2,1,0:T(8,128)}, f32[3,2,192,256]{3,2,1,0:T(8,128)S(1)}, f32[3,2...) custom-call(f32[3,2,192,256]{3,2,1,0:T(8,128)S(1)} %copy-done, ...), custom_call_target="tpu_custom_call" | custom-call | flops 5898240 | bytes 14297088 | tf_op jit(solution)/shard_map/pallas_call | solution.py:447
  14.9 1.0 %copy-done.6 = f32[3,2,192,256]{3,2,1,0:T(8,128)} copy-done((f32[3,2,192,256]{3,2,1,0:T(8,128)}, f32[3,2,192,256]{3,2,1,0:T(8,128)S(1)}, u32[]{:S(2)}) %copy-start.6) | copy-done | bytes 1179672
  15.9 1.0 %copy-done.8 = f32[3,2,192,256]{3,2,1,0:T(8,128)} copy-done((f32[3,2,192,256]{3,2,1,0:T(8,128)}, f32[3,2,192,256]{3,2,1,0:T(8,128)S(1)}, u32[]{:S(2)}) %copy-start.8) | copy-done | bytes 1179672
  16.9 0.7 %copy-done.10 = f32[2,192,256]{2,1,0:T(8,128)} copy-done((f32[2,192,256]{2,1,0:T(8,128)}, f32[2,192,256]{2,1,0:T(8,128)S(1)}, u32[]{:S(2)}) %copy-start.10) | copy-done | bytes 393240
  17.7 3.1 %collective-permute-start.2 = (f32[2,192,256]{2,1,0:T(8,128)}, f32[2,192,256]{2,1,0:T(8,128)}, u32[]{:S(2)}, u32[]{:S(2)}) collective-permute-start(f32[2,192,256]{2,1,0:T(8,128)} %get-tuple-element.31), channel_id=1, source_target_pairs={{0,1},{1,0},{2,3},{3,2},{4,5},{5,4},{6,7},{7,6},{8,9},{9,8},{10,11... | collective-permute-start | bytes 1179656 | tf_op jit(solution)/shard_map/ppermute | solution.py:513
  20.7 1.4 %collective-permute-start.3 = (f32[2,192,256]{2,1,0:T(8,128)}, f32[2,192,256]{2,1,0:T(8,128)}, u32[]{:S(2)}, u32[]{:S(2)}) collective-permute-start(f32[2,192,256]{2,1,0:T(8,128)} %get-tuple-element.32), channel_id=1, source_target_pairs={{1,2},{2,1},{3,4},{4,3},{5,6},{6,5},{7,8},{8,7},{9,10},{10,9},{11,... | collective-permute-start | bytes 1179656 | tf_op jit(solution)/shard_map/ppermute | solution.py:512
  22.1 6.9 %all-to-all-start = ((f32[16,8,128]{2,1,0:T(8,128)}), f32[16,8,128]{2,1,0:T(8,128)S(1)}, u32[]{:S(2)}, u32[]{:S(2)}) async-start(f32[16,8,128]{2,1,0:T(8,128)} %get-tuple-element.22), calls=%async_computation | async-start | bytes 131072 | tf_op jit(solution)/shard_map/all_to_all | solution.py:511
  29.1 0.1 copy.13.bounds_ref
  29.2 6.8 %all-to-all-done.got_ref = f32[16,8,128]{2,1,0:T(8,128)S(1)} async-done(((f32[16,8,128]{2,1,0:T(8,128)}), f32[16,8,128]{2,1,0:T(8,128)S(1)}, u32[]{:S(2)}, u32[]{:S(2)}) %all-to-all-start) | async-done | bytes 65568 | tf_op jit(solution)/shard_map/all_to_all | solution.py:511
  36.0 2.4 %shard_map.122 = (f32[3,2,192,256]{3,2,1,0:T(8,128)S(1)}, f32[3,192,256]{2,1,0:T(8,128)S(1)}, f32[2,192,256]{2,1,0:T(8,128)S(1)}) custom-call(f32[16,8,128]{2,1,0:T(8,128)S(1)} %all-to-all-done.got_ref), custom_call_target="tpu_custom_call" | custom-call | flops 5898240 | bytes 4456448 | tf_op jit(solution)/shard_map/pallas_call | solution.py:447
  38.4 1.3 %copy-done.7 = f32[3,2,192,256]{3,2,1,0:T(8,128)S(1)} copy-done((f32[3,2,192,256]{3,2,1,0:T(8,128)S(1)}, f32[3,2,192,256]{3,2,1,0:T(8,128)}, u32[]{:S(2)}) %copy-start.7) | copy-done | bytes 1179672
  39.7 1.3 %copy-done.9 = f32[3,2,192,256]{3,2,1,0:T(8,128)S(1)} copy-done((f32[3,2,192,256]{3,2,1,0:T(8,128)S(1)}, f32[3,2,192,256]{3,2,1,0:T(8,128)}, u32[]{:S(2)}) %copy-start.9) | copy-done | bytes 1179672
  41.0 1.0 %copy-done.11 = f32[2,192,256]{2,1,0:T(8,128)S(1)} copy-done((f32[2,192,256]{2,1,0:T(8,128)S(1)}, f32[2,192,256]{2,1,0:T(8,128)}, u32[]{:S(2)}) %copy-start.11) | copy-done | bytes 393240
  42.0 4.1 %shard_map.124 = (f32[3,2,192,256]{3,2,1,0:T(8,128)S(1)}, f32[3,2,192,256]{3,2,1,0:T(8,128)S(1)}, f32[2,192,256]{2,1,0:T(8,128)S(1)}) custom-call(f32[3,2,192,256]{3,2,1,0:T(8,128)S(1)} %copy-done.1, f32[3,2,192,256]{3,2,1,0:T(8,128)S(1)} %copy-done.2, f32[3,2,192,256]{3,2,1,0:T(8,128)S(1)} %copy-done.7, f32[3,2,192,256]{3,2,1,0:T(8,128)S(1)} %copy-done.9, ...), custom_call_target="tpu_custom_call" | custom-call | flops 9830400 | bytes 23199824 | tf_op jit(solution)/shard_map/pallas_call | solution.py:447
  46.1 3.6 %shard_map.125 = (f32[3,2,192,256]{3,2,1,0:T(8,128)}, f32[3,2,192,256]{3,2,1,0:T(8,128)}, f32[2,192,256]{2,1,0:T(8,128)}) custom-call(f32[3,2,192,256]{3,2,1,0:T(8,128)S(1)} %copy-done.2, f32[3,2,192,256]{3,2,1,0:T(8,128)S(1)} %get-tuple-element.28.h2_ref, f32[3,2,192,256]{3,2,1,0:T(8,128)S(1)} %get-tuple-element.29.e2_ref, ...), custom_call_target="tpu_custom_call" | custom-call | flops 1966080 | bytes 15728720 | tf_op jit(solution)/shard_map/pallas_call | solution.py:447
  (26 shorter events, 0.1 us)
Async XLA Ops:
  0.6 1.3 %copy-start = (f32[3,2,192,256]{3,2,1,0:T(8,128)S(1)}, f32[3,2,192,256]{3,2,1,0:T(8,128)}, u32[]{:S(2)}) copy-start(f32[3,2,192,256]{3,2,1,0:T(8,128)} %e_ref.5) | copy-start | bytes 3538948
  1.9 1.3 %copy-start.3 = (f32[3,2,192,256]{3,2,1,0:T(8,128)S(1)}, f32[3,2,192,256]{3,2,1,0:T(8,128)}, u32[]{:S(2)}) copy-start(f32[3,2,192,256]{3,2,1,0:T(8,128)} %h_ref.3) | copy-start | bytes 3538948
  3.2 1.0 %copy-start.4 = (f32[2,192,256]{2,1,0:T(8,128)S(1)}, f32[2,192,256]{2,1,0:T(8,128)}, u32[]{:S(2)}) copy-start(f32[2,192,256]{2,1,0:T(8,128)} %eps_ref.3) | copy-start | bytes 1179652
  4.2 1.0 %copy-start.5 = (f32[2,192,256]{2,1,0:T(8,128)S(1)}, f32[2,192,256]{2,1,0:T(8,128)}, u32[]{:S(2)}) copy-start(f32[2,192,256]{2,1,0:T(8,128)} %sigma_ref.3) | copy-start | bytes 1179652
  5.2 3.7 %copy-start.12 = (f32[3,256]{1,0:T(4,128)S(1)}, f32[3,256]{1,0:T(4,128)}, u32[]{:S(2)}) copy-start(f32[3,256]{1,0:T(4,128)} %amplitude_ref.1) | copy-start | bytes 9220
  5.2 3.7 %copy-start.14 = (s32[256,1]{0,1:T(1,128)S(1)}, s32[256,1]{0,1:T(1,128)}, u32[]{:S(2)}) copy-start(s32[256,1]{0,1:T(1,128)} %param.15) | copy-start | bytes 3076
  5.2 3.7 %copy-start.15 = (s32[256,1]{0,1:T(1,128)S(1)}, s32[256,1]{0,1:T(1,128)}, u32[]{:S(2)}) copy-start(s32[256,1]{0,1:T(1,128)} %param.16) | copy-start | bytes 3076
  6.9 31.5 %collective-permute-start = (f32[3,192,256]{2,1,0:T(8,128)}, f32[3,192,256]{2,1,0:T(8,128)S(1)}, u32[]{:S(2)}, u32[]{:S(2)}) collective-permute-start(f32[3,192,256]{2,1,0:T(8,128)} %get-tuple-element.26), channel_id=1, source_target_pairs={{0,1},{1,0},{2,3},{3,2},{4,5},{5,4},{6,7},{7,6},{8,9},{9,8},{10,11... | collective-permute-start | bytes 1769480 | tf_op jit(solution)/shard_map/ppermute | solution.py:488
  7.4 31.0 %collective-permute-start.1 = (f32[3,192,256]{2,1,0:T(8,128)}, f32[3,192,256]{2,1,0:T(8,128)}, u32[]{:S(2)}, u32[]{:S(2)}) collective-permute-start(f32[3,192,256]{2,1,0:T(8,128)} %get-tuple-element.27), channel_id=1, source_target_pairs={{1,2},{2,1},{3,4},{4,3},{5,6},{6,5},{7,8},{8,7},{9,10},{10,9},{11,... | collective-permute-start | bytes 1769480 | tf_op jit(solution)/shard_map/ppermute | solution.py:487
  8.9 20.2 %copy-start.16 = (s32[3,2]{0,1:T(2,128)S(1)}, s32[3,2]{0,1:T(2,128)}, u32[]{:S(2)}) copy-start(s32[3,2]{0,1:T(2,128)} %param.19) | copy-start | bytes 76
  8.9 29.5 %copy-start.1 = (f32[3,2,192,256]{3,2,1,0:T(8,128)S(1)}, f32[3,2,192,256]{3,2,1,0:T(8,128)}, u32[]{:S(2)}) copy-start(f32[3,2,192,256]{3,2,1,0:T(8,128)} %e_ref.5) | copy-start | bytes 3538948
  8.9 29.5 %copy-start.2 = (f32[3,2,192,256]{3,2,1,0:T(8,128)S(1)}, f32[3,2,192,256]{3,2,1,0:T(8,128)}, u32[]{:S(2)}) copy-start(f32[3,2,192,256]{3,2,1,0:T(8,128)} %forward_ref.3) | copy-start | bytes 3538948
  8.9 29.5 %copy-start.13 = (f32[2,2]{1,0:T(2,128)S(1)}, f32[2,2]{1,0:T(2,128)}, u32[]{:S(2)}) copy-start(f32[2,2]{1,0:T(2,128)} %timing_ref.3) | copy-start | bytes 52
  14.9 1.0 %copy-start.6 = (f32[3,2,192,256]{3,2,1,0:T(8,128)}, f32[3,2,192,256]{3,2,1,0:T(8,128)S(1)}, u32[]{:S(2)}) copy-start(f32[3,2,192,256]{3,2,1,0:T(8,128)S(1)} %get-tuple-element.18.h1_ref) | copy-start | bytes 3538948
  15.9 1.0 %copy-start.8 = (f32[3,2,192,256]{3,2,1,0:T(8,128)}, f32[3,2,192,256]{3,2,1,0:T(8,128)S(1)}, u32[]{:S(2)}) copy-start(f32[3,2,192,256]{3,2,1,0:T(8,128)S(1)} %get-tuple-element.19.e1_ref) | copy-start | bytes 3538948
  16.9 0.8 %copy-start.10 = (f32[2,192,256]{2,1,0:T(8,128)}, f32[2,192,256]{2,1,0:T(8,128)S(1)}, u32[]{:S(2)}) copy-start(f32[2,192,256]{2,1,0:T(8,128)S(1)} %get-tuple-element.20.ca_ref) | copy-start | bytes 1179652
  17.7 28.4 %collective-permute-start.2 = (f32[2,192,256]{2,1,0:T(8,128)}, f32[2,192,256]{2,1,0:T(8,128)}, u32[]{:S(2)}, u32[]{:S(2)}) collective-permute-start(f32[2,192,256]{2,1,0:T(8,128)} %get-tuple-element.31), channel_id=1, source_target_pairs={{0,1},{1,0},{2,3},{3,2},{4,5},{5,4},{6,7},{7,6},{8,9},{9,8},{10,11... | collective-permute-start | bytes 1179656 | tf_op jit(solution)/shard_map/ppermute | solution.py:513
  20.7 25.4 %collective-permute-start.3 = (f32[2,192,256]{2,1,0:T(8,128)}, f32[2,192,256]{2,1,0:T(8,128)}, u32[]{:S(2)}, u32[]{:S(2)}) collective-permute-start(f32[2,192,256]{2,1,0:T(8,128)} %get-tuple-element.32), channel_id=1, source_target_pairs={{1,2},{2,1},{3,4},{4,3},{5,6},{6,5},{7,8},{8,7},{9,10},{10,9},{11,... | collective-permute-start | bytes 1179656 | tf_op jit(solution)/shard_map/ppermute | solution.py:512
  22.1 13.8 %all-to-all-start = ((f32[16,8,128]{2,1,0:T(8,128)}), f32[16,8,128]{2,1,0:T(8,128)S(1)}, u32[]{:S(2)}, u32[]{:S(2)}) async-start(f32[16,8,128]{2,1,0:T(8,128)} %get-tuple-element.22), calls=%async_computation | async-start | bytes 131072 | tf_op jit(solution)/shard_map/all_to_all | solution.py:511
  38.4 1.3 %copy-start.7 = (f32[3,2,192,256]{3,2,1,0:T(8,128)S(1)}, f32[3,2,192,256]{3,2,1,0:T(8,128)}, u32[]{:S(2)}) copy-start(f32[3,2,192,256]{3,2,1,0:T(8,128)} %copy-done.6) | copy-start | bytes 3538948
  39.7 1.3 %copy-start.9 = (f32[3,2,192,256]{3,2,1,0:T(8,128)S(1)}, f32[3,2,192,256]{3,2,1,0:T(8,128)}, u32[]{:S(2)}) copy-start(f32[3,2,192,256]{3,2,1,0:T(8,128)} %copy-done.8) | copy-start | bytes 3538948
  41.0 1.0 %copy-start.11 = (f32[2,192,256]{2,1,0:T(8,128)S(1)}, f32[2,192,256]{2,1,0:T(8,128)}, u32[]{:S(2)}) copy-start(f32[2,192,256]{2,1,0:T(8,128)} %copy-done.10) | copy-start | bytes 1179652

commit v2 on v1

--- a/solution.py
+++ b/solution.py
@@ -1,4 +1,5 @@
 import functools
+import math
 
 import jax
 import jax.numpy as jnp
@@ -9,6 +10,7 @@
 
 STEPS = 2
 ROWS = 24
+PARTS = 4
 LANES = 128
 HALF = 0.5
 F32 = jnp.float32
@@ -58,42 +60,89 @@
         return here - pltpu.roll(both, 1, axis=0)[8:]
 
 
-def over_rows(width_x, body):
-    size = ROWS if width_x % ROWS == 0 else 8
+def over_rows(width_x, body, begin=0, end=None):
+    end = width_x if end is None else end
+    size = ROWS if (end - begin) % ROWS == 0 else 8
 
     def step(i, carry):
-        body(Chunk(pl.multiple_of(i * size, 8), size, width_x))
+        body(Chunk(pl.multiple_of(begin + i * size, 8), size, width_x))
         return carry
 
-    lax.fori_loop(0, width_x // size, step, 0)
-
-
-def coefficient(c, eps_ref, sigma_ref, z):
-    eps, sigma = c.get(eps_ref, z), c.get(sigma_ref, z)
-    return 1.0 / (2.0 * eps + sigma), eps, sigma
+    lax.fori_loop(0, (end - begin) // size, step, 0)
 
 
 def odd_device():
     return lax.rem(lax.axis_index("gz"), 2) == 1
 
 
-def halves_first(e_ref, h_ref, eps_ref, sigma_ref, chip_ref, far_ref):
-    top, width_x = e_ref.shape[1] - 1, e_ref.shape[2]
+def send_rows(g, part, chip_ref, far_ref, chip_hbm, far_hbm, sems):
+    rows = pl.ds(g * part, part)
+    far = pltpu.make_async_copy(far_ref.at[:, rows], far_hbm.at[:, rows], sems.at[g, 0])
+    chip = pltpu.make_async_copy(chip_ref.at[:, rows], chip_hbm.at[:, rows], sems.at[g, 1])
+    far.start()
+    chip.start()
+    return [far, chip]
+
+
+def halves_first(
+    e_hbm,
+    h_hbm,
+    eps_hbm,
+    sigma_hbm,
+    chip_hbm,
+    far_hbm,
+    e_ref,
+    h_ref,
+    low_ref,
+    mat_ref,
+    chip_ref,
+    far_ref,
+    sems,
+    out_sems,
+):
+    slab, width_x = e_hbm.shape[1], e_hbm.shape[2]
+    top = slab - 1
     odd = odd_device()
+    part = width_x // PARTS
+    copies = []
+    for g in range(PARTS):
+        rows = pl.ds(g * part, part)
+        pairs = (
+            (e_hbm.at[:, top, rows], e_ref.at[:, rows]),
+            (h_hbm.at[0:2, top, rows], h_ref.at[:, rows]),
+            (eps_hbm.at[:, rows], mat_ref.at[0, :, rows]),
+            (sigma_hbm.at[:, rows], mat_ref.at[1, :, rows]),
+            (e_hbm.at[0:2, 0, rows], low_ref.at[:, rows]),
+        )
+        copies.append(
+            [pltpu.make_async_copy(a, b, sems.at[g, i]) for i, (a, b) in enumerate(pairs)]
+        )
+        for copy in copies[-1]:
+            copy.start()
 
     def body(c):
-        ez = c.get(e_ref, 2, top)
-        hx = c.get(h_ref, 0, top) - HALF * (ahead_y(ez) + c.get(e_ref, 1, top))
-        hy = c.get(h_ref, 1, top) + HALF * (c.get(e_ref, 0, top) + c.ahead_x(e_ref, 2, top))
-        cb_top = coefficient(c, eps_ref, sigma_ref, top)[0]
-        cb_low = coefficient(c, eps_ref, sigma_ref, 0)[0]
+        ez = c.get(e_ref, 2)
+        hx = c.get(h_ref, 0) - HALF * (ahead_y(ez) + c.get(e_ref, 1))
+        hy = c.get(h_ref, 1) + HALF * (c.get(e_ref, 0) + c.ahead_x(e_ref, 2))
+        cb_top = 1.0 / (2.0 * c.get(mat_ref, 0, top) + c.get(mat_ref, 1, top))
+        cb_low = 1.0 / (2.0 * c.get(mat_ref, 0, 0) + c.get(mat_ref, 1, 0))
         upward = (hx, hy, cb_top)
-        downward = (c.get(e_ref, 0, 0), c.get(e_ref, 1, 0), cb_low)
+        downward = (c.get(low_ref, 0), c.get(low_ref, 1), cb_low)
         for k in range(3):
             c.put(chip_ref, k, jnp.where(odd, downward[k], upward[k]))
             c.put(far_ref, k, jnp.where(odd, upward[k], downward[k]))
 
-    over_rows(width_x, body)
+    for copy in copies[0]:
+        copy.wait()
+    out = []
+    for g in range(PARTS):
+        if g + 1 < PARTS:
+            for copy in copies[g + 1]:
+                copy.wait()
+        over_rows(width_x, body, g * part, (g + 1) * part)
+        out = out + send_rows(g, part, chip_ref, far_ref, chip_hbm, far_hbm, out_sems)
+    for copy in out:
+        copy.wait()
 
 
 def split3(v):
@@ -104,7 +153,7 @@
     return one, two, three
 
 
-def pack_entries(owners_ref, cells_ref, amplitude_ref, packed_ref, slab, top, width_x, width_y, cap):
+def pack_entries(cap, top, width_x, width_y, owners_ref, cells_ref, amplitude_ref, packed_ref):
     peers, _, lanes = packed_ref.shape
     owner, cell, amp = owners_ref[...], cells_ref[...], amplitude_ref[...]
     entries = owner.shape[1]
@@ -141,78 +190,106 @@
     lax.fori_loop(0, peers, body, 0)
 
 
+def magnetic_step(c, e_ref, h_ref, h1_ref):
+    slab = e_ref.shape[1]
+    for z in range(slab):
+        ex, ey, ez = (c.get(e_ref, k, z) for k in range(3))
+        up_x = c.get(e_ref, 0, z + 1) - ex if z + 1 < slab else -ex
+        up_y = c.get(e_ref, 1, z + 1) - ey if z + 1 < slab else -ey
+        c.put(h1_ref, 0, z, c.get(h_ref, 0, z) - HALF * (ahead_y(ez) - up_y))
+        c.put(h1_ref, 1, z, c.get(h_ref, 1, z) - HALF * (up_x - c.ahead_x(e_ref, 2, z)))
+        c.put(h1_ref, 2, z, c.get(h_ref, 2, z) - HALF * (c.ahead_x(e_ref, 1, z) - ahead_y(ex)))
+
+
+def electric_step(c, z, comps, e_ref, h1_ref, ca, cb):
+    hx, hy, hz = (c.get(h1_ref, k, z) for k in range(3))
+    down_x = hx - c.get(h1_ref, 0, z - 1) if z > 0 else hx
+    down_y = hy - c.get(h1_ref, 1, z - 1) if z > 0 else hy
+    ex = ca * c.get(e_ref, 0, z) + cb * (behind_y(hz) - down_y)
+    ey = ca * c.get(e_ref, 1, z) + cb * (down_x - c.behind_x(h1_ref, 2, z))
+    if comps == 2:
+        return ex, ey
+    ez = ca * c.get(e_ref, 2, z) + cb * (c.behind_x(h1_ref, 1, z) - behind_y(hx))
+    return ex, ey, ez
+
+
+def coefficients(c, eps_ref, sigma_ref, z):
+    eps, sigma = c.get(eps_ref, z), c.get(sigma_ref, z)
+    cb = 1.0 / (2.0 * eps + sigma)
+    return (2.0 * eps - sigma) * cb, cb
+
+
 def halves_second(
-    cap,
     e_ref,
     h_ref,
     eps_ref,
     sigma_ref,
-    owners_ref,
-    cells_ref,
-    amplitude_ref,
+    packed_hbm,
+    chip_hbm,
+    far_hbm,
+    h1_ref,
+    e1_ref,
+    low_ref,
     chip_ref,
     far_ref,
-    packed_ref,
+    out_sems,
+):
+    slab, width_x = e_ref.shape[1], e_ref.shape[2]
+    top = slab - 1
+    odd = odd_device()
+    over_rows(width_x, lambda c: magnetic_step(c, e_ref, h_ref, h1_ref))
+
+    def electric(c):
+        for z, ref, comps in ((0, low_ref, 2), (top, e1_ref, 3)):
+            ca, cb = coefficients(c, eps_ref, sigma_ref, z)
+            for k, v in enumerate(electric_step(c, z, comps, e_ref, h1_ref, ca, cb)):
+                c.put(ref, k, v)
+
+    over_rows(width_x, electric)
+
+    def boundary(c):
+        ex, ey, ez = (c.get(e1_ref, k) for k in range(3))
+        hx = c.get(h1_ref, 0, top) - HALF * (ahead_y(ez) + ey)
+        hy = c.get(h1_ref, 1, top) + HALF * (ex + c.ahead_x(e1_ref, 2))
+        upward = (hx, hy)
+        downward = (c.get(low_ref, 0), c.get(low_ref, 1))
+        for k in range(2):
+            c.put(chip_ref, k, jnp.where(odd, downward[k], upward[k]))
+            c.put(far_ref, k, jnp.where(odd, upward[k], downward[k]))
+
+    part = width_x // PARTS
+    out = []
+    for g in range(PARTS):
+        over_rows(width_x, boundary, g * part, (g + 1) * part)
+        out = out + send_rows(g, part, chip_ref, far_ref, chip_hbm, far_hbm, out_sems)
+    for copy in out:
+        copy.wait()
+
+
+def place_entries(
+    cap,
+    got_hbm,
+    e_ref,
+    h_ref,
+    eps_ref,
+    sigma_ref,
+    timing_ref,
+    own_ref,
+    below_ref,
+    above_ref,
     h1_ref,
     e1_ref,
     ca_ref,
     cb_ref,
+    got_ref,
+    sem,
 ):
-    slab, width_x, width_y = e_ref.shape[1], e_ref.shape[2], e_ref.shape[3]
-    top = slab - 1
-    odd = odd_device()
-    pack_entries(
-        owners_ref, cells_ref, amplitude_ref, packed_ref, slab, top, width_x, width_y, cap
-    )
-
-    def magnetic(c):
-        for z in range(slab):
-            ex, ey, ez = (c.get(e_ref, k, z) for k in range(3))
-            up_x = c.get(e_ref, 0, z + 1) - ex if z < top else -ex
-            up_y = c.get(e_ref, 1, z + 1) - ey if z < top else -ey
-            c.put(h1_ref, 0, z, c.get(h_ref, 0, z) - HALF * (ahead_y(ez) - up_y))
-            c.put(h1_ref, 1, z, c.get(h_ref, 1, z) - HALF * (up_x - c.ahead_x(e_ref, 2, z)))
-            c.put(h1_ref, 2, z, c.get(h_ref, 2, z) - HALF * (c.ahead_x(e_ref, 1, z) - ahead_y(ex)))
-
-    over_rows(width_x, magnetic)
-
-    def electric(c):
-        for z in range(slab):
-            cb, eps, sigma = coefficient(c, eps_ref, sigma_ref, z)
-            ca = (2.0 * eps - sigma) * cb
-            c.put(ca_ref, z, ca)
-            c.put(cb_ref, z, cb)
-            hx, hy, hz = (c.get(h1_ref, k, z) for k in range(3))
-            by_x, by_y = behind_y(hx), behind_y(hz)
-            if z > 0:
-                down_x, down_y = hx - c.get(h1_ref, 0, z - 1), hy - c.get(h1_ref, 1, z - 1)
-            else:
-                down_x, down_y = hx, hy
-            ex = ca * c.get(e_ref, 0, z) + cb * (by_y - down_y)
-            ey = ca * c.get(e_ref, 1, z) + cb * (down_x - c.behind_x(h1_ref, 2, z))
-            ez = ca * c.get(e_ref, 2, z) + cb * (c.behind_x(h1_ref, 1, z) - by_x)
-            c.put(e1_ref, 0, z, ex)
-            c.put(e1_ref, 1, z, ey)
-            c.put(e1_ref, 2, z, ez)
-
-    over_rows(width_x, electric)
-
-    def boundary(c):
-        ex, ey, ez = (c.get(e1_ref, k, top) for k in range(3))
-        hx = c.get(h1_ref, 0, top) - HALF * (ahead_y(ez) + ey)
-        hy = c.get(h1_ref, 1, top) + HALF * (ex + c.ahead_x(e1_ref, 2, top))
-        upward = (hx, hy)
-        downward = (c.get(e1_ref, 0, 0), c.get(e1_ref, 1, 0))
-        for k in range(2):
-            c.put(chip_ref, k, jnp.where(odd, downward[k], upward[k]))
-            c.put(far_ref, k, jnp.where(odd, upward[k], downward[k]))
-
-    over_rows(width_x, boundary)
-
-
-def place_entries(cap, slab, got_ref, own_ref, below_ref, above_ref):
+    arrive = pltpu.make_async_copy(got_hbm, got_ref, sem)
+    arrive.start()
+    over_rows(e_ref.shape[2], lambda c: magnetic_step(c, e_ref, h_ref, h1_ref))
+    arrive.wait()
     peers, _, lanes = got_ref.shape
-    width_x, width_y = own_ref.shape[2], own_ref.shape[3]
+    slab, width_x, width_y = own_ref.shape[1:]
     group = LANES // cap
     part = lax.broadcasted_iota(jnp.int32, (8, LANES), 1) // cap
 
@@ -259,6 +336,18 @@
     fill(0, 0, slab * width_x, 3, store_own)
     fill(1, (slab - 1) * width_x, width_x, 3, store_below)
     fill(2, 0, width_x, 2, store_above)
+
+    wave0 = timing_ref[0, 0]
+
+    def electric(c):
+        for z in range(slab):
+            ca, cb = coefficients(c, eps_ref, sigma_ref, z)
+            c.put(ca_ref, z, ca)
+            c.put(cb_ref, z, cb)
+            for k, v in enumerate(electric_step(c, z, 3, e_ref, h1_ref, ca, cb)):
+                c.put(e1_ref, k, z, v - wave0 * cb * c.get(own_ref, k, z))
+
+    over_rows(width_x, electric)
 
 
 def inside(c, bounds_ref, z, slab, shape):
@@ -311,10 +400,7 @@
         hay = has_below * (low[1] - HALF * ex)
         cb_a, cb_b = low[2], high[2]
         cb = [c.get(cb_ref, z) for z in range(slab)]
-        e1 = [
-            [c.get(e1_ref, k, z) - wave0 * cb[z] * c.get(own_ref, k, z) for k in range(3)]
-            for z in range(slab)
-        ]
+        e1 = [[c.get(e1_ref, k, z) for k in range(3)] for z in range(slab)]
         e1[0][0] = e1[0][0] + cb[0] * hay
         e1[0][1] = e1[0][1] - cb[0] * hax
         hx = c.get(h1_ref, 0, top) + HALF * high[1]
@@ -396,14 +482,27 @@
     far_ref,
     timing_ref,
     bounds_ref,
-    eout_ref,
-    hout_ref,
+    eout_hbm,
+    hout_hbm,
+    grad_hbm,
+    e_ref,
+    h_ref,
     grad_ref,
+    sems,
+    rest_sems,
 ):
     slab, width_x = e2_ref.shape[1], e2_ref.shape[2]
     top = slab - 1
     odd = odd_device()
     weight1 = timing_ref[1, 1]
+    rest = [
+        (h2_ref.at[0:2, 0:top], hout_hbm.at[0:2, 0:top]),
+        (h2_ref.at[2], hout_hbm.at[2]),
+        (e2_ref.at[2, 0:top], eout_hbm.at[2, 0:top]),
+    ]
+    rest = [pltpu.make_async_copy(a, b, rest_sems.at[i]) for i, (a, b) in enumerate(rest)]
+    for copy in rest:
+        copy.start()
 
     def body(c):
         chip = [c.get(chip_ref, k) for k in range(2)]
@@ -411,48 +510,80 @@
         low = [jnp.where(odd, a, b) for a, b in zip(chip, far)]
         high = [jnp.where(odd, b, a) for a, b in zip(chip, far)]
         bx = jnp.where(odd, c.behind_x(far_ref, 0), c.behind_x(chip_ref, 0))
-        more = [[None] * 3 for _ in range(slab)]
         cb_low, cb_top = c.get(cb_ref, 0), HALF * c.get(cb_ref, top)
+        more = [[0.0] * 3 for _ in range(slab)]
         more[0][0] = cb_low * low[1]
         more[0][1] = -cb_low * low[0]
-        more[top][0] = cb_top * high[0]
-        more[top][1] = cb_top * high[1]
+        more[top][0] = more[top][0] + cb_top * high[0]
+        more[top][1] = more[top][1] + cb_top * high[1]
         more[top][2] = -cb_top * (bx + behind_y(high[1]))
         for z in range(slab):
             dot = 0.0
-            for k in range(3):
-                e2 = c.get(e2_ref, k, z)
-                if more[z][k] is not None:
-                    e2 = e2 + more[z][k]
-                    dot = dot + more[z][k] * c.get(forward_ref, k, z)
-                c.put(eout_ref, k, z, e2)
+            for k in range(3 if z == top else 2):
+                delta = more[z][k]
+                dot = dot + delta * c.get(forward_ref, k, z)
+                c.put(e_ref, k, z, c.get(e2_ref, k, z) + delta)
             mask = inside(c, bounds_ref, z, slab, cb_low.shape)
             c.put(grad_ref, z, c.get(gradp_ref, z) + (weight1 * mask) * dot)
-            hx, hy = c.get(h2_ref, 0, z), c.get(h2_ref, 1, z)
-            if z == top:
-                hx, hy = hx + HALF * high[1], hy - HALF * high[0]
-            c.put(hout_ref, 0, z, hx)
-            c.put(hout_ref, 1, z, hy)
-            c.put(hout_ref, 2, z, c.get(h2_ref, 2, z))
-
-    over_rows(width_x, body)
+        c.put(h_ref, 0, c.get(h2_ref, 0, top) + HALF * high[1])
+        c.put(h_ref, 1, c.get(h2_ref, 1, top) - HALF * high[0])
+
+    part = width_x // PARTS
+    copies = []
+    for g in range(PARTS):
+        over_rows(width_x, body, g * part, (g + 1) * part)
+        rows = pl.ds(g * part, part)
+        pairs = (
+            (e_ref.at[0:2, :, rows], eout_hbm.at[0:2, :, rows]),
+            (e_ref.at[2, top, rows], eout_hbm.at[2, top, rows]),
+            (h_ref.at[:, rows], hout_hbm.at[0:2, top, rows]),
+            (grad_ref.at[:, rows], grad_hbm.at[:, rows]),
+        )
+        for i, (a, b) in enumerate(pairs):
+            copy = pltpu.make_async_copy(a, b, sems.at[g, i])
+            copy.start()
+            copies.append(copy)
+    for copy in rest + copies:
+        copy.wait()
 
 
 def shape(*dims):
     return jax.ShapeDtypeStruct(dims, F32)
 
 
-def call(body, outs, ins, flops, scratch=()):
-    total = sum(8 * x.size for x in jax.tree.leaves((outs, list(ins))))
+def kept(*dims):
+    return VMEM(dims, F32)
+
+
+def sent(*dims):
+    return pltpu.HBM(dims, F32)
+
+
+def call(body, outs, ins, flops, limit, scratch=(), in_hbm=(), anywhere=(), out_hbm=False):
+    total = sum(
+        4 * math.prod(x.shape) for x in jax.tree.leaves(outs) + list(ins)
+    )
+
+    def place(i, x):
+        if i in in_hbm:
+            return pl.BlockSpec(memory_space=pltpu.HBM)
+        if i in anywhere:
+            return pl.BlockSpec(memory_space=pl.ANY)
+        return pl.BlockSpec(memory_space=SMEM if x.size < 16 else VMEM)
+
+    ins = [
+        pltpu.with_memory_space_constraint(x, pltpu.HBM) if i in in_hbm else x
+        for i, x in enumerate(ins)
+    ]
     return pl.pallas_call(
         body,
         out_shape=outs,
-        in_specs=[
-            pl.BlockSpec(memory_space=SMEM if x.size < 16 else VMEM) for x in ins
-        ],
-        out_specs=jax.tree.map(lambda _: pl.BlockSpec(memory_space=VMEM), outs),
+        in_specs=[place(i, x) for i, x in enumerate(ins)],
+        out_specs=jax.tree.map(
+            lambda _: pl.BlockSpec(memory_space=pltpu.HBM if out_hbm else VMEM), outs
+        ),
         scratch_shapes=list(scratch),
-        compiler_params=pltpu.CompilerParams(vmem_limit_bytes=40 * 1024 * 1024),
+        compiler_params=pltpu.CompilerParams(vmem_limit_bytes=limit << 20),
         cost_estimate=pl.CostEstimate(flops=flops, bytes_accessed=total, transcendentals=0),
     )(*ins)
 
@@ -480,46 +611,73 @@
 
     chip1, far1 = call(
         halves_first,
-        (shape(3, wx, wy), shape(3, wx, wy)),
+        (sent(3, wx, wy), sent(3, wx, wy)),
         (e_field, h_field, permittivity, conductivity),
         cells_all * 20,
+        8,
+        scratch=(
+            VMEM((3, wx, wy), F32),
+            VMEM((2, wx, wy), F32),
+            VMEM((2, wx, wy), F32),
+            VMEM((2, slab, wx, wy), F32),
+            VMEM((3, wx, wy), F32),
+            VMEM((3, wx, wy), F32),
+            pltpu.SemaphoreType.DMA((PARTS, 5)),
+            pltpu.SemaphoreType.DMA((PARTS, 2)),
+        ),
+        in_hbm=(0, 1, 2, 3),
+        out_hbm=True,
     )
     far1 = lax.ppermute(far1, "gz", far_pairs)
     chip1 = lax.ppermute(chip1, "gz", chip_pairs)
-    chip2, far2, packed, h1, e1, ca, cb = call(
-        functools.partial(halves_second, cap),
-        (
-            shape(2, wx, wy),
-            shape(2, wx, wy),
-            shape(peers, 8, lanes),
-            shape(3, slab, wx, wy),
-            shape(3, slab, wx, wy),
-            shape(slab, wx, wy),
-            shape(slab, wx, wy),
+    packed = call(
+        functools.partial(pack_entries, cap, slab - 1, wx, wy),
+        shape(peers, 8, lanes),
+        (owners.reshape(1, rows), cells.reshape(1, rows), amplitude),
+        cells_all * 10,
+        8,
+    )
+    got = lax.all_to_all(packed, "gz", 0, 0, tiled=True)
+    chip2, far2 = call(
+        halves_second,
+        (sent(2, wx, wy), sent(2, wx, wy)),
+        (e_field, h_field, permittivity, conductivity, packed),
+        cells_all * 60,
+        16,
+        scratch=(
+            VMEM((3, slab, wx, wy), F32),
+            VMEM((3, wx, wy), F32),
+            VMEM((2, wx, wy), F32),
+            VMEM((2, wx, wy), F32),
+            VMEM((2, wx, wy), F32),
+            pltpu.SemaphoreType.DMA((PARTS, 2)),
         ),
-        (
-            e_field,
-            h_field,
-            permittivity,
-            conductivity,
-            owners.reshape(1, rows),
-            cells.reshape(1, rows),
-            amplitude,
-        ),
-        cells_all * 60,
-    )
-    got = lax.all_to_all(packed, "gz", 0, 0, tiled=True)
+        in_hbm=(4,),
+        out_hbm=True,
+    )
+    _, far2, chip2 = lax.optimization_barrier((got, far2, chip2))
     far2 = lax.ppermute(far2, "gz", far_pairs)
     chip2 = lax.ppermute(chip2, "gz", chip_pairs)
-    own, sbelow, sabove = call(
-        functools.partial(place_entries, cap, slab),
-        (shape(3, slab, wx, wy), shape(3, wx, wy), shape(2, wx, wy)),
-        (got,),
+    own, sbelow, sabove, h1, e1, ca, cb = call(
+        functools.partial(place_entries, cap),
+        (
+            kept(3, slab, wx, wy),
+            kept(3, wx, wy),
+            kept(2, wx, wy),
+            kept(3, slab, wx, wy),
+            kept(3, slab, wx, wy),
+            kept(slab, wx, wy),
+            kept(slab, wx, wy),
+        ),
+        (got, e_field, h_field, permittivity, conductivity, timing),
         cells_all * 60,
+        16,
+        scratch=(VMEM((peers, 8, lanes), F32), pltpu.SemaphoreType.DMA),
+        anywhere=(0,),
     )
     h2, e2, grad = call(
         middle,
-        (shape(3, slab, wx, wy), shape(3, slab, wx, wy), shape(slab, wx, wy)),
+        (kept(3, slab, wx, wy), kept(3, slab, wx, wy), kept(slab, wx, wy)),
         (
             e_field,
             forward_field,
@@ -536,6 +694,7 @@
             bounds,
         ),
         cells_all * 100,
+        24,
         scratch=(
             VMEM((3, slab, wx, wy), F32),
             VMEM((2, wx, wy), F32),
@@ -549,6 +708,15 @@
         (shape(3, slab, wx, wy), shape(3, slab, wx, wy), shape(slab, wx, wy)),
         (forward_field, h2, e2, grad, cb, chip2, far2, timing, bounds),
         cells_all * 20,
+        16,
+        scratch=(
+            VMEM((3, slab, wx, wy), F32),
+            VMEM((2, wx, wy), F32),
+            VMEM((slab, wx, wy), F32),
+            pltpu.SemaphoreType.DMA((PARTS, 4)),
+            pltpu.SemaphoreType.DMA((3,)),
+        ),
+        out_hbm=True,
     )
 
 

time: 50.3 us -> 41 us (0.82)
  the two profiles are of different devices: /device:TPU:0 before, /device:TPU:1 now
where the time goes in v2:
time: 41 us; the launch traced here: 40.4 us
  Pallas kernels  21.3 us (52%)
  starting transfers between devices  13.7 us (33%)
  waiting for transfers between devices  3.02 us (7%)
  local copies, waits for them, and re-layouts  1.61 us (4%)
  between operations  0.86 us (2%)
    pallas_call x6, Pallas kernels, call(): pl.pallas_call(body, out_shape=outs, in_specs=[place(i, x) for i, x in en...  21.3 us
    all_to_all x1, starting transfers between devices, local(): got = lax.all_to_all(packed, 'gz', 0, 0, tiled=True)  5.31 us
    ppermute x1, starting transfers between devices, local(): far1 = lax.ppermute(far1, 'gz', far_pairs)  4.5 us
    all_to_all x1, waiting for transfers between devices, local(): got = lax.all_to_all(packed, 'gz', 0, 0, tiled=True)  3.01 us
    ppermute x1, starting transfers between devices, local(): far2 = lax.ppermute(far2, 'gz', far_pairs)  2.78 us
    unnamed x25, local copies, waits for them, and re-layouts  1.61 us
    ppermute x1, starting transfers between devices, local(): chip2 = lax.ppermute(chip2, 'gz', chip_pairs)  0.95 us
  transfers between devices with their start and end apart: 5, of which 1 were waited for; matrix products, arithmetic and copies ran while one was open for 0% of the time, Pallas kernels for 38%

profile of v2, /device:TPU:1, one launch (start us, length us, event | category | flops | bytes accessed | tf_op | source)
XLA Modules:
  0.0 40.4 jit_solution(13030123343270673562)
XLA Ops:
  0.7 3.1 %shard_map.123 = (f32[3,192,256]{2,1,0:T(8,128)}, f32[3,192,256]{2,1,0:T(8,128)}) custom-call(f32[3,2,192,256]{3,2,1,0:T(8,128)} %e_ref.5, f32[3,2,192,256]{3,2,1,0:T(8,128)} %h_ref.3, f32[2,192,256]{2,1,0:T(8,128)} %eps_ref.3, f32[2,192,256]{2,1,0:T(8,128)} %sigma_ref.3), custom_call_target="tpu_custom_call" | custom-call | flops 1966080 | bytes 4325376 | tf_op jit(solution)/shard_map/pallas_call | solution.py:578
  3.8 0.1 collective-permute-start
  3.9 4.5 %collective-permute-start.1 = (f32[3,192,256]{2,1,0:T(8,128)}, f32[3,192,256]{2,1,0:T(8,128)}, u32[]{:S(2)}, u32[]{:S(2)}) collective-permute-start(f32[3,192,256]{2,1,0:T(8,128)} %get-tuple-element.27), channel_id=1, source_target_pairs={{1,2},{2,1},{3,4},{4,3},{5,6},{6,5},{7,8},{8,7},{9,10},{10,9},{11,... | collective-permute-start | bytes 1769480 | tf_op jit(solution)/shard_map/ppermute | solution.py:631
  8.4 0.0 copy-done.9
  8.4 0.0 copy-done.10
  8.4 0.0 copy-done.8
  8.4 3.4 %shard_map.121.packed_hbm = f32[16,8,128]{2,1,0:T(8,128)} custom-call(s32[1,256]{1,0:T(1,128)S(1)} %bitcast.2, s32[1,256]{1,0:T(1,128)S(1)} %bitcast.3, f32[3,256]{1,0:T(4,128)S(1)} %copy-done.8), custom_call_target="tpu_custom_call" | custom-call | flops 983040 | bytes 70656 | tf_op jit(solution)/shard_map/pallas_call | solution.py:578
  11.9 5.3 %all-to-all-start = ((f32[16,8,128]{2,1,0:T(8,128)}), f32[16,8,128]{2,1,0:T(8,128)S(1)}, u32[]{:S(2)}, u32[]{:S(2)}) async-start(f32[16,8,128]{2,1,0:T(8,128)} %shard_map.121.packed_hbm), calls=%async_computation | async-start | bytes 131072 | tf_op jit(solution)/shard_map/all_to_all | solution.py:640
  17.2 0.0 copy-start.11
  17.2 0.0 copy-start.7
  17.2 3.0 %shard_map.125 = (f32[2,192,256]{2,1,0:T(8,128)}, f32[2,192,256]{2,1,0:T(8,128)}) custom-call(f32[3,2,192,256]{3,2,1,0:T(8,128)S(1)} %copy-done, f32[3,2,192,256]{3,2,1,0:T(8,128)S(1)} %copy-done.1, f32[2,192,256]{2,1,0:T(8,128)S(1)} %copy-done.3, f32[2,192,256]{2,1,0:T(8,128)S(1)} %copy-done.4, f32[16,8,128]{2,1,0:T(8,128)} %shard_map.121.packed_hbm), custom_call_target="tpu_custom_call" | custom-call | flops 5898240 | bytes 3997696 | tf_op jit(solution)/shard_map/pallas_call | solution.py:578
  20.2 3.0 %all-to-all-done.got_hbm = f32[16,8,128]{2,1,0:T(8,128)S(1)} async-done(((f32[16,8,128]{2,1,0:T(8,128)}), f32[16,8,128]{2,1,0:T(8,128)S(1)}, u32[]{:S(2)}, u32[]{:S(2)}) %all-to-all-start) | async-done | bytes 65568 | tf_op jit(solution)/shard_map/all_to_all | solution.py:640
  23.2 0.6 %copy-done.5 = f32[16,8,128]{2,1,0:T(8,128)} copy-done((f32[16,8,128]{2,1,0:T(8,128)}, f32[16,8,128]{2,1,0:T(8,128)S(1)}, u32[]{:S(2)}) %copy-start.5) | copy-done | bytes 65560
  23.8 1.0 %collective-permute-start.2 = (f32[2,192,256]{2,1,0:T(8,128)}, f32[2,192,256]{2,1,0:T(8,128)S(1)}, u32[]{:S(2)}, u32[]{:S(2)}) collective-permute-start(f32[2,192,256]{2,1,0:T(8,128)} %get-tuple-element.33), channel_id=1, source_target_pairs={{0,1},{1,0},{2,3},{3,2},{4,5},{5,4},{6,7},{7,6},{8,9},{9,8},{10,11... | collective-permute-start | bytes 1179656 | tf_op jit(solution)/shard_map/ppermute | solution.py:660
  24.8 2.8 %collective-permute-start.3 = (f32[2,192,256]{2,1,0:T(8,128)}, f32[2,192,256]{2,1,0:T(8,128)}, u32[]{:S(2)}, u32[]{:S(2)}) collective-permute-start(f32[2,192,256]{2,1,0:T(8,128)} %get-tuple-element.34), channel_id=1, source_target_pairs={{1,2},{2,1},{3,4},{4,3},{5,6},{6,5},{7,8},{8,7},{9,10},{10,9},{11,... | collective-permute-start | bytes 1179656 | tf_op jit(solution)/shard_map/ppermute | solution.py:659
  27.6 0.1 copy.13.bounds_ref
  27.7 0.8 %copy-done.6 = f32[16,8,128]{2,1,0:T(8,128)S(1)} copy-done((f32[16,8,128]{2,1,0:T(8,128)S(1)}, f32[16,8,128]{2,1,0:T(8,128)}, u32[]{:S(2)}) %copy-start.6) | copy-done | bytes 65560
  28.5 4.7 %shard_map.122 = (f32[3,2,192,256]{3,2,1,0:T(8,128)S(1)}, f32[3,192,256]{2,1,0:T(8,128)S(1)}, f32[2,192,256]{2,1,0:T(8,128)S(1)}, f32[3,2,192,256]{3,2,1,0:T(8,1...) custom-call(f32[16,8,128]{2,1,0:T(8,128)S(1)} %copy-done.6, ...), custom_call_target="tpu_custom_call" | custom-call | flops 5898240 | bytes 8519696 | tf_op jit(solution)/shard_map/pallas_call | solution.py:578
  33.2 0.0 collective-permute-done.chip_ref
  33.2 0.0 collective-permute-done.1.far_ref
  33.3 4.3 %shard_map.124 = (f32[3,2,192,256]{3,2,1,0:T(8,128)S(1)}, f32[3,2,192,256]{3,2,1,0:T(8,128)S(1)}, f32[2,192,256]{2,1,0:T(8,128)S(1)}) custom-call(f32[3,2,192,256]{3,2,1,0:T(8,128)S(1)} %copy-done, f32[3,2,192,256]{3,2,1,0:T(8,128)S(1)} %copy-done.2, f32[3,2,192,256]{3,2,1,0:T(8,128)S(1)} %get-tuple-element.19.h1_ref, ...), custom_call_target="tpu_custom_call" | custom-call | flops 9830400 | bytes 11599912 | tf_op jit(solution)/shard_map/pallas_call | solution.py:578
  37.6 0.0 collective-permute-done.2.chip_ref
  37.6 0.0 collective-permute-done.3.far_ref
  37.6 2.8 %shard_map.126 = (f32[3,2,192,256]{3,2,1,0:T(8,128)}, f32[3,2,192,256]{3,2,1,0:T(8,128)}, f32[2,192,256]{2,1,0:T(8,128)}) custom-call(f32[3,2,192,256]{3,2,1,0:T(8,128)S(1)} %copy-done.2, f32[3,2,192,256]{3,2,1,0:T(8,128)S(1)} %get-tuple-element.28.h2_ref, f32[3,2,192,256]{3,2,1,0:T(8,128)S(1)} %get-tuple-element.29.e2_ref, ...), custom_call_target="tpu_custom_call" | custom-call | flops 1966080 | bytes 7864360 | tf_op jit(solution)/shard_map/pallas_call | solution.py:578
  (17 shorter events, 0.0 us)
Async XLA Ops:
  0.6 16.5 %copy-start = (f32[3,2,192,256]{3,2,1,0:T(8,128)S(1)}, f32[3,2,192,256]{3,2,1,0:T(8,128)}, u32[]{:S(2)}) copy-start(f32[3,2,192,256]{3,2,1,0:T(8,128)} %e_ref.5) | copy-start | bytes 3538948
  0.6 16.5 %copy-start.1 = (f32[3,2,192,256]{3,2,1,0:T(8,128)S(1)}, f32[3,2,192,256]{3,2,1,0:T(8,128)}, u32[]{:S(2)}) copy-start(f32[3,2,192,256]{3,2,1,0:T(8,128)} %h_ref.3) | copy-start | bytes 3538948
  0.7 16.5 %copy-start.3 = (f32[2,192,256]{2,1,0:T(8,128)S(1)}, f32[2,192,256]{2,1,0:T(8,128)}, u32[]{:S(2)}) copy-start(f32[2,192,256]{2,1,0:T(8,128)} %eps_ref.3) | copy-start | bytes 1179652
  0.7 16.5 %copy-start.4 = (f32[2,192,256]{2,1,0:T(8,128)S(1)}, f32[2,192,256]{2,1,0:T(8,128)}, u32[]{:S(2)}) copy-start(f32[2,192,256]{2,1,0:T(8,128)} %sigma_ref.3) | copy-start | bytes 1179652
  0.7 7.7 %copy-start.9 = (s32[256,1]{0,1:T(1,128)S(1)}, s32[256,1]{0,1:T(1,128)}, u32[]{:S(2)}) copy-start(s32[256,1]{0,1:T(1,128)} %param.15) | copy-start | bytes 3076
  0.7 7.7 %copy-start.10 = (s32[256,1]{0,1:T(1,128)S(1)}, s32[256,1]{0,1:T(1,128)}, u32[]{:S(2)}) copy-start(s32[256,1]{0,1:T(1,128)} %param.16) | copy-start | bytes 3076
  0.7 7.7 %copy-start.8 = (f32[3,256]{1,0:T(4,128)S(1)}, f32[3,256]{1,0:T(4,128)}, u32[]{:S(2)}) copy-start(f32[3,256]{1,0:T(4,128)} %amplitude_ref.1) | copy-start | bytes 9220
  3.8 29.5 %collective-permute-start = (f32[3,192,256]{2,1,0:T(8,128)}, f32[3,192,256]{2,1,0:T(8,128)}, u32[]{:S(2)}, u32[]{:S(2)}) collective-permute-start(f32[3,192,256]{2,1,0:T(8,128)} %get-tuple-element.26), channel_id=1, source_target_pairs={{0,1},{1,0},{2,3},{3,2},{4,5},{5,4},{6,7},{7,6},{8,9},{9,8},{10,11... | collective-permute-start | bytes 1769480 | tf_op jit(solution)/shard_map/ppermute | solution.py:632
  3.9 29.3 %collective-permute-start.1 = (f32[3,192,256]{2,1,0:T(8,128)}, f32[3,192,256]{2,1,0:T(8,128)}, u32[]{:S(2)}, u32[]{:S(2)}) collective-permute-start(f32[3,192,256]{2,1,0:T(8,128)} %get-tuple-element.27), channel_id=1, source_target_pairs={{1,2},{2,1},{3,4},{4,3},{5,6},{6,5},{7,8},{8,7},{9,10},{10,9},{11,... | collective-permute-start | bytes 1769480 | tf_op jit(solution)/shard_map/ppermute | solution.py:631
  11.9 11.4 %all-to-all-start = ((f32[16,8,128]{2,1,0:T(8,128)}), f32[16,8,128]{2,1,0:T(8,128)S(1)}, u32[]{:S(2)}, u32[]{:S(2)}) async-start(f32[16,8,128]{2,1,0:T(8,128)} %shard_map.121.packed_hbm), calls=%async_computation | async-start | bytes 131072 | tf_op jit(solution)/shard_map/all_to_all | solution.py:640
  17.2 10.4 %copy-start.11 = (s32[3,2]{0,1:T(2,128)S(1)}, s32[3,2]{0,1:T(2,128)}, u32[]{:S(2)}) copy-start(s32[3,2]{0,1:T(2,128)} %param.19) | copy-start | bytes 76
  17.2 10.5 %copy-start.7 = (f32[2,2]{1,0:T(2,128)S(1)}, f32[2,2]{1,0:T(2,128)}, u32[]{:S(2)}) copy-start(f32[2,2]{1,0:T(2,128)} %timing_ref.5) | copy-start | bytes 52
  23.2 0.6 %copy-start.5 = (f32[16,8,128]{2,1,0:T(8,128)}, f32[16,8,128]{2,1,0:T(8,128)S(1)}, u32[]{:S(2)}) copy-start(f32[16,8,128]{2,1,0:T(8,128)S(1)} %all-to-all-done.got_hbm) | copy-start | bytes 196612
  23.8 13.7 %collective-permute-start.2 = (f32[2,192,256]{2,1,0:T(8,128)}, f32[2,192,256]{2,1,0:T(8,128)S(1)}, u32[]{:S(2)}, u32[]{:S(2)}) collective-permute-start(f32[2,192,256]{2,1,0:T(8,128)} %get-tuple-element.33), channel_id=1, source_target_pairs={{0,1},{1,0},{2,3},{3,2},{4,5},{5,4},{6,7},{7,6},{8,9},{9,8},{10,11... | collective-permute-start | bytes 1179656 | tf_op jit(solution)/shard_map/ppermute | solution.py:660
  24.8 12.8 %collective-permute-start.3 = (f32[2,192,256]{2,1,0:T(8,128)}, f32[2,192,256]{2,1,0:T(8,128)}, u32[]{:S(2)}, u32[]{:S(2)}) collective-permute-start(f32[2,192,256]{2,1,0:T(8,128)} %get-tuple-element.34), channel_id=1, source_target_pairs={{1,2},{2,1},{3,4},{4,3},{5,6},{6,5},{7,8},{8,7},{9,10},{10,9},{11,... | collective-permute-start | bytes 1179656 | tf_op jit(solution)/shard_map/ppermute | solution.py:659
  27.7 0.8 %copy-start.6 = (f32[16,8,128]{2,1,0:T(8,128)S(1)}, f32[16,8,128]{2,1,0:T(8,128)}, u32[]{:S(2)}) copy-start(f32[16,8,128]{2,1,0:T(8,128)} %copy-done.5) | copy-start | bytes 196612
  28.5 4.7 %copy-start.2 = (f32[3,2,192,256]{3,2,1,0:T(8,128)S(1)}, f32[3,2,192,256]{3,2,1,0:T(8,128)}, u32[]{:S(2)}) copy-start(f32[3,2,192,256]{3,2,1,0:T(8,128)} %forward_ref.3) | copy-start | bytes 3538948

commit v3 on v2

--- a/solution.py
+++ b/solution.py
@@ -1,5 +1,4 @@
 import functools
-import math
 
 import jax
 import jax.numpy as jnp
@@ -11,6 +10,7 @@
 STEPS = 2
 ROWS = 24
 PARTS = 4
+FLOPS_US = 1.15e9
 LANES = 128
 HALF = 0.5
 F32 = jnp.float32
@@ -153,7 +153,7 @@
     return one, two, three
 
 
-def pack_entries(cap, top, width_x, width_y, owners_ref, cells_ref, amplitude_ref, packed_ref):
+def pack_entries(cap, top, width_x, width_y, owners_ref, cells_ref, amplitude_ref, after_hbm, packed_ref):
     peers, _, lanes = packed_ref.shape
     owner, cell, amp = owners_ref[...], cells_ref[...], amplitude_ref[...]
     entries = owner.shape[1]
@@ -165,29 +165,32 @@
     before = jnp.dot(hot, ahead, preferred_element_type=F32)
     rank = jnp.sum(jnp.where(named, before, 0.0), axis=0, keepdims=True).astype(jnp.int32)
     layer = width_x * width_y
-    own = owner * lanes + rank
-    above = jnp.where((cell >= top * layer) & (owner + 1 < peers), own + (lanes + cap), -1)
-    below = jnp.where((cell < layer) & (owner > 0), own + (2 * cap - lanes), -1)
+    spread = lambda v: jnp.broadcast_to(v, (8, entries))
+    names = (
+        spread(owner),
+        spread(jnp.where(cell >= top * layer, owner + 1, -1)),
+        spread(jnp.where(cell < layer, owner - 1, -1)),
+    )
     line = cell // width_y
     column = cell - line * width_y
     rows = jnp.concatenate(
         [amp, line.astype(F32), column.astype(F32), jnp.zeros((3, entries), F32)], axis=0
     )
-    one, two, three = split3(rows)
-    values = jnp.concatenate(
-        [one.astype(F32), two.astype(F32), three.astype(F32), jnp.zeros((8, entries), F32)], axis=0
-    ).astype(BF16)
     slot = lax.broadcasted_iota(jnp.int32, (lanes, entries), 0)
-
-    def body(d, carry):
-        want = slot + d * lanes
-        hit = (want == own) | (want == above) | (want == below)
-        place = hit.astype(F32).astype(BF16)
+    hits = [(slot == rank + k * cap).astype(F32) for k in range(3)]
+    place = jnp.concatenate(hits, axis=1).astype(BF16)
+    total = None
+    for term in split3(rows):
+        term = term.astype(F32)
+        values = [
+            jnp.concatenate([jnp.where(name == d, term, 0.0) for d in range(peers)], axis=0)
+            for name in names
+        ]
+        values = jnp.concatenate(values, axis=1).astype(BF16)
         out = lax.dot_general(values, place, (((1,), (1,)), ((), ())), preferred_element_type=F32)
-        packed_ref[d] = out[0:8] + out[8:16] + out[16:24]
-        return carry
-
-    lax.fori_loop(0, peers, body, 0)
+        total = out if total is None else total + out
+    for d in range(peers):
+        packed_ref[d] = total[d * 8 : (d + 1) * 8]
 
 
 def magnetic_step(c, e_ref, h_ref, h1_ref):
@@ -266,28 +269,50 @@
         copy.wait()
 
 
-def place_entries(
-    cap,
-    got_hbm,
+def first_step(
     e_ref,
     h_ref,
     eps_ref,
     sigma_ref,
-    timing_ref,
-    own_ref,
-    below_ref,
-    above_ref,
+    after_hbm,
+    h1_hbm,
+    e1_hbm,
+    mat_hbm,
     h1_ref,
     e1_ref,
-    ca_ref,
-    cb_ref,
-    got_ref,
-    sem,
+    mat_ref,
+    h1_sem,
+    sems,
 ):
-    arrive = pltpu.make_async_copy(got_hbm, got_ref, sem)
-    arrive.start()
-    over_rows(e_ref.shape[2], lambda c: magnetic_step(c, e_ref, h_ref, h1_ref))
-    arrive.wait()
+    slab, width_x = e_ref.shape[1], e_ref.shape[2]
+    over_rows(width_x, lambda c: magnetic_step(c, e_ref, h_ref, h1_ref))
+    out = [pltpu.make_async_copy(h1_ref, h1_hbm, h1_sem)]
+    out[0].start()
+
+    def electric(c):
+        for z in range(slab):
+            ca, cb = coefficients(c, eps_ref, sigma_ref, z)
+            c.put(mat_ref, 0, z, ca)
+            c.put(mat_ref, 1, z, cb)
+            for k, v in enumerate(electric_step(c, z, 3, e_ref, h1_ref, ca, cb)):
+                c.put(e1_ref, k, z, v)
+
+    part = width_x // PARTS
+    for g in range(PARTS):
+        over_rows(width_x, electric, g * part, (g + 1) * part)
+        rows = pl.ds(g * part, part)
+        pairs = (
+            (e1_ref.at[:, :, rows], e1_hbm.at[:, :, rows]),
+            (mat_ref.at[:, :, rows], mat_hbm.at[:, :, rows]),
+        )
+        for i, (a, b) in enumerate(pairs):
+            out.append(pltpu.make_async_copy(a, b, sems.at[g, i]))
+            out[-1].start()
+    for copy in out:
+        copy.wait()
+
+
+def place_entries(cap, got_ref, own_ref, below_ref, above_ref):
     peers, _, lanes = got_ref.shape
     slab, width_x, width_y = own_ref.shape[1:]
     group = LANES // cap
@@ -337,18 +362,6 @@
     fill(1, (slab - 1) * width_x, width_x, 3, store_below)
     fill(2, 0, width_x, 2, store_above)
 
-    wave0 = timing_ref[0, 0]
-
-    def electric(c):
-        for z in range(slab):
-            ca, cb = coefficients(c, eps_ref, sigma_ref, z)
-            c.put(ca_ref, z, ca)
-            c.put(cb_ref, z, cb)
-            for k, v in enumerate(electric_step(c, z, 3, e_ref, h1_ref, ca, cb)):
-                c.put(e1_ref, k, z, v - wave0 * cb * c.get(own_ref, k, z))
-
-    over_rows(width_x, electric)
-
 
 def inside(c, bounds_ref, z, slab, shape):
     deep = lax.axis_index("gz") * slab + z
@@ -361,28 +374,49 @@
 
 
 def middle(
+    cap,
     e_ref,
-    forward_ref,
-    h1_ref,
-    e1_ref,
-    ca_ref,
-    cb_ref,
-    own_ref,
-    sbelow_ref,
-    sabove_ref,
-    chip_ref,
-    far_ref,
+    forward_hbm,
+    got_ref,
+    h1_hbm,
+    e1_hbm,
+    mat_hbm,
+    chip_hbm,
+    far_hbm,
     timing_ref,
     bounds_ref,
     h2_ref,
     e2_ref,
     grad_ref,
-    e1s,
-    h1s,
+    cb_ref,
+    forward_ref,
+    h1_ref,
+    e1_ref,
+    mat_ref,
+    chip_ref,
+    far_ref,
+    own_ref,
+    sbelow_ref,
+    sabove_ref,
     fs,
     h2a,
     dza,
+    sems,
 ):
+    pairs = (
+        (far_hbm, far_ref),
+        (chip_hbm, chip_ref),
+        (e1_hbm, e1_ref),
+        (h1_hbm, h1_ref),
+        (mat_hbm, mat_ref),
+        (forward_hbm, forward_ref),
+    )
+    copies = [pltpu.make_async_copy(a, b, sems.at[i]) for i, (a, b) in enumerate(pairs)]
+    for copy in copies:
+        copy.start()
+    place_entries(cap, got_ref, own_ref, sbelow_ref, sabove_ref)
+    for copy in copies[:-1]:
+        copy.wait()
     slab, width_x = e_ref.shape[1], e_ref.shape[2]
     top = slab - 1
     odd = odd_device()
@@ -399,14 +433,17 @@
         hax = has_below * (low[0] + HALF * ey)
         hay = has_below * (low[1] - HALF * ex)
         cb_a, cb_b = low[2], high[2]
-        cb = [c.get(cb_ref, z) for z in range(slab)]
-        e1 = [[c.get(e1_ref, k, z) for k in range(3)] for z in range(slab)]
+        cb = [c.get(mat_ref, 1, z) for z in range(slab)]
+        e1 = [
+            [c.get(e1_ref, k, z) - wave0 * cb[z] * c.get(own_ref, k, z) for k in range(3)]
+            for z in range(slab)
+        ]
         e1[0][0] = e1[0][0] + cb[0] * hay
         e1[0][1] = e1[0][1] - cb[0] * hax
         hx = c.get(h1_ref, 0, top) + HALF * high[1]
         hy = c.get(h1_ref, 1, top) - HALF * high[0]
-        c.put(h1s, 0, hx)
-        c.put(h1s, 1, hy)
+        c.put(h1_ref, 0, top, hx)
+        c.put(h1_ref, 1, top, hy)
         bx_far, bx_chip = c.behind_x(far_ref, 0), c.behind_x(chip_ref, 0)
         bx = jnp.where(odd, bx_far, bx_chip)
         e1[top][0] = e1[top][0] + HALF * cb[top] * high[0]
@@ -416,7 +453,7 @@
         c.put(fs, 1, -cb_b * (hx + wave0 * c.get(sabove_ref, 1)))
         for z in range(slab):
             for k in range(3):
-                c.put(e1s, k, z, e1[z][k])
+                c.put(e1_ref, k, z, e1[z][k])
         dx = cb_a * (HALF * ex - wave0 * c.get(sbelow_ref, 0))
         dy = cb_a * (HALF * ey - wave0 * c.get(sbelow_ref, 1))
         dz = -cb_a * (
@@ -431,23 +468,23 @@
     def second(c):
         c.put(h2a, 1, c.get(h2a, 1) + has_below * HALF * c.ahead_x(dza))
         for z in range(slab):
-            ex, ey, ez = (c.get(e1s, k, z) for k in range(3))
+            ex, ey, ez = (c.get(e1_ref, k, z) for k in range(3))
             if z < top:
-                up_x, up_y = c.get(e1s, 0, z + 1) - ex, c.get(e1s, 1, z + 1) - ey
-                hx, hy = c.get(h1_ref, 0, z), c.get(h1_ref, 1, z)
+                up_x, up_y = c.get(e1_ref, 0, z + 1) - ex, c.get(e1_ref, 1, z + 1) - ey
             else:
                 up_x, up_y = c.get(fs, 0) - ex, c.get(fs, 1) - ey
-                hx, hy = c.get(h1s, 0), c.get(h1s, 1)
+            hx, hy = c.get(h1_ref, 0, z), c.get(h1_ref, 1, z)
             c.put(h2_ref, 0, z, hx - HALF * (ahead_y(ez) - up_y))
-            c.put(h2_ref, 1, z, hy - HALF * (up_x - c.ahead_x(e1s, 2, z)))
+            c.put(h2_ref, 1, z, hy - HALF * (up_x - c.ahead_x(e1_ref, 2, z)))
             hz = c.get(h1_ref, 2, z)
-            c.put(h2_ref, 2, z, hz - HALF * (c.ahead_x(e1s, 1, z) - ahead_y(ex)))
+            c.put(h2_ref, 2, z, hz - HALF * (c.ahead_x(e1_ref, 1, z) - ahead_y(ex)))
 
     over_rows(width_x, second)
 
     def third(c):
         for z in range(slab):
-            ca, cb = c.get(ca_ref, z), c.get(cb_ref, z)
+            ca, cb = c.get(mat_ref, 0, z), c.get(mat_ref, 1, z)
+            c.put(cb_ref, z, cb)
             hx, hy, hz = (c.get(h2_ref, k, z) for k in range(3))
             if z > 0:
                 down_x, down_y = hx - c.get(h2_ref, 0, z - 1), hy - c.get(h2_ref, 1, z - 1)
@@ -460,7 +497,7 @@
             )
             dot1, dot2 = 0.0, 0.0
             for k in range(3):
-                e1 = c.get(e1s, k, z)
+                e1 = c.get(e1_ref, k, z)
                 e2 = ca * e1 + cb * (curl[k] - wave1 * c.get(own_ref, k, z))
                 c.put(e2_ref, k, z, e2)
                 fwd = c.get(forward_ref, k, z)
@@ -469,6 +506,7 @@
             mask = inside(c, bounds_ref, z, slab, ca.shape)
             c.put(grad_ref, z, mask * (weight0 * dot1 + weight1 * dot2))
 
+    copies[-1].wait()
     over_rows(width_x, third)
 
 
@@ -478,16 +516,19 @@
     e2_ref,
     gradp_ref,
     cb_ref,
-    chip_ref,
-    far_ref,
+    chip_hbm,
+    far_hbm,
     timing_ref,
     bounds_ref,
     eout_hbm,
     hout_hbm,
     grad_hbm,
+    chip_ref,
+    far_ref,
     e_ref,
     h_ref,
     grad_ref,
+    in_sems,
     sems,
     rest_sems,
 ):
@@ -495,6 +536,19 @@
     top = slab - 1
     odd = odd_device()
     weight1 = timing_ref[1, 1]
+    part = width_x // PARTS
+    arriving = []
+    for g in range(PARTS):
+        rows = pl.ds(g * part, part)
+        pairs = ((far_hbm, far_ref), (chip_hbm, chip_ref))
+        arriving.append(
+            [
+                pltpu.make_async_copy(a.at[:, rows], b.at[:, rows], in_sems.at[g, i])
+                for i, (a, b) in enumerate(pairs)
+            ]
+        )
+        for copy in arriving[-1]:
+            copy.start()
     rest = [
         (h2_ref.at[0:2, 0:top], hout_hbm.at[0:2, 0:top]),
         (h2_ref.at[2], hout_hbm.at[2]),
@@ -528,9 +582,10 @@
         c.put(h_ref, 0, c.get(h2_ref, 0, top) + HALF * high[1])
         c.put(h_ref, 1, c.get(h2_ref, 1, top) - HALF * high[0])
 
-    part = width_x // PARTS
     copies = []
     for g in range(PARTS):
+        for copy in arriving[g]:
+            copy.wait()
         over_rows(width_x, body, g * part, (g + 1) * part)
         rows = pl.ds(g * part, part)
         pairs = (
@@ -559,11 +614,7 @@
     return pltpu.HBM(dims, F32)
 
 
-def call(body, outs, ins, flops, limit, scratch=(), in_hbm=(), anywhere=(), out_hbm=False):
-    total = sum(
-        4 * math.prod(x.shape) for x in jax.tree.leaves(outs) + list(ins)
-    )
-
+def call(body, outs, ins, us, limit, scratch=(), in_hbm=(), anywhere=(), out_hbm=False):
     def place(i, x):
         if i in in_hbm:
             return pl.BlockSpec(memory_space=pltpu.HBM)
@@ -584,7 +635,7 @@
         ),
         scratch_shapes=list(scratch),
         compiler_params=pltpu.CompilerParams(vmem_limit_bytes=limit << 20),
-        cost_estimate=pl.CostEstimate(flops=flops, bytes_accessed=total, transcendentals=0),
+        cost_estimate=pl.CostEstimate(flops=int(us * FLOPS_US), bytes_accessed=0, transcendentals=0),
     )(*ins)
 
 
@@ -609,113 +660,114 @@
     chip_pairs = [p for i in range(0, peers - 1, 2) for p in ((i, i + 1), (i + 1, i))]
     far_pairs = [p for i in range(1, peers - 1, 2) for p in ((i, i + 1), (i + 1, i))]
 
+    layer, slabs, fields = (wx, wy), (slab, wx, wy), (3, slab, wx, wy)
+    dma = pltpu.SemaphoreType.DMA
     chip1, far1 = call(
         halves_first,
-        (sent(3, wx, wy), sent(3, wx, wy)),
+        (sent(3, *layer), sent(3, *layer)),
         (e_field, h_field, permittivity, conductivity),
-        cells_all * 20,
-        8,
+        3,
+        56,
         scratch=(
-            VMEM((3, wx, wy), F32),
-            VMEM((2, wx, wy), F32),
-            VMEM((2, wx, wy), F32),
-            VMEM((2, slab, wx, wy), F32),
-            VMEM((3, wx, wy), F32),
-            VMEM((3, wx, wy), F32),
-            pltpu.SemaphoreType.DMA((PARTS, 5)),
-            pltpu.SemaphoreType.DMA((PARTS, 2)),
+            VMEM((3, *layer), F32),
+            VMEM((2, *layer), F32),
+            VMEM((2, *layer), F32),
+            VMEM((2, *slabs), F32),
+            VMEM((3, *layer), F32),
+            VMEM((3, *layer), F32),
+            dma((PARTS, 5)),
+            dma((PARTS, 2)),
         ),
         in_hbm=(0, 1, 2, 3),
         out_hbm=True,
     )
+    begun = far1
     far1 = lax.ppermute(far1, "gz", far_pairs)
     chip1 = lax.ppermute(chip1, "gz", chip_pairs)
     packed = call(
         functools.partial(pack_entries, cap, slab - 1, wx, wy),
         shape(peers, 8, lanes),
-        (owners.reshape(1, rows), cells.reshape(1, rows), amplitude),
-        cells_all * 10,
+        (owners.reshape(1, rows), cells.reshape(1, rows), amplitude, begun),
+        1,
         8,
+        in_hbm=(3,),
     )
     got = lax.all_to_all(packed, "gz", 0, 0, tiled=True)
     chip2, far2 = call(
         halves_second,
-        (sent(2, wx, wy), sent(2, wx, wy)),
+        (sent(2, *layer), sent(2, *layer)),
         (e_field, h_field, permittivity, conductivity, packed),
-        cells_all * 60,
+        3,
         16,
         scratch=(
-            VMEM((3, slab, wx, wy), F32),
-            VMEM((3, wx, wy), F32),
-            VMEM((2, wx, wy), F32),
-            VMEM((2, wx, wy), F32),
-            VMEM((2, wx, wy), F32),
-            pltpu.SemaphoreType.DMA((PARTS, 2)),
+            VMEM(fields, F32),
+            VMEM((3, *layer), F32),
+            VMEM((2, *layer), F32),
+            VMEM((2, *layer), F32),
+            VMEM((2, *layer), F32),
+            dma((PARTS, 2)),
         ),
         in_hbm=(4,),
         out_hbm=True,
     )
-    _, far2, chip2 = lax.optimization_barrier((got, far2, chip2))
+    h1, e1, mat = call(
+        first_step,
+        (sent(*fields), sent(*fields), sent(2, *slabs)),
+        (e_field, h_field, permittivity, conductivity, far2),
+        3,
+        16,
+        scratch=(
+            VMEM(fields, F32),
+            VMEM(fields, F32),
+            VMEM((2, *slabs), F32),
+            dma,
+            dma((PARTS, 2)),
+        ),
+        in_hbm=(4,),
+        out_hbm=True,
+    )
     far2 = lax.ppermute(far2, "gz", far_pairs)
     chip2 = lax.ppermute(chip2, "gz", chip_pairs)
-    own, sbelow, sabove, h1, e1, ca, cb = call(
-        functools.partial(place_entries, cap),
-        (
-            kept(3, slab, wx, wy),
-            kept(3, wx, wy),
-            kept(2, wx, wy),
-            kept(3, slab, wx, wy),
-            kept(3, slab, wx, wy),
-            kept(slab, wx, wy),
-            kept(slab, wx, wy),
-        ),
-        (got, e_field, h_field, permittivity, conductivity, timing),
-        cells_all * 60,
-        16,
-        scratch=(VMEM((peers, 8, lanes), F32), pltpu.SemaphoreType.DMA),
-        anywhere=(0,),
-    )
-    h2, e2, grad = call(
-        middle,
-        (kept(3, slab, wx, wy), kept(3, slab, wx, wy), kept(slab, wx, wy)),
-        (
-            e_field,
-            forward_field,
-            h1,
-            e1,
-            ca,
-            cb,
-            own,
-            sbelow,
-            sabove,
-            chip1,
-            far1,
-            timing,
-            bounds,
-        ),
-        cells_all * 100,
+    h2, e2, grad, cb, forward = call(
+        functools.partial(middle, cap),
+        (kept(*fields), kept(*fields), kept(*slabs), kept(*slabs), kept(*fields)),
+        (e_field, forward_field, got, h1, e1, mat, chip1, far1, timing, bounds),
+        6,
         24,
         scratch=(
-            VMEM((3, slab, wx, wy), F32),
-            VMEM((2, wx, wy), F32),
-            VMEM((2, wx, wy), F32),
-            VMEM((2, wx, wy), F32),
-            VMEM((wx, wy), F32),
+            VMEM(fields, F32),
+            VMEM(fields, F32),
+            VMEM((2, *slabs), F32),
+            VMEM((3, *layer), F32),
+            VMEM((3, *layer), F32),
+            VMEM(fields, F32),
+            VMEM((3, *layer), F32),
+            VMEM((2, *layer), F32),
+            VMEM((2, *layer), F32),
+            VMEM((2, *layer), F32),
+            VMEM(layer, F32),
+            dma((6,)),
         ),
+        in_hbm=(1, 3, 4, 5),
+        anywhere=(6, 7),
     )
     return call(
         last,
-        (shape(3, slab, wx, wy), shape(3, slab, wx, wy), shape(slab, wx, wy)),
-        (forward_field, h2, e2, grad, cb, chip2, far2, timing, bounds),
-        cells_all * 20,
+        (shape(*fields), shape(*fields), shape(*slabs)),
+        (forward, h2, e2, grad, cb, chip2, far2, timing, bounds),
+        2.5,
         16,
         scratch=(
-            VMEM((3, slab, wx, wy), F32),
-            VMEM((2, wx, wy), F32),
-            VMEM((slab, wx, wy), F32),
-            pltpu.SemaphoreType.DMA((PARTS, 4)),
-            pltpu.SemaphoreType.DMA((3,)),
+            VMEM((2, *layer), F32),
+            VMEM((2, *layer), F32),
+            VMEM(fields, F32),
+            VMEM((2, *layer), F32),
+            VMEM(slabs, F32),
+            dma((PARTS, 2)),
+            dma((PARTS, 4)),
+            dma((3,)),
         ),
+        anywhere=(5, 6),
         out_hbm=True,
     )
 

time: 41 us -> 36.7 us (0.90)
  waiting for transfers between devices: 3.02 us -> 0.01 us
  Pallas kernels: 21.3 us -> 20.7 us
  local copies, waits for them, and re-layouts: 1.61 us -> 1.12 us
    all_to_all x1, waiting for transfers between devices: 3.01 us -> 0.01 us  [local(): got = lax.all_to_all(packed, 'gz', 0, 0, tiled=True)]
    ppermute x1, starting transfers between devices: 2.78 us -> 3.66 us  [local(): far2 = lax.ppermute(far2, 'gz', far_pairs)]
    pallas_call x6, Pallas kernels: 21.3 us -> 20.7 us  [call(): pl.pallas_call(body, out_shape=outs, in_specs=[place(i, x) for i, x in en...]
    ppermute x1, starting transfers between devices: 0.95 us -> 0.41 us  [local(): chip2 = lax.ppermute(chip2, 'gz', chip_pairs)]
    unnamed x25 -> x19, local copies, waits for them, and re-layouts: 1.61 us -> 1.12 us
  transfers between devices with their start and end apart: 5 -> 5, of which waited for: 1 -> 0; matrix products, arithmetic and copies ran while one was open for 0% -> 0% of each run, Pallas kernels for 38% -> 39%
where the time goes in v3:
time: 36.7 us; the launch traced here: 36.4 us
  Pallas kernels  20.7 us (56%)
  starting transfers between devices  13.8 us (38%)
  local copies, waits for them, and re-layouts  1.12 us (3%)
  between operations  0.8 us (2%)
    pallas_call x6, Pallas kernels, call(): pl.pallas_call(body, out_shape=outs, in_specs=[place(i, x) for i, x in en...  20.7 us
    all_to_all x1, starting transfers between devices, local(): got = lax.all_to_all(packed, 'gz', 0, 0, tiled=True)  5.01 us
    ppermute x1, starting transfers between devices, local(): far1 = lax.ppermute(far1, 'gz', far_pairs)  4.54 us
    ppermute x1, starting transfers between devices, local(): far2 = lax.ppermute(far2, 'gz', far_pairs)  3.66 us
    unnamed x19, local copies, waits for them, and re-layouts  1.12 us
  transfers between devices with their start and end apart: 5, of which 0 were waited for; matrix products, arithmetic and copies ran while one was open for 0% of the time, Pallas kernels for 39%

profile of v3, /device:TPU:1, one launch (start us, length us, event | category | flops | bytes accessed | tf_op | source)
XLA Modules:
  0.0 36.4 jit_solution(18364382470600299038)
XLA Ops:
  0.6 0.0 copy-start.4
  0.7 3.0 %shard_map.121 = (f32[3,192,256]{2,1,0:T(8,128)}, f32[3,192,256]{2,1,0:T(8,128)}) custom-call(f32[3,2,192,256]{3,2,1,0:T(8,128)} %e_ref.5, f32[3,2,192,256]{3,2,1,0:T(8,128)} %h_ref.3, f32[2,192,256]{2,1,0:T(8,128)} %eps_ref.3, f32[2,192,256]{2,1,0:T(8,128)} %sigma_ref.3), custom_call_target="tpu_custom_call" | custom-call | flops 3449999872 | tf_op jit(solution)/shard_map/pallas_call | solution.py:629
  3.6 4.5 %collective-permute-start.1 = (f32[3,192,256]{2,1,0:T(8,128)}, f32[3,192,256]{2,1,0:T(8,128)S(1)}, u32[]{:S(2)}, u32[]{:S(2)}) collective-permute-start(f32[3,192,256]{2,1,0:T(8,128)} %get-tuple-element.15.after_hbm), channel_id=1, source_target_pairs={{1,2},{2,1},{3,4},{4,3},{5,6},{6,5},{7,8},{8,7},{9,10},{10,9},{11,... | collective-permute-start | bytes 1769480 | tf_op jit(solution)/shard_map/ppermute | solution.py:685
  8.2 0.0 copy-start
  8.2 0.0 copy-start.1
  8.2 0.0 copy-start.2
  8.2 1.1 %shard_map.122.packed_hbm = f32[16,8,128]{2,1,0:T(8,128)} custom-call(s32[1,256]{1,0:T(1,128)S(1)} %bitcast.2, s32[1,256]{1,0:T(1,128)S(1)} %bitcast.3, f32[3,256]{1,0:T(4,128)S(1)} %copy-done.4, f32[3,192,256]{2,1,0:T(8,128)} %get-tuple-element.15.after_hbm), custom_call_target="tpu_custom_call" | custom-call | flops 1150000000 | tf_op jit(solution)/shard_map/pallas_call | solution.py:629
  9.4 5.0 %all-to-all-start = ((f32[16,8,128]{2,1,0:T(8,128)}), f32[16,8,128]{2,1,0:T(8,128)S(1)}, u32[]{:S(2)}, u32[]{:S(2)}) async-start(f32[16,8,128]{2,1,0:T(8,128)} %shard_map.122.packed_hbm), calls=%async_computation | async-start | bytes 131072 | tf_op jit(solution)/shard_map/all_to_all | solution.py:695
  14.4 0.2 collective-permute-start
  14.5 0.0 copy-done.1
  14.6 1.0 %copy-done.3 = f32[2,192,256]{2,1,0:T(8,128)S(1)} copy-done((f32[2,192,256]{2,1,0:T(8,128)S(1)}, f32[2,192,256]{2,1,0:T(8,128)}, u32[]{:S(2)}) %copy-start.3) | copy-done | bytes 393240
  15.5 3.0 %shard_map.123 = (f32[2,192,256]{2,1,0:T(8,128)}, f32[2,192,256]{2,1,0:T(8,128)}) custom-call(f32[3,2,192,256]{3,2,1,0:T(8,128)S(1)} %copy-done.1, f32[3,2,192,256]{3,2,1,0:T(8,128)S(1)} %copy-done, f32[2,192,256]{2,1,0:T(8,128)S(1)} %copy-done.2, f32[2,192,256]{2,1,0:T(8,128)S(1)} %copy-done.3, f32[16,8,128]{2,1,0:T(8,128)} %shard_map.122.packed_hbm), custom_call_target="tpu_custom_call" | custom-call | flops 3449999872 | tf_op jit(solution)/shard_map/pallas_call | solution.py:629
  18.5 0.4 %collective-permute-start.2 = (f32[2,192,256]{2,1,0:T(8,128)}, f32[2,192,256]{2,1,0:T(8,128)}, u32[]{:S(2)}, u32[]{:S(2)}) collective-permute-start(f32[2,192,256]{2,1,0:T(8,128)} %get-tuple-element.26), channel_id=1, source_target_pairs={{0,1},{1,0},{2,3},{3,2},{4,5},{5,4},{6,7},{7,6},{8,9},{9,8},{10,11... | collective-permute-start | bytes 1179656 | tf_op jit(solution)/shard_map/ppermute | solution.py:730
  18.9 3.7 %collective-permute-start.3 = (f32[2,192,256]{2,1,0:T(8,128)}, f32[2,192,256]{2,1,0:T(8,128)}, u32[]{:S(2)}, u32[]{:S(2)}) collective-permute-start(f32[2,192,256]{2,1,0:T(8,128)} %get-tuple-element.16.after_hbm), channel_id=1, source_target_pairs={{1,2},{2,1},{3,4},{4,3},{5,6},{6,5},{7,8},{8,7},{9,10},{10,9},{11,... | collective-permute-start | bytes 1179656 | tf_op jit(solution)/shard_map/ppermute | solution.py:729
  22.6 2.6 %shard_map.124 = (f32[3,2,192,256]{3,2,1,0:T(8,128)}, f32[3,2,192,256]{3,2,1,0:T(8,128)}, f32[2,2,192,256]{3,2,1,0:T(8,128)}) custom-call(f32[3,2,192,256]{3,2,1,0:T(8,128)S(1)} %copy-done.1, f32[3,2,192,256]{3,2,1,0:T(8,128)S(1)} %copy-done, f32[2,192,256]{2,1,0:T(8,128)S(1)} %copy-done.2, f32[2,192,256]{2,1,0:T(8,128)S(1)} %copy-done.3, ...), custom_call_target="tpu_custom_call" | custom-call | flops 3449999872 | tf_op jit(solution)/shard_map/pallas_call | solution.py:629
  25.2 0.0 copy-done.8
  25.2 0.1 copy.13.bounds_ref
  25.3 0.0 all-to-all-done.got_ref
  25.3 0.0 collective-permute-done.chip_hbm
  25.3 0.0 collective-permute-done.1.far_hbm
  25.3 7.5 %shard_map.125 = (f32[3,2,192,256]{3,2,1,0:T(8,128)S(1)}, f32[3,2,192,256]{3,2,1,0:T(8,128)S(1)}, f32[2,192,256]{2,1,0:T(8,128)S(1)}, f32[2,192,256]{2,1,0:T(8,128)S(1)}, f32[3,2,192,256]{3,2,1,0:T(8,128)S(1)}) custom-call(f32[3,2,192,256]{3,2,1,0:T(8,128)S(1)} %copy-done.1, f32[3,2,192,256]{3,2,1,0:T(8,128)} %forward_hbm.1, ...), custom_call_target="tpu_custom_call" | custom-call | flops 6899999744 | tf_op jit(solution)/shard_map/pallas_call | solution.py:629
  32.7 0.0 collective-permute-done.2.chip_hbm
  32.8 0.0 collective-permute-done.3.far_hbm
  32.8 3.6 %shard_map.126 = (f32[3,2,192,256]{3,2,1,0:T(8,128)}, f32[3,2,192,256]{3,2,1,0:T(8,128)}, f32[2,192,256]{2,1,0:T(8,128)}) custom-call(f32[3,2,192,256]{3,2,1,0:T(8,128)S(1)} %get-tuple-element.21.forward_ref, f32[3,2,192,256]{3,2,1,0:T(8,128)S(1)} %get-tuple-element.22.h2_ref, f32[3,2,192,256]{3,2,1,0:T(8,128)S(1)} %get-tuple-element.23.e2_ref, ...), custom_call_target="tpu_custom_call" | custom-call | flops 2875000064 | tf_op jit(solution)/shard_map/pallas_call | solution.py:629
  (11 shorter events, 0.0 us)
Async XLA Ops:
  0.6 7.5 %copy-start.4 = (f32[3,256]{1,0:T(4,128)S(1)}, f32[3,256]{1,0:T(4,128)}, u32[]{:S(2)}) copy-start(f32[3,256]{1,0:T(4,128)} %amplitude_ref.1) | copy-start | bytes 9220
  0.6 7.5 %copy-start.6 = (s32[256,1]{0,1:T(1,128)S(1)}, s32[256,1]{0,1:T(1,128)}, u32[]{:S(2)}) copy-start(s32[256,1]{0,1:T(1,128)} %param.16) | copy-start | bytes 3076
  0.7 7.5 %copy-start.5 = (s32[256,1]{0,1:T(1,128)S(1)}, s32[256,1]{0,1:T(1,128)}, u32[]{:S(2)}) copy-start(s32[256,1]{0,1:T(1,128)} %param.15) | copy-start | bytes 3076
  3.6 21.6 %collective-permute-start.1 = (f32[3,192,256]{2,1,0:T(8,128)}, f32[3,192,256]{2,1,0:T(8,128)S(1)}, u32[]{:S(2)}, u32[]{:S(2)}) collective-permute-start(f32[3,192,256]{2,1,0:T(8,128)} %get-tuple-element.15.after_hbm), channel_id=1, source_target_pairs={{1,2},{2,1},{3,4},{4,3},{5,6},{6,5},{7,8},{8,7},{9,10},{10,9},{11,... | collective-permute-start | bytes 1769480 | tf_op jit(solution)/shard_map/ppermute | solution.py:685
  8.2 6.3 %copy-start = (f32[3,2,192,256]{3,2,1,0:T(8,128)S(1)}, f32[3,2,192,256]{3,2,1,0:T(8,128)}, u32[]{:S(2)}) copy-start(f32[3,2,192,256]{3,2,1,0:T(8,128)} %h_ref.3) | copy-start | bytes 3538948
  8.2 6.3 %copy-start.1 = (f32[3,2,192,256]{3,2,1,0:T(8,128)S(1)}, f32[3,2,192,256]{3,2,1,0:T(8,128)}, u32[]{:S(2)}) copy-start(f32[3,2,192,256]{3,2,1,0:T(8,128)} %e_ref.5) | copy-start | bytes 3538948
  8.2 6.3 %copy-start.2 = (f32[2,192,256]{2,1,0:T(8,128)S(1)}, f32[2,192,256]{2,1,0:T(8,128)}, u32[]{:S(2)}) copy-start(f32[2,192,256]{2,1,0:T(8,128)} %eps_ref.3) | copy-start | bytes 1179652
  9.4 15.9 %all-to-all-start = ((f32[16,8,128]{2,1,0:T(8,128)}), f32[16,8,128]{2,1,0:T(8,128)S(1)}, u32[]{:S(2)}, u32[]{:S(2)}) async-start(f32[16,8,128]{2,1,0:T(8,128)} %shard_map.122.packed_hbm), calls=%async_computation | async-start | bytes 131072 | tf_op jit(solution)/shard_map/all_to_all | solution.py:695
  14.4 10.9 %collective-permute-start = (f32[3,192,256]{2,1,0:T(8,128)}, f32[3,192,256]{2,1,0:T(8,128)}, u32[]{:S(2)}, u32[]{:S(2)}) collective-permute-start(f32[3,192,256]{2,1,0:T(8,128)} %get-tuple-element.20), channel_id=1, source_target_pairs={{0,1},{1,0},{2,3},{3,2},{4,5},{5,4},{6,7},{7,6},{8,9},{9,8},{10,11... | collective-permute-start | bytes 1769480 | tf_op jit(solution)/shard_map/ppermute | solution.py:686
  14.5 1.0 %copy-start.3 = (f32[2,192,256]{2,1,0:T(8,128)S(1)}, f32[2,192,256]{2,1,0:T(8,128)}, u32[]{:S(2)}) copy-start(f32[2,192,256]{2,1,0:T(8,128)} %sigma_ref.3) | copy-start | bytes 1179652
  18.5 14.2 %collective-permute-start.2 = (f32[2,192,256]{2,1,0:T(8,128)}, f32[2,192,256]{2,1,0:T(8,128)}, u32[]{:S(2)}, u32[]{:S(2)}) collective-permute-start(f32[2,192,256]{2,1,0:T(8,128)} %get-tuple-element.26), channel_id=1, source_target_pairs={{0,1},{1,0},{2,3},{3,2},{4,5},{5,4},{6,7},{7,6},{8,9},{9,8},{10,11... | collective-permute-start | bytes 1179656 | tf_op jit(solution)/shard_map/ppermute | solution.py:730
  18.9 6.2 %copy-start.8 = (s32[3,2]{0,1:T(2,128)S(1)}, s32[3,2]{0,1:T(2,128)}, u32[]{:S(2)}) copy-start(s32[3,2]{0,1:T(2,128)} %param.19) | copy-start | bytes 76
  18.9 6.4 %copy-start.7 = (f32[2,2]{1,0:T(2,128)S(1)}, f32[2,2]{1,0:T(2,128)}, u32[]{:S(2)}) copy-start(f32[2,2]{1,0:T(2,128)} %timing_ref.3) | copy-start | bytes 52
  18.9 13.8 %collective-permute-start.3 = (f32[2,192,256]{2,1,0:T(8,128)}, f32[2,192,256]{2,1,0:T(8,128)}, u32[]{:S(2)}, u32[]{:S(2)}) collective-permute-start(f32[2,192,256]{2,1,0:T(8,128)} %get-tuple-element.16.after_hbm), channel_id=1, source_target_pairs={{1,2},{2,1},{3,4},{4,3},{5,6},{6,5},{7,8},{8,7},{9,10},{10,9},{11,... | collective-permute-start | bytes 1179656 | tf_op jit(solution)/shard_map/ppermute | solution.py:729

commit v4 on v3

--- a/solution.py
+++ b/solution.py
@@ -171,11 +171,7 @@
         spread(jnp.where(cell >= top * layer, owner + 1, -1)),
         spread(jnp.where(cell < layer, owner - 1, -1)),
     )
-    line = cell // width_y
-    column = cell - line * width_y
-    rows = jnp.concatenate(
-        [amp, line.astype(F32), column.astype(F32), jnp.zeros((3, entries), F32)], axis=0
-    )
+    rows = jnp.concatenate([amp, cell.astype(F32), jnp.zeros((4, entries), F32)], axis=0)
     slot = lax.broadcasted_iota(jnp.int32, (lanes, entries), 0)
     hits = [(slot == rank + k * cap).astype(F32) for k in range(3)]
     place = jnp.concatenate(hits, axis=1).astype(BF16)
@@ -190,7 +186,7 @@
         out = lax.dot_general(values, place, (((1,), (1,)), ((), ())), preferred_element_type=F32)
         total = out if total is None else total + out
     for d in range(peers):
-        packed_ref[d] = total[d * 8 : (d + 1) * 8]
+        packed_ref[d] = total[d * 8 : d * 8 + 4]
 
 
 def magnetic_step(c, e_ref, h_ref, h1_ref):
@@ -216,98 +212,71 @@
     return ex, ey, ez
 
 
-def coefficients(c, eps_ref, sigma_ref, z):
-    eps, sigma = c.get(eps_ref, z), c.get(sigma_ref, z)
-    cb = 1.0 / (2.0 * eps + sigma)
-    return (2.0 * eps - sigma) * cb, cb
-
-
 def halves_second(
     e_ref,
     h_ref,
-    eps_ref,
-    sigma_ref,
+    eps_hbm,
+    sigma_hbm,
     packed_hbm,
     chip_hbm,
     far_hbm,
-    h1_ref,
-    e1_ref,
-    low_ref,
-    chip_ref,
-    far_ref,
-    out_sems,
-):
-    slab, width_x = e_ref.shape[1], e_ref.shape[2]
-    top = slab - 1
-    odd = odd_device()
-    over_rows(width_x, lambda c: magnetic_step(c, e_ref, h_ref, h1_ref))
-
-    def electric(c):
-        for z, ref, comps in ((0, low_ref, 2), (top, e1_ref, 3)):
-            ca, cb = coefficients(c, eps_ref, sigma_ref, z)
-            for k, v in enumerate(electric_step(c, z, comps, e_ref, h1_ref, ca, cb)):
-                c.put(ref, k, v)
-
-    over_rows(width_x, electric)
-
-    def boundary(c):
-        ex, ey, ez = (c.get(e1_ref, k) for k in range(3))
-        hx = c.get(h1_ref, 0, top) - HALF * (ahead_y(ez) + ey)
-        hy = c.get(h1_ref, 1, top) + HALF * (ex + c.ahead_x(e1_ref, 2))
-        upward = (hx, hy)
-        downward = (c.get(low_ref, 0), c.get(low_ref, 1))
-        for k in range(2):
-            c.put(chip_ref, k, jnp.where(odd, downward[k], upward[k]))
-            c.put(far_ref, k, jnp.where(odd, upward[k], downward[k]))
-
-    part = width_x // PARTS
-    out = []
-    for g in range(PARTS):
-        over_rows(width_x, boundary, g * part, (g + 1) * part)
-        out = out + send_rows(g, part, chip_ref, far_ref, chip_hbm, far_hbm, out_sems)
-    for copy in out:
-        copy.wait()
-
-
-def first_step(
-    e_ref,
-    h_ref,
-    eps_ref,
-    sigma_ref,
-    after_hbm,
     h1_hbm,
     e1_hbm,
     mat_hbm,
     h1_ref,
     e1_ref,
     mat_ref,
-    h1_sem,
-    sems,
+    chip_ref,
+    far_ref,
+    in_sems,
+    step_sems,
+    out_sems,
 ):
     slab, width_x = e_ref.shape[1], e_ref.shape[2]
+    top = slab - 1
+    odd = odd_device()
+    copies = [
+        pltpu.make_async_copy(a, mat_ref.at[i], in_sems.at[i])
+        for i, a in enumerate((eps_hbm, sigma_hbm))
+    ]
+    for copy in copies:
+        copy.start()
     over_rows(width_x, lambda c: magnetic_step(c, e_ref, h_ref, h1_ref))
-    out = [pltpu.make_async_copy(h1_ref, h1_hbm, h1_sem)]
+    out = [pltpu.make_async_copy(h1_ref, h1_hbm, step_sems.at[0])]
     out[0].start()
+    for copy in copies:
+        copy.wait()
 
     def electric(c):
         for z in range(slab):
-            ca, cb = coefficients(c, eps_ref, sigma_ref, z)
+            eps, sigma = c.get(mat_ref, 0, z), c.get(mat_ref, 1, z)
+            cb = 1.0 / (2.0 * eps + sigma)
+            ca = (2.0 * eps - sigma) * cb
             c.put(mat_ref, 0, z, ca)
             c.put(mat_ref, 1, z, cb)
             for k, v in enumerate(electric_step(c, z, 3, e_ref, h1_ref, ca, cb)):
                 c.put(e1_ref, k, z, v)
 
+    over_rows(width_x, electric)
+
+    def boundary(c):
+        ex, ey, ez = (c.get(e1_ref, k, top) for k in range(3))
+        hx = c.get(h1_ref, 0, top) - HALF * (ahead_y(ez) + ey)
+        hy = c.get(h1_ref, 1, top) + HALF * (ex + c.ahead_x(e1_ref, 2, top))
+        upward = (hx, hy)
+        downward = (c.get(e1_ref, 0, 0), c.get(e1_ref, 1, 0))
+        for k in range(2):
+            c.put(chip_ref, k, jnp.where(odd, downward[k], upward[k]))
+            c.put(far_ref, k, jnp.where(odd, upward[k], downward[k]))
+
     part = width_x // PARTS
     for g in range(PARTS):
-        over_rows(width_x, electric, g * part, (g + 1) * part)
-        rows = pl.ds(g * part, part)
-        pairs = (
-            (e1_ref.at[:, :, rows], e1_hbm.at[:, :, rows]),
-            (mat_ref.at[:, :, rows], mat_hbm.at[:, :, rows]),
-        )
-        for i, (a, b) in enumerate(pairs):
-            out.append(pltpu.make_async_copy(a, b, sems.at[g, i]))
-            out[-1].start()
+        over_rows(width_x, boundary, g * part, (g + 1) * part)
+        out = out + send_rows(g, part, chip_ref, far_ref, chip_hbm, far_hbm, out_sems)
+        if g == 0:
+            for i, (a, b) in enumerate(((e1_ref, e1_hbm), (mat_ref, mat_hbm))):
+                out.append(pltpu.make_async_copy(a, b, step_sems.at[1 + i]))
+                out[-1].start()
     for copy in out:
         copy.wait()
 
@@ -316,12 +285,12 @@
     peers, _, lanes = got_ref.shape
     slab, width_x, width_y = own_ref.shape[1:]
     group = LANES // cap
-    part = lax.broadcasted_iota(jnp.int32, (8, LANES), 1) // cap
+    part = lax.broadcasted_iota(jnp.int32, (4, LANES), 1) // cap
 
     def row_of(segment):
         blocks = []
         for g in range(0, peers, group):
-            block = jnp.zeros((8, LANES), F32)
+            block = jnp.zeros((4, LANES), F32)
             for p in range(min(group, peers - g)):
                 shift = ((p - segment) * cap) % LANES
                 there = got_ref[g + p]
@@ -333,8 +302,10 @@
     def fill(segment, first_line, lines, comps, store):
         row = row_of(segment)
         count = row.shape[1]
-        line = row[3:4].astype(jnp.int32) - first_line
-        column = row[4:5].astype(jnp.int32)
+        cell = row[3:4].astype(jnp.int32)
+        line = cell // width_y
+        column = cell - line * width_y
+        line = line - first_line
         where_line = lax.broadcasted_iota(jnp.int32, (lines, count), 0) == line
         left = where_line.astype(F32).astype(BF16)
         where_column = lax.broadcasted_iota(jnp.int32, (width_y, count), 0) == column
@@ -686,44 +657,30 @@
     chip1 = lax.ppermute(chip1, "gz", chip_pairs)
     packed = call(
         functools.partial(pack_entries, cap, slab - 1, wx, wy),
-        shape(peers, 8, lanes),
+        shape(peers, 4, lanes),
         (owners.reshape(1, rows), cells.reshape(1, rows), amplitude, begun),
         1,
         8,
         in_hbm=(3,),
     )
     got = lax.all_to_all(packed, "gz", 0, 0, tiled=True)
-    chip2, far2 = call(
+    chip2, far2, h1, e1, mat = call(
         halves_second,
-        (sent(2, *layer), sent(2, *layer)),
+        (sent(2, *layer), sent(2, *layer), sent(*fields), sent(*fields), sent(2, *slabs)),
         (e_field, h_field, permittivity, conductivity, packed),
-        3,
-        16,
-        scratch=(
-            VMEM(fields, F32),
-            VMEM((3, *layer), F32),
-            VMEM((2, *layer), F32),
-            VMEM((2, *layer), F32),
-            VMEM((2, *layer), F32),
-            dma((PARTS, 2)),
-        ),
-        in_hbm=(4,),
-        out_hbm=True,
-    )
-    h1, e1, mat = call(
-        first_step,
-        (sent(*fields), sent(*fields), sent(2, *slabs)),
-        (e_field, h_field, permittivity, conductivity, far2),
         3,
         16,
         scratch=(
             VMEM(fields, F32),
             VMEM(fields, F32),
             VMEM((2, *slabs), F32),
-            dma,
+            VMEM((2, *layer), F32),
+            VMEM((2, *layer), F32),
+            dma((2,)),
+            dma((3,)),
             dma((PARTS, 2)),
         ),
-        in_hbm=(4,),
+        in_hbm=(2, 3, 4),
         out_hbm=True,
     )
     far2 = lax.ppermute(far2, "gz", far_pairs)

time: 36.7 us -> 34.8 us (0.948)
  Pallas kernels: 20.7 us -> 18 us
  waiting for transfers between devices: 0.01 us -> 1.79 us
  local copies, waits for them, and re-layouts: 1.12 us -> 0.13 us
    pallas_call x6 -> x5, Pallas kernels: 20.7 us -> 18 us  [call(): pl.pallas_call(body, out_shape=outs, in_specs=[place(i, x) for i, x in en...]
    ppermute x1, waiting for transfers between devices: 0.01 us -> 1.78 us  [local(): far2 = lax.ppermute(far2, 'gz', far_pairs)]
    unnamed x19 -> x15, local copies, waits for them, and re-layouts: 1.12 us -> 0.13 us
  transfers between devices with their start and end apart: 5 -> 5, of which waited for: 0 -> 1; matrix products, arithmetic and copies ran while one was open for 0% -> 0% of each run, Pallas kernels for 39% -> 35%
where the time goes in v4:
time: 34.8 us; the launch traced here: 34.4 us
  Pallas kernels  18 us (52%)
  starting transfers between devices  13.7 us (39%)
  waiting for transfers between devices  1.79 us (5%)
  between operations  0.79 us (2%)
    pallas_call x5, Pallas kernels, call(): pl.pallas_call(body, out_shape=outs, in_specs=[place(i, x) for i, x in en...  18 us
    all_to_all x1, starting transfers between devices, local(): got = lax.all_to_all(packed, 'gz', 0, 0, tiled=True)  5.32 us
    ppermute x1, starting transfers between devices, local(): far1 = lax.ppermute(far1, 'gz', far_pairs)  4.49 us
    ppermute x1, starting transfers between devices, local(): far2 = lax.ppermute(far2, 'gz', far_pairs)  3.57 us
    ppermute x1, waiting for transfers between devices, local(): far2 = lax.ppermute(far2, 'gz', far_pairs)  1.78 us
  transfers between devices with their start and end apart: 5, of which 1 were waited for; matrix products, arithmetic and copies ran while one was open for 0% of the time, Pallas kernels for 35%

profile of v4, /device:TPU:1, one launch (start us, length us, event | category | flops | bytes accessed | tf_op | source)
XLA Modules:
  0.0 34.4 jit_solution(12823712169854655352)
XLA Ops:
  0.6 0.0 copy-start.2
  0.6 0.0 copy-start.4
  0.7 3.0 %shard_map.121 = (f32[3,192,256]{2,1,0:T(8,128)}, f32[3,192,256]{2,1,0:T(8,128)}) custom-call(f32[3,2,192,256]{3,2,1,0:T(8,128)} %e_ref.3, f32[3,2,192,256]{3,2,1,0:T(8,128)} %h_ref.1, f32[2,192,256]{2,1,0:T(8,128)} %eps_hbm.3, f32[2,192,256]{2,1,0:T(8,128)} %sigma_hbm.3), custom_call_target="tpu_custom_call" | custom-call | flops 3449999872 | tf_op jit(solution)/shard_map/pallas_call | solution.py:600
  3.6 0.1 collective-permute-start
  3.8 4.5 %collective-permute-start.1 = (f32[3,192,256]{2,1,0:T(8,128)}, f32[3,192,256]{2,1,0:T(8,128)}, u32[]{:S(2)}, u32[]{:S(2)}) collective-permute-start(f32[3,192,256]{2,1,0:T(8,128)} %get-tuple-element.15.after_hbm), channel_id=1, source_target_pairs={{1,2},{2,1},{3,4},{4,3},{5,6},{6,5},{7,8},{8,7},{9,10},{10,9},{11,... | collective-permute-start | bytes 1769480 | tf_op jit(solution)/shard_map/ppermute | solution.py:656
  8.3 0.0 copy-start
  8.3 0.0 copy-start.1
  8.3 1.1 %shard_map.122.packed_hbm = f32[16,4,128]{2,1,0:T(4,128)} custom-call(s32[1,256]{1,0:T(1,128)S(1)} %bitcast.2, s32[1,256]{1,0:T(1,128)S(1)} %bitcast.3, f32[3,256]{1,0:T(4,128)S(1)} %copy-done.2, f32[3,192,256]{2,1,0:T(8,128)} %get-tuple-element.15.after_hbm), custom_call_target="tpu_custom_call" | custom-call | flops 1150000000 | tf_op jit(solution)/shard_map/pallas_call | solution.py:600
  9.4 5.3 %all-to-all-start = ((f32[16,4,128]{2,1,0:T(4,128)}), f32[16,4,128]{2,1,0:T(4,128)S(1)}, u32[]{:S(2)}, u32[]{:S(2)}) async-start(f32[16,4,128]{2,1,0:T(4,128)} %shard_map.122.packed_hbm), calls=%async_computation | async-start | bytes 65536 | tf_op jit(solution)/shard_map/all_to_all | solution.py:666
  14.7 0.0 copy-done
  14.7 0.0 copy-done.1
  14.7 0.0 copy-start.6
  14.8 0.0 copy-start.5
  14.8 3.6 %shard_map.123 = (f32[2,192,256]{2,1,0:T(8,128)}, f32[2,192,256]{2,1,0:T(8,128)}, f32[3,2,192,256]{3,2,1,0:T(8,128)}, f32[3,2,192,256]{3,2,1,0:T(8,128)}, f32[2,2,192,256]{3,2,1,0:T(8,128)}) custom-call(f32[3,2,192,256]{3,2,1,0:T(8,128)S(1)} %copy-done.1, f32[3,2,192,256]{3,2,1,0:T(8,128)S(1)} %copy-done, f32[2,192,256]{2,1,0:T(8,128)} %eps_hbm.3, ...), custom_call_target="tpu_custom_call" | custom-call | flops 3449999872 | tf_op jit(solution)/shard_map/pallas_call | solution.py:600
  18.4 0.2 collective-permute-start.2
  18.6 3.6 %collective-permute-start.3 = (f32[2,192,256]{2,1,0:T(8,128)}, f32[2,192,256]{2,1,0:T(8,128)S(1)}, u32[]{:S(2)}, u32[]{:S(2)}) collective-permute-start(f32[2,192,256]{2,1,0:T(8,128)} %get-tuple-element.26), channel_id=1, source_target_pairs={{1,2},{2,1},{3,4},{4,3},{5,6},{6,5},{7,8},{8,7},{9,10},{10,9},{11,... | collective-permute-start | bytes 1179656 | tf_op jit(solution)/shard_map/ppermute | solution.py:686
  22.2 0.1 copy.13.bounds_ref
  22.3 0.0 all-to-all-done.got_ref
  22.3 0.0 collective-permute-done.chip_hbm
  22.3 0.0 collective-permute-done.1.far_hbm
  22.3 7.3 %shard_map.124 = (f32[3,2,192,256]{3,2,1,0:T(8,128)S(1)}, f32[3,2,192,256]{3,2,1,0:T(8,128)S(1)}, f32[2,192,256]{2,1,0:T(8,128)S(1)}, f32[2,192,256]{2,1,0:T(8,128)S(1)}, f32[3,2,192,256]{3,2,1,0:T(8,128)S(1)}) custom-call(f32[3,2,192,256]{3,2,1,0:T(8,128)S(1)} %copy-done.1, f32[3,2,192,256]{3,2,1,0:T(8,128)} %forward_hbm.1, ...), custom_call_target="tpu_custom_call" | custom-call | flops 6899999744 | tf_op jit(solution)/shard_map/pallas_call | solution.py:600
  29.6 0.0 collective-permute-done.2.chip_hbm
  29.6 1.8 %collective-permute-done.3.far_hbm = f32[2,192,256]{2,1,0:T(8,128)S(1)} collective-permute-done((f32[2,192,256]{2,1,0:T(8,128)}, f32[2,192,256]{2,1,0:T(8,128)S(1)}, u32[]{:S(2)}, u32[]{:S(2)}) %collective-permute-start.3) | collective-permute-done | bytes 393248 | tf_op jit(solution)/shard_map/ppermute | solution.py:686
  31.4 3.0 %shard_map.125 = (f32[3,2,192,256]{3,2,1,0:T(8,128)}, f32[3,2,192,256]{3,2,1,0:T(8,128)}, f32[2,192,256]{2,1,0:T(8,128)}) custom-call(f32[3,2,192,256]{3,2,1,0:T(8,128)S(1)} %get-tuple-element.20.forward_ref, f32[3,2,192,256]{3,2,1,0:T(8,128)S(1)} %get-tuple-element.21.h2_ref, f32[3,2,192,256]{3,2,1,0:T(8,128)S(1)} %get-tuple-element.22.e2_ref, ...), custom_call_target="tpu_custom_call" | custom-call | flops 2875000064 | tf_op jit(solution)/shard_map/pallas_call | solution.py:600
  (6 shorter events, 0.0 us)
Async XLA Ops:
  0.6 7.6 %copy-start.2 = (f32[3,256]{1,0:T(4,128)S(1)}, f32[3,256]{1,0:T(4,128)}, u32[]{:S(2)}) copy-start(f32[3,256]{1,0:T(4,128)} %amplitude_ref.1) | copy-start | bytes 9220
  0.6 7.6 %copy-start.4 = (s32[256,1]{0,1:T(1,128)S(1)}, s32[256,1]{0,1:T(1,128)}, u32[]{:S(2)}) copy-start(s32[256,1]{0,1:T(1,128)} %param.16) | copy-start | bytes 3076
  0.7 7.6 %copy-start.3 = (s32[256,1]{0,1:T(1,128)S(1)}, s32[256,1]{0,1:T(1,128)}, u32[]{:S(2)}) copy-start(s32[256,1]{0,1:T(1,128)} %param.15) | copy-start | bytes 3076
  3.6 18.6 %collective-permute-start = (f32[3,192,256]{2,1,0:T(8,128)}, f32[3,192,256]{2,1,0:T(8,128)S(1)}, u32[]{:S(2)}, u32[]{:S(2)}) collective-permute-start(f32[3,192,256]{2,1,0:T(8,128)} %get-tuple-element.19), channel_id=1, source_target_pairs={{0,1},{1,0},{2,3},{3,2},{4,5},{5,4},{6,7},{7,6},{8,9},{9,8},{10,11... | collective-permute-start | bytes 1769480 | tf_op jit(solution)/shard_map/ppermute | solution.py:657
  3.8 18.5 %collective-permute-start.1 = (f32[3,192,256]{2,1,0:T(8,128)}, f32[3,192,256]{2,1,0:T(8,128)}, u32[]{:S(2)}, u32[]{:S(2)}) collective-permute-start(f32[3,192,256]{2,1,0:T(8,128)} %get-tuple-element.15.after_hbm), channel_id=1, source_target_pairs={{1,2},{2,1},{3,4},{4,3},{5,6},{6,5},{7,8},{8,7},{9,10},{10,9},{11,... | collective-permute-start | bytes 1769480 | tf_op jit(solution)/shard_map/ppermute | solution.py:656
  8.3 6.4 %copy-start = (f32[3,2,192,256]{3,2,1,0:T(8,128)S(1)}, f32[3,2,192,256]{3,2,1,0:T(8,128)}, u32[]{:S(2)}) copy-start(f32[3,2,192,256]{3,2,1,0:T(8,128)} %h_ref.1) | copy-start | bytes 3538948
  8.3 6.4 %copy-start.1 = (f32[3,2,192,256]{3,2,1,0:T(8,128)S(1)}, f32[3,2,192,256]{3,2,1,0:T(8,128)}, u32[]{:S(2)}) copy-start(f32[3,2,192,256]{3,2,1,0:T(8,128)} %e_ref.3) | copy-start | bytes 3538948
  9.4 12.8 %all-to-all-start = ((f32[16,4,128]{2,1,0:T(4,128)}), f32[16,4,128]{2,1,0:T(4,128)S(1)}, u32[]{:S(2)}, u32[]{:S(2)}) async-start(f32[16,4,128]{2,1,0:T(4,128)} %shard_map.122.packed_hbm), calls=%async_computation | async-start | bytes 65536 | tf_op jit(solution)/shard_map/all_to_all | solution.py:666
  14.7 7.4 %copy-start.6 = (s32[3,2]{0,1:T(2,128)S(1)}, s32[3,2]{0,1:T(2,128)}, u32[]{:S(2)}) copy-start(s32[3,2]{0,1:T(2,128)} %param.19) | copy-start | bytes 76
  14.8 7.5 %copy-start.5 = (f32[2,2]{1,0:T(2,128)S(1)}, f32[2,2]{1,0:T(2,128)}, u32[]{:S(2)}) copy-start(f32[2,2]{1,0:T(2,128)} %timing_ref.3) | copy-start | bytes 52
  18.4 11.2 %collective-permute-start.2 = (f32[2,192,256]{2,1,0:T(8,128)}, f32[2,192,256]{2,1,0:T(8,128)S(1)}, u32[]{:S(2)}, u32[]{:S(2)}) collective-permute-start(f32[2,192,256]{2,1,0:T(8,128)} %get-tuple-element.25), channel_id=1, source_target_pairs={{0,1},{1,0},{2,3},{3,2},{4,5},{5,4},{6,7},{7,6},{8,9},{9,8},{10,11... | collective-permute-start | bytes 1179656 | tf_op jit(solution)/shard_map/ppermute | solution.py:687
  18.6 12.8 %collective-permute-start.3 = (f32[2,192,256]{2,1,0:T(8,128)}, f32[2,192,256]{2,1,0:T(8,128)S(1)}, u32[]{:S(2)}, u32[]{:S(2)}) collective-permute-start(f32[2,192,256]{2,1,0:T(8,128)} %get-tuple-element.26), channel_id=1, source_target_pairs={{1,2},{2,1},{3,4},{4,3},{5,6},{6,5},{7,8},{8,7},{9,10},{10,9},{11,... | collective-permute-start | bytes 1179656 | tf_op jit(solution)/shard_map/ppermute | solution.py:686

commit v5 on v4

--- a/solution.py
+++ b/solution.py
@@ -8,7 +8,7 @@
 from jax.sharding import PartitionSpec as P
 
 STEPS = 2
-ROWS = 24
+ROWS = 64
 PARTS = 4
 FLOPS_US = 1.15e9
 LANES = 128
@@ -62,7 +62,7 @@
 
 def over_rows(width_x, body, begin=0, end=None):
     end = width_x if end is None else end
-    size = ROWS if (end - begin) % ROWS == 0 else 8
+    size = next(k for k in (96, 48, 8) if (end - begin) % k == 0)
 
     def step(i, carry):
         body(Chunk(pl.multiple_of(begin + i * size, 8), size, width_x))
@@ -75,74 +75,73 @@
     return lax.rem(lax.axis_index("gz"), 2) == 1
 
 
-def send_rows(g, part, chip_ref, far_ref, chip_hbm, far_hbm, sems):
-    rows = pl.ds(g * part, part)
-    far = pltpu.make_async_copy(far_ref.at[:, rows], far_hbm.at[:, rows], sems.at[g, 0])
-    chip = pltpu.make_async_copy(chip_ref.at[:, rows], chip_hbm.at[:, rows], sems.at[g, 1])
-    far.start()
-    chip.start()
-    return [far, chip]
-
-
-def halves_first(
-    e_hbm,
-    h_hbm,
-    eps_hbm,
-    sigma_hbm,
-    chip_hbm,
-    far_hbm,
-    e_ref,
-    h_ref,
-    low_ref,
-    mat_ref,
-    chip_ref,
-    far_ref,
-    sems,
-    out_sems,
-):
-    slab, width_x = e_hbm.shape[1], e_hbm.shape[2]
-    top = slab - 1
+class Half:
+    def __init__(self, up, ins, out_hbm, e_ref, h_ref, mat_ref, out_ref, sems, out_sems):
+        e_hbm, h_hbm, eps_hbm, sigma_hbm = ins
+        self.up, self.width = up, e_hbm.shape[2]
+        self.part = self.width // PARTS
+        self.refs = e_ref, h_ref, mat_ref, out_ref
+        z = e_hbm.shape[1] - 1 if up else 0
+        self.copies, self.out = [], []
+        for g in range(PARTS):
+            rows = pl.ds(g * self.part, self.part)
+            pairs = [
+                (eps_hbm.at[z, rows], mat_ref.at[0, rows]),
+                (sigma_hbm.at[z, rows], mat_ref.at[1, rows]),
+            ]
+            if up:
+                pairs.append((e_hbm.at[:, z, rows], e_ref.at[:, rows]))
+                pairs.append((h_hbm.at[0:2, z, rows], h_ref.at[:, rows]))
+            else:
+                pairs.append((e_hbm.at[0:2, z, rows], out_ref.at[0:2, rows]))
+            self.copies.append(
+                [pltpu.make_async_copy(a, b, sems.at[g, i]) for i, (a, b) in enumerate(pairs)]
+            )
+            self.out.append(
+                pltpu.make_async_copy(out_ref.at[:, rows], out_hbm.at[:, rows], out_sems.at[g])
+            )
+
+    def start(self):
+        for copies in self.copies:
+            for copy in copies:
+                copy.start()
+
+    def body(self, c):
+        e_ref, h_ref, mat_ref, out_ref = self.refs
+        c.put(out_ref, 2, 1.0 / (2.0 * c.get(mat_ref, 0) + c.get(mat_ref, 1)))
+        if self.up:
+            ez = c.get(e_ref, 2)
+            c.put(out_ref, 0, c.get(h_ref, 0) - HALF * (ahead_y(ez) + c.get(e_ref, 1)))
+            c.put(out_ref, 1, c.get(h_ref, 1) + HALF * (c.get(e_ref, 0) + c.ahead_x(e_ref, 2)))
+
+    def finish(self):
+        for copy in self.copies[0]:
+            copy.wait()
+        for g in range(PARTS):
+            if g + 1 < PARTS:
+                for copy in self.copies[g + 1]:
+                    copy.wait()
+            over_rows(self.width, self.body, g * self.part, (g + 1) * self.part)
+            self.out[g].start()
+        for copy in self.out:
+            copy.wait()
+
+
+def by_parity(when_odd, when_even):
     odd = odd_device()
-    part = width_x // PARTS
-    copies = []
-    for g in range(PARTS):
-        rows = pl.ds(g * part, part)
-        pairs = (
-            (e_hbm.at[:, top, rows], e_ref.at[:, rows]),
-            (h_hbm.at[0:2, top, rows], h_ref.at[:, rows]),
-            (eps_hbm.at[:, rows], mat_ref.at[0, :, rows]),
-            (sigma_hbm.at[:, rows], mat_ref.at[1, :, rows]),
-            (e_hbm.at[0:2, 0, rows], low_ref.at[:, rows]),
-        )
-        copies.append(
-            [pltpu.make_async_copy(a, b, sems.at[g, i]) for i, (a, b) in enumerate(pairs)]
-        )
-        for copy in copies[-1]:
-            copy.start()
-
-    def body(c):
-        ez = c.get(e_ref, 2)
-        hx = c.get(h_ref, 0) - HALF * (ahead_y(ez) + c.get(e_ref, 1))
-        hy = c.get(h_ref, 1) + HALF * (c.get(e_ref, 0) + c.ahead_x(e_ref, 2))
-        cb_top = 1.0 / (2.0 * c.get(mat_ref, 0, top) + c.get(mat_ref, 1, top))
-        cb_low = 1.0 / (2.0 * c.get(mat_ref, 0, 0) + c.get(mat_ref, 1, 0))
-        upward = (hx, hy, cb_top)
-        downward = (c.get(low_ref, 0), c.get(low_ref, 1), cb_low)
-        for k in range(3):
-            c.put(chip_ref, k, jnp.where(odd, downward[k], upward[k]))
-            c.put(far_ref, k, jnp.where(odd, upward[k], downward[k]))
-
-    for copy in copies[0]:
-        copy.wait()
-    out = []
-    for g in range(PARTS):
-        if g + 1 < PARTS:
-            for copy in copies[g + 1]:
-                copy.wait()
-        over_rows(width_x, body, g * part, (g + 1) * part)
-        out = out + send_rows(g, part, chip_ref, far_ref, chip_hbm, far_hbm, out_sems)
-    for copy in out:
-        copy.wait()
+    pl.when(odd)(when_odd)
+    pl.when(jnp.logical_not(odd))(when_even)
+
+
+def halves_first(e_hbm, h_hbm, eps_hbm, sigma_hbm, far_hbm, *scratch):
+    ins = e_hbm, h_hbm, eps_hbm, sigma_hbm
+
+    def run(up):
+        half = Half(up, ins, far_hbm, *scratch)
+        half.start()
+        half.finish()
+
+    by_parity(lambda: run(True), lambda: run(False))
 
 
 def split3(v):
@@ -153,7 +152,9 @@
     return one, two, three
 
 
-def pack_entries(cap, top, width_x, width_y, owners_ref, cells_ref, amplitude_ref, after_hbm, packed_ref):
+def pack_entries(cap, field, owners_ref, cells_ref, amplitude_ref, packed_ref):
+    _, slab, width_x, width_y = field
+    top = slab - 1
     peers, _, lanes = packed_ref.shape
     owner, cell, amp = owners_ref[...], cells_ref[...], amplitude_ref[...]
     entries = owner.shape[1]
@@ -213,12 +214,19 @@
 
 
 def halves_second(
+    cap,
     e_ref,
     h_ref,
     eps_hbm,
     sigma_hbm,
+    owners_ref,
+    cells_ref,
+    amplitude_ref,
+    after_hbm,
     packed_hbm,
-    chip_hbm,
+    chip1_hbm,
+    chip2_hbm,
+    chip3_hbm,
     far_hbm,
     h1_hbm,
     e1_hbm,
@@ -228,6 +236,7 @@
     mat_ref,
     chip_ref,
     far_ref,
+    packed_ref,
     in_sems,
     step_sems,
     out_sems,
@@ -241,9 +250,12 @@
     ]
     for copy in copies:
         copy.start()
+    pack_entries(cap, e_ref.shape, owners_ref, cells_ref, amplitude_ref, packed_ref)
+    out = [pltpu.make_async_copy(packed_ref, packed_hbm, step_sems.at[3])]
+    out[0].start()
     over_rows(width_x, lambda c: magnetic_step(c, e_ref, h_ref, h1_ref))
-    out = [pltpu.make_async_copy(h1_ref, h1_hbm, step_sems.at[0])]
-    out[0].start()
+    out.append(pltpu.make_async_copy(h1_ref, h1_hbm, step_sems.at[0]))
+    out[1].start()
     for copy in copies:
         copy.wait()
 
@@ -263,16 +275,38 @@
         ex, ey, ez = (c.get(e1_ref, k, top) for k in range(3))
         hx = c.get(h1_ref, 0, top) - HALF * (ahead_y(ez) + ey)
         hy = c.get(h1_ref, 1, top) + HALF * (ex + c.ahead_x(e1_ref, 2, top))
-        upward = (hx, hy)
-        downward = (c.get(e1_ref, 0, 0), c.get(e1_ref, 1, 0))
+        upward = (
+            c.get(h1_ref, 0, top),
+            c.get(h1_ref, 1, top),
+            c.get(mat_ref, 1, top),
+            hx,
+            hy,
+        )
+        downward = (
+            c.get(e_ref, 0, 0),
+            c.get(e_ref, 1, 0),
+            c.get(mat_ref, 1, 0),
+            c.get(e1_ref, 0, 0),
+            c.get(e1_ref, 1, 0),
+        )
+        for k in range(5):
+            c.put(chip_ref, k, jnp.where(odd, downward[k], upward[k]))
         for k in range(2):
-            c.put(chip_ref, k, jnp.where(odd, downward[k], upward[k]))
-            c.put(far_ref, k, jnp.where(odd, upward[k], downward[k]))
+            c.put(far_ref, k, jnp.where(odd, upward[k + 3], downward[k + 3]))
 
     part = width_x // PARTS
     for g in range(PARTS):
         over_rows(width_x, boundary, g * part, (g + 1) * part)
-        out = out + send_rows(g, part, chip_ref, far_ref, chip_hbm, far_hbm, out_sems)
+        rows = pl.ds(g * part, part)
+        pairs = (
+            (far_ref, far_hbm),
+            (chip_ref.at[0:2], chip1_hbm),
+            (chip_ref.at[2:3], chip2_hbm),
+            (chip_ref.at[3:5], chip3_hbm),
+        )
+        for i, (a, b) in enumerate(pairs):
+            out.append(pltpu.make_async_copy(a.at[:, rows], b.at[:, rows], out_sems.at[g, i]))
+            out[-1].start()
         if g == 0:
             for i, (a, b) in enumerate(((e1_ref, e1_hbm), (mat_ref, mat_hbm))):
                 out.append(pltpu.make_async_copy(a, b, step_sems.at[1 + i]))
@@ -352,7 +386,8 @@
     h1_hbm,
     e1_hbm,
     mat_hbm,
-    chip_hbm,
+    chip1_hbm,
+    chip2_hbm,
     far_hbm,
     timing_ref,
     bounds_ref,
@@ -361,6 +396,8 @@
     grad_ref,
     cb_ref,
     forward_ref,
+    eout_hbm,
+    hout_hbm,
     h1_ref,
     e1_ref,
     mat_ref,
@@ -373,10 +410,12 @@
     h2a,
     dza,
     sems,
+    out_sems,
 ):
     pairs = (
         (far_hbm, far_ref),
-        (chip_hbm, chip_ref),
+        (chip1_hbm, chip_ref.at[0:2]),
+        (chip2_hbm, chip_ref.at[2:3]),
         (e1_hbm, e1_ref),
         (h1_hbm, h1_ref),
         (mat_hbm, mat_ref),
@@ -478,7 +517,18 @@
             c.put(grad_ref, z, mask * (weight0 * dot1 + weight1 * dot2))
 
     copies[-1].wait()
+    pairs = (
+        (h2_ref.at[0:2, 0:top], hout_hbm.at[0:2, 0:top]),
+        (h2_ref.at[2], hout_hbm.at[2]),
+        (e2_ref.at[2, 0:top], eout_hbm.at[2, 0:top]),
+    )
+    done = [pltpu.make_async_copy(a, b, out_sems.at[i]) for i, (a, b) in enumerate(pairs)]
+    done[0].start()
+    done[1].start()
     over_rows(width_x, third)
+    done[2].start()
+    for copy in done:
+        copy.wait()
 
 
 def last(
@@ -487,47 +537,25 @@
     e2_ref,
     gradp_ref,
     cb_ref,
-    chip_hbm,
-    far_hbm,
+    chip_ref,
+    far_ref,
     timing_ref,
     bounds_ref,
+    ein_hbm,
+    hin_hbm,
     eout_hbm,
     hout_hbm,
     grad_hbm,
-    chip_ref,
-    far_ref,
     e_ref,
     h_ref,
     grad_ref,
-    in_sems,
     sems,
-    rest_sems,
 ):
     slab, width_x = e2_ref.shape[1], e2_ref.shape[2]
     top = slab - 1
     odd = odd_device()
     weight1 = timing_ref[1, 1]
     part = width_x // PARTS
-    arriving = []
-    for g in range(PARTS):
-        rows = pl.ds(g * part, part)
-        pairs = ((far_hbm, far_ref), (chip_hbm, chip_ref))
-        arriving.append(
-            [
-                pltpu.make_async_copy(a.at[:, rows], b.at[:, rows], in_sems.at[g, i])
-                for i, (a, b) in enumerate(pairs)
-            ]
-        )
-        for copy in arriving[-1]:
-            copy.start()
-    rest = [
-        (h2_ref.at[0:2, 0:top], hout_hbm.at[0:2, 0:top]),
-        (h2_ref.at[2], hout_hbm.at[2]),
-        (e2_ref.at[2, 0:top], eout_hbm.at[2, 0:top]),
-    ]
-    rest = [pltpu.make_async_copy(a, b, rest_sems.at[i]) for i, (a, b) in enumerate(rest)]
-    for copy in rest:
-        copy.start()
 
     def body(c):
         chip = [c.get(chip_ref, k) for k in range(2)]
@@ -555,8 +583,6 @@
 
     copies = []
     for g in range(PARTS):
-        for copy in arriving[g]:
-            copy.wait()
         over_rows(width_x, body, g * part, (g + 1) * part)
         rows = pl.ds(g * part, part)
         pairs = (
@@ -569,7 +595,7 @@
             copy = pltpu.make_async_copy(a, b, sems.at[g, i])
             copy.start()
             copies.append(copy)
-    for copy in rest + copies:
+    for copy in copies:
         copy.wait()
 
 
@@ -585,7 +611,7 @@
     return pltpu.HBM(dims, F32)
 
 
-def call(body, outs, ins, us, limit, scratch=(), in_hbm=(), anywhere=(), out_hbm=False):
+def call(body, outs, ins, us, limit, scratch=(), in_hbm=(), anywhere=(), aliases=None):
     def place(i, x):
         if i in in_hbm:
             return pl.BlockSpec(memory_space=pltpu.HBM)
@@ -602,8 +628,9 @@
         out_shape=outs,
         in_specs=[place(i, x) for i, x in enumerate(ins)],
         out_specs=jax.tree.map(
-            lambda _: pl.BlockSpec(memory_space=pltpu.HBM if out_hbm else VMEM), outs
-        ),
+            lambda x: pl.BlockSpec(memory_space=getattr(x, "memory_space", VMEM)), outs
+        ),
+        input_output_aliases=aliases or {},
         scratch_shapes=list(scratch),
         compiler_params=pltpu.CompilerParams(vmem_limit_bytes=limit << 20),
         cost_estimate=pl.CostEstimate(flops=int(us * FLOPS_US), bytes_accessed=0, transcendentals=0),
@@ -633,62 +660,75 @@
 
     layer, slabs, fields = (wx, wy), (slab, wx, wy), (3, slab, wx, wy)
     dma = pltpu.SemaphoreType.DMA
-    chip1, far1 = call(
+    begun = call(
         halves_first,
-        (sent(3, *layer), sent(3, *layer)),
+        sent(3, *layer),
         (e_field, h_field, permittivity, conductivity),
-        3,
+        2,
         56,
         scratch=(
             VMEM((3, *layer), F32),
             VMEM((2, *layer), F32),
             VMEM((2, *layer), F32),
-            VMEM((2, *slabs), F32),
             VMEM((3, *layer), F32),
-            VMEM((3, *layer), F32),
-            dma((PARTS, 5)),
-            dma((PARTS, 2)),
+            dma((PARTS, 4)),
+            dma((PARTS,)),
         ),
         in_hbm=(0, 1, 2, 3),
-        out_hbm=True,
-    )
-    begun = far1
-    far1 = lax.ppermute(far1, "gz", far_pairs)
-    chip1 = lax.ppermute(chip1, "gz", chip_pairs)
-    packed = call(
-        functools.partial(pack_entries, cap, slab - 1, wx, wy),
-        shape(peers, 4, lanes),
-        (owners.reshape(1, rows), cells.reshape(1, rows), amplitude, begun),
-        1,
-        8,
-        in_hbm=(3,),
-    )
-    got = lax.all_to_all(packed, "gz", 0, 0, tiled=True)
-    chip2, far2, h1, e1, mat = call(
-        halves_second,
-        (sent(2, *layer), sent(2, *layer), sent(*fields), sent(*fields), sent(2, *slabs)),
-        (e_field, h_field, permittivity, conductivity, packed),
+    )
+    far1 = lax.ppermute(begun, "gz", far_pairs)
+    packed, chip1, chip2, chip3, far2, h1, e1, mat = call(
+        functools.partial(halves_second, cap),
+        (
+            sent(peers, 4, lanes),
+            sent(2, *layer),
+            sent(1, *layer),
+            sent(2, *layer),
+            sent(2, *layer),
+            sent(*fields),
+            sent(*fields),
+            sent(2, *slabs),
+        ),
+        (
+            e_field,
+            h_field,
+            permittivity,
+            conductivity,
+            owners.reshape(1, rows),
+            cells.reshape(1, rows),
+            amplitude,
+            begun,
+        ),
         3,
         16,
         scratch=(
             VMEM(fields, F32),
             VMEM(fields, F32),
             VMEM((2, *slabs), F32),
+            VMEM((5, *layer), F32),
             VMEM((2, *layer), F32),
-            VMEM((2, *layer), F32),
+            VMEM((peers, 4, lanes), F32),
             dma((2,)),
-            dma((3,)),
-            dma((PARTS, 2)),
-        ),
-        in_hbm=(2, 3, 4),
-        out_hbm=True,
-    )
+            dma((4,)),
+            dma((PARTS, 4)),
+        ),
+        in_hbm=(2, 3, 7),
+    )
+    got = lax.all_to_all(packed, "gz", 0, 0, tiled=True)
     far2 = lax.ppermute(far2, "gz", far_pairs)
-    chip2 = lax.ppermute(chip2, "gz", chip_pairs)
-    h2, e2, grad, cb, forward = call(
+    chip1, chip2, chip3 = (lax.ppermute(x, "gz", chip_pairs) for x in (chip1, chip2, chip3))
+    h2, e2, grad, cb, forward, e_part, h_part = call(
         functools.partial(middle, cap),
-        (kept(*fields), kept(*fields), kept(*slabs), kept(*slabs), kept(*fields)),
-        (e_field, forward_field, got, h1, e1, mat, chip1, far1, timing, bounds),
+        (
+            kept(*fields),
+            kept(*fields),
+            kept(*slabs),
+            kept(*slabs),
+            kept(*fields),
+            sent(*fields),
+            sent(*fields),
+        ),
+        (e_field, forward_field, got, h1, e1, mat, chip1, chip2, far1, timing, bounds),
         6,
         24,
         scratch=(
@@ -703,29 +743,26 @@
             VMEM((2, *layer), F32),
             VMEM((2, *layer), F32),
             VMEM(layer, F32),
-            dma((6,)),
+            dma((7,)),
+            dma((3,)),
         ),
         in_hbm=(1, 3, 4, 5),
-        anywhere=(6, 7),
+        anywhere=(6, 7, 8),
     )
     return call(
         last,
-        (shape(*fields), shape(*fields), shape(*slabs)),
-        (forward, h2, e2, grad, cb, chip2, far2, timing, bounds),
+        (sent(*fields), sent(*fields), sent(*slabs)),
+        (forward, h2, e2, grad, cb, chip3, far2, timing, bounds, e_part, h_part),
         2.5,
         16,
         scratch=(
-            VMEM((2, *layer), F32),
-            VMEM((2, *layer), F32),
             VMEM(fields, F32),
             VMEM((2, *layer), F32),
             VMEM(slabs, F32),
-            dma((PARTS, 2)),
             dma((PARTS, 4)),
-            dma((3,)),
-        ),
-        anywhere=(5, 6),
-        out_hbm=True,
+        ),
+        in_hbm=(9, 10),
+        aliases={9: 0, 10: 1},
     )
 
 

time: 34.8 us -> 33 us (0.948)
  the two profiles are of different devices: /device:TPU:1 before, /device:TPU:0 now
where the time goes in v5:
time: 33 us; the launch traced here: 32.8 us
  Pallas kernels  15.1 us (46%)
  starting transfers between devices  11.3 us (34%)
  waiting for transfers between devices  5.45 us (17%)
  between operations  0.81 us (2%)
    pallas_call x4, Pallas kernels, call(): pl.pallas_call(body, out_shape=outs, in_specs=[place(i, x) for i, x in en...  15.1 us
    all_to_all x1, waiting for transfers between devices, local(): got = lax.all_to_all(packed, 'gz', 0, 0, tiled=True)  5.44 us
    all_to_all x1, starting transfers between devices, local(): got = lax.all_to_all(packed, 'gz', 0, 0, tiled=True)  5.03 us
    ppermute x3, starting transfers between devices, local(): lax.ppermute(x, 'gz', chip_pairs)  4.84 us
    ppermute x1, starting transfers between devices, local(): far1 = lax.ppermute(begun, 'gz', far_pairs)  0.7 us
    ppermute x1, starting transfers between devices, local(): far2 = lax.ppermute(far2, 'gz', far_pairs)  0.67 us
  transfers between devices with their start and end apart: 6, of which 1 were waited for; matrix products, arithmetic and copies ran while one was open for 0% of the time, Pallas kernels for 32%

profile of v5, /device:TPU:0, one launch (start us, length us, event | category | flops | bytes accessed | tf_op | source)
XLA Modules:
  0.0 32.8 jit_solution(7261091839496111855)
XLA Ops:
  0.6 0.0 copy-start.1
  0.6 0.0 copy-start
  0.7 0.0 copy-start.2
  0.7 0.0 copy-start.4
  0.7 0.0 copy-start.3
  0.7 2.3 %shard_map.121.after_hbm = f32[3,192,256]{2,1,0:T(8,128)} custom-call(f32[3,2,192,256]{3,2,1,0:T(8,128)} %e_ref.3, f32[3,2,192,256]{3,2,1,0:T(8,128)} %h_ref.1, f32[2,192,256]{2,1,0:T(8,128)} %eps_hbm.3, f32[2,192,256]{2,1,0:T(8,128)} %sigma_hbm.3), custom_call_target="tpu_custom_call" | custom-call | flops 2300000000 | tf_op jit(solution)/shard_map/pallas_call | solution.py:626
  3.0 0.7 %collective-permute-start.2 = (f32[3,192,256]{2,1,0:T(8,128)}, f32[3,192,256]{2,1,0:T(8,128)S(1)}, u32[]{:S(2)}, u32[]{:S(2)}) collective-permute-start(f32[3,192,256]{2,1,0:T(8,128)} %shard_map.121.after_hbm), channel_id=1, source_target_pairs={{1,2},{2,1},{3,4},{4,3},{5,6},{6,5},{7,8},{8,7},{9,10},{10,9},{11,... | collective-permute-start | bytes 1769480 | tf_op jit(solution)/shard_map/ppermute | solution.py:679
  3.7 0.0 copy-start.6
  3.7 0.0 copy-start.5
  3.7 3.4 %shard_map.122 = (f32[16,4,128]{2,1,0:T(4,128)}, f32[2,192,256]{2,1,0:T(8,128)}, f32[1,192,256]{2,1,0:T(8,128)}, f32[2,192,256]{2,1,0:T(8,128)}, f32[2,192,256]{...) custom-call(f32[3,2,192,256]{3,2,1,0:T(8,128)S(1)} %copy-done.1, ...), custom_call_target="tpu_custom_call" | custom-call | flops 3449999872 | tf_op jit(solution)/shard_map/pallas_call | solution.py:626
  7.2 4.4 %collective-permute-start = (f32[2,192,256]{2,1,0:T(8,128)}, f32[2,192,256]{2,1,0:T(8,128)S(1)}, u32[]{:S(2)}, u32[]{:S(2)}) collective-permute-start(f32[2,192,256]{2,1,0:T(8,128)} %get-tuple-element.22), channel_id=1, source_target_pairs={{0,1},{1,0},{2,3},{3,2},{4,5},{5,4},{6,7},{7,6},{8,9},{9,8},{10,11... | collective-permute-start | bytes 1179656 | tf_op jit(solution)/shard_map/ppermute | solution.py:719
  11.5 0.1 collective-permute-start.1
  11.6 5.0 %all-to-all-start = ((f32[16,4,128]{2,1,0:T(4,128)}), f32[16,4,128]{2,1,0:T(4,128)S(1)}, u32[]{:S(2)}, u32[]{:S(2)}) async-start(f32[16,4,128]{2,1,0:T(4,128)} %get-tuple-element.18), calls=%async_computation | async-start | bytes 65536 | tf_op jit(solution)/shard_map/all_to_all | solution.py:717
  16.6 0.4 %collective-permute-start.3 = (f32[2,192,256]{2,1,0:T(8,128)}, f32[2,192,256]{2,1,0:T(8,128)S(1)}, u32[]{:S(2)}, u32[]{:S(2)}) collective-permute-start(f32[2,192,256]{2,1,0:T(8,128)} %get-tuple-element.29), channel_id=1, source_target_pairs={{0,1},{1,0},{2,3},{3,2},{4,5},{5,4},{6,7},{7,6},{8,9},{9,8},{10,11... | collective-permute-start | bytes 1179656 | tf_op jit(solution)/shard_map/ppermute | solution.py:719
  17.1 0.7 %collective-permute-start.4 = (f32[2,192,256]{2,1,0:T(8,128)}, f32[2,192,256]{2,1,0:T(8,128)S(1)}, u32[]{:S(2)}, u32[]{:S(2)}) collective-permute-start(f32[2,192,256]{2,1,0:T(8,128)} %get-tuple-element.30), channel_id=1, source_target_pairs={{1,2},{2,1},{3,4},{4,3},{5,6},{6,5},{7,8},{8,7},{9,10},{10,9},{11,... | collective-permute-start | bytes 1179656 | tf_op jit(solution)/shard_map/ppermute | solution.py:718
  17.8 0.1 copy.15.bounds_ref
  17.8 5.4 %all-to-all-done.got_ref = f32[16,4,128]{2,1,0:T(4,128)S(1)} async-done(((f32[16,4,128]{2,1,0:T(4,128)}), f32[16,4,128]{2,1,0:T(4,128)S(1)}, u32[]{:S(2)}, u32[]{:S(2)}) %all-to-all-start) | async-done | bytes 32800 | tf_op jit(solution)/shard_map/all_to_all | solution.py:717
  23.3 0.0 collective-permute-done.1.chip2_hbm
  23.3 0.0 collective-permute-done.chip1_hbm
  23.3 0.0 collective-permute-done.2.far_hbm
  23.3 7.2 %shard_map.123 = (f32[3,2,192,256]{3,2,1,0:T(8,128)S(1)}, f32[3,2,192,256]{3,2,1,0:T(8,128)S(1)}, f32[2,192,256]{2,1,0:T(8,128)S(1)}, f32[2,192,256]{2,1,0:T(8,1...) custom-call(f32[3,2,192,256]{3,2,1,0:T(8,128)S(1)} %copy-done.1, ...), custom_call_target="tpu_custom_call" | custom-call | flops 6899999744 | tf_op jit(solution)/shard_map/pallas_call | solution.py:626
  30.6 0.0 collective-permute-done.3.chip_ref
  30.6 0.0 collective-permute-done.4.far_ref
  30.6 2.2 %shard_map.124 = (f32[3,2,192,256]{3,2,1,0:T(8,128)}, f32[3,2,192,256]{3,2,1,0:T(8,128)}, f32[2,192,256]{2,1,0:T(8,128)}) custom-call(f32[3,2,192,256]{3,2,1,0:T(8,128)S(1)} %get-tuple-element.24.forward_ref, f32[3,2,192,256]{3,2,1,0:T(8,128)S(1)} %get-tuple-element.25.h2_ref, ...), custom_call_target="tpu_custom_call", output_to_operand_aliasing={{0}: (9, {}), {1}: (10, {})} | custom-call | flops 2875000064 | tf_op jit(solution)/shard_map/pallas_call | solution.py:626
  (7 shorter events, 0.0 us)
Async XLA Ops:
  0.6 3.0 %copy-start.1 = (f32[3,2,192,256]{3,2,1,0:T(8,128)S(1)}, f32[3,2,192,256]{3,2,1,0:T(8,128)}, u32[]{:S(2)}) copy-start(f32[3,2,192,256]{3,2,1,0:T(8,128)} %e_ref.3) | copy-start | bytes 3538948
  0.6 3.0 %copy-start = (f32[3,2,192,256]{3,2,1,0:T(8,128)S(1)}, f32[3,2,192,256]{3,2,1,0:T(8,128)}, u32[]{:S(2)}) copy-start(f32[3,2,192,256]{3,2,1,0:T(8,128)} %h_ref.1) | copy-start | bytes 3538948
  0.7 3.0 %copy-start.2 = (f32[3,256]{1,0:T(4,128)S(1)}, f32[3,256]{1,0:T(4,128)}, u32[]{:S(2)}) copy-start(f32[3,256]{1,0:T(4,128)} %amplitude_ref.1) | copy-start | bytes 9220
  0.7 3.0 %copy-start.4 = (s32[256,1]{0,1:T(1,128)S(1)}, s32[256,1]{0,1:T(1,128)}, u32[]{:S(2)}) copy-start(s32[256,1]{0,1:T(1,128)} %param.16) | copy-start | bytes 3076
  0.7 3.0 %copy-start.3 = (s32[256,1]{0,1:T(1,128)S(1)}, s32[256,1]{0,1:T(1,128)}, u32[]{:S(2)}) copy-start(s32[256,1]{0,1:T(1,128)} %param.15) | copy-start | bytes 3076
  3.0 20.3 %collective-permute-start.2 = (f32[3,192,256]{2,1,0:T(8,128)}, f32[3,192,256]{2,1,0:T(8,128)S(1)}, u32[]{:S(2)}, u32[]{:S(2)}) collective-permute-start(f32[3,192,256]{2,1,0:T(8,128)} %shard_map.121.after_hbm), channel_id=1, source_target_pairs={{1,2},{2,1},{3,4},{4,3},{5,6},{6,5},{7,8},{8,7},{9,10},{10,9},{11,... | collective-permute-start | bytes 1769480 | tf_op jit(solution)/shard_map/ppermute | solution.py:679
  3.7 14.0 %copy-start.6 = (s32[3,2]{0,1:T(2,128)S(1)}, s32[3,2]{0,1:T(2,128)}, u32[]{:S(2)}) copy-start(s32[3,2]{0,1:T(2,128)} %param.19) | copy-start | bytes 76
  3.7 19.6 %copy-start.5 = (f32[2,2]{1,0:T(2,128)S(1)}, f32[2,2]{1,0:T(2,128)}, u32[]{:S(2)}) copy-start(f32[2,2]{1,0:T(2,128)} %timing_ref.3) | copy-start | bytes 52
  7.2 16.1 %collective-permute-start = (f32[2,192,256]{2,1,0:T(8,128)}, f32[2,192,256]{2,1,0:T(8,128)S(1)}, u32[]{:S(2)}, u32[]{:S(2)}) collective-permute-start(f32[2,192,256]{2,1,0:T(8,128)} %get-tuple-element.22), channel_id=1, source_target_pairs={{0,1},{1,0},{2,3},{3,2},{4,5},{5,4},{6,7},{7,6},{8,9},{9,8},{10,11... | collective-permute-start | bytes 1179656 | tf_op jit(solution)/shard_map/ppermute | solution.py:719
  11.5 11.8 %collective-permute-start.1 = (f32[1,192,256]{2,1,0:T(8,128)}, f32[1,192,256]{2,1,0:T(8,128)S(1)}, u32[]{:S(2)}, u32[]{:S(2)}) collective-permute-start(f32[1,192,256]{2,1,0:T(8,128)} %get-tuple-element.23), channel_id=1, source_target_pairs={{0,1},{1,0},{2,3},{3,2},{4,5},{5,4},{6,7},{7,6},{8,9},{9,8},{10,11... | collective-permute-start | bytes 589832 | tf_op jit(solution)/shard_map/ppermute | solution.py:719
  11.6 11.7 %all-to-all-start = ((f32[16,4,128]{2,1,0:T(4,128)}), f32[16,4,128]{2,1,0:T(4,128)S(1)}, u32[]{:S(2)}, u32[]{:S(2)}) async-start(f32[16,4,128]{2,1,0:T(4,128)} %get-tuple-element.18), calls=%async_computation | async-start | bytes 65536 | tf_op jit(solution)/shard_map/all_to_all | solution.py:717
  16.6 13.9 %collective-permute-start.3 = (f32[2,192,256]{2,1,0:T(8,128)}, f32[2,192,256]{2,1,0:T(8,128)S(1)}, u32[]{:S(2)}, u32[]{:S(2)}) collective-permute-start(f32[2,192,256]{2,1,0:T(8,128)} %get-tuple-element.29), channel_id=1, source_target_pairs={{0,1},{1,0},{2,3},{3,2},{4,5},{5,4},{6,7},{7,6},{8,9},{9,8},{10,11... | collective-permute-start | bytes 1179656 | tf_op jit(solution)/shard_map/ppermute | solution.py:719
  17.1 13.5 %collective-permute-start.4 = (f32[2,192,256]{2,1,0:T(8,128)}, f32[2,192,256]{2,1,0:T(8,128)S(1)}, u32[]{:S(2)}, u32[]{:S(2)}) collective-permute-start(f32[2,192,256]{2,1,0:T(8,128)} %get-tuple-element.30), channel_id=1, source_target_pairs={{1,2},{2,1},{3,4},{4,3},{5,6},{6,5},{7,8},{8,7},{9,10},{10,9},{11,... | collective-permute-start | bytes 1179656 | tf_op jit(solution)/shard_map/ppermute | solution.py:718

commit v6 on v5

--- a/solution.py
+++ b/solution.py
@@ -213,6 +213,17 @@
     return ex, ey, ez
 
 
+def electric_all(c, e_ref, h1_ref, e1_ref, mat_ref):
+    for z in range(e_ref.shape[1]):
+        eps, sigma = c.get(mat_ref, 0, z), c.get(mat_ref, 1, z)
+        cb = 1.0 / (2.0 * eps + sigma)
+        ca = (2.0 * eps - sigma) * cb
+        c.put(mat_ref, 0, z, ca)
+        c.put(mat_ref, 1, z, cb)
+        for k, v in enumerate(electric_step(c, z, 3, e_ref, h1_ref, ca, cb)):
+            c.put(e1_ref, k, z, v)
+
+
 def halves_second(
     cap,
     e_ref,
@@ -224,13 +235,11 @@
     amplitude_ref,
     after_hbm,
     packed_hbm,
+    chip0_hbm,
     chip1_hbm,
     chip2_hbm,
     chip3_hbm,
     far_hbm,
-    h1_hbm,
-    e1_hbm,
-    mat_hbm,
     h1_ref,
     e1_ref,
     mat_ref,
@@ -251,25 +260,13 @@
     for copy in copies:
         copy.start()
     pack_entries(cap, e_ref.shape, owners_ref, cells_ref, amplitude_ref, packed_ref)
-    out = [pltpu.make_async_copy(packed_ref, packed_hbm, step_sems.at[3])]
+    out = [pltpu.make_async_copy(packed_ref, packed_hbm, step_sems.at[0])]
     out[0].start()
     over_rows(width_x, lambda c: magnetic_step(c, e_ref, h_ref, h1_ref))
-    out.append(pltpu.make_async_copy(h1_ref, h1_hbm, step_sems.at[0]))
-    out[1].start()
     for copy in copies:
         copy.wait()
 
-    def electric(c):
-        for z in range(slab):
-            eps, sigma = c.get(mat_ref, 0, z), c.get(mat_ref, 1, z)
-            cb = 1.0 / (2.0 * eps + sigma)
-            ca = (2.0 * eps - sigma) * cb
-            c.put(mat_ref, 0, z, ca)
-            c.put(mat_ref, 1, z, cb)
-            for k, v in enumerate(electric_step(c, z, 3, e_ref, h1_ref, ca, cb)):
-                c.put(e1_ref, k, z, v)
-
-    over_rows(width_x, electric)
+    over_rows(width_x, lambda c: electric_all(c, e_ref, h1_ref, e1_ref, mat_ref))
 
     def boundary(c):
         ex, ey, ez = (c.get(e1_ref, k, top) for k in range(3))
@@ -300,17 +297,14 @@
         rows = pl.ds(g * part, part)
         pairs = (
             (far_ref, far_hbm),
-            (chip_ref.at[0:2], chip1_hbm),
+            (chip_ref.at[0:1], chip0_hbm),
+            (chip_ref.at[1:2], chip1_hbm),
             (chip_ref.at[2:3], chip2_hbm),
             (chip_ref.at[3:5], chip3_hbm),
         )
         for i, (a, b) in enumerate(pairs):
             out.append(pltpu.make_async_copy(a.at[:, rows], b.at[:, rows], out_sems.at[g, i]))
             out[-1].start()
-        if g == 0:
-            for i, (a, b) in enumerate(((e1_ref, e1_hbm), (mat_ref, mat_hbm))):
-                out.append(pltpu.make_async_copy(a, b, step_sems.at[1 + i]))
-                out[-1].start()
     for copy in out:
         copy.wait()
 
@@ -380,12 +374,13 @@
 
 def middle(
     cap,
-    e_ref,
+    e_hbm,
     forward_hbm,
     got_ref,
-    h1_hbm,
-    e1_hbm,
-    mat_hbm,
+    h_hbm,
+    eps_hbm,
+    sigma_hbm,
+    chip0_hbm,
     chip1_hbm,
     chip2_hbm,
     far_hbm,
@@ -396,8 +391,9 @@
     grad_ref,
     cb_ref,
     forward_ref,
-    eout_hbm,
     hout_hbm,
+    e_ref,
+    h_ref,
     h1_ref,
     e1_ref,
     mat_ref,
@@ -413,20 +409,26 @@
     out_sems,
 ):
     pairs = (
+        (e_hbm, e_ref),
+        (h_hbm, h_ref),
         (far_hbm, far_ref),
-        (chip1_hbm, chip_ref.at[0:2]),
+        (chip0_hbm, chip_ref.at[0:1]),
+        (chip1_hbm, chip_ref.at[1:2]),
         (chip2_hbm, chip_ref.at[2:3]),
-        (e1_hbm, e1_ref),
-        (h1_hbm, h1_ref),
-        (mat_hbm, mat_ref),
+        (eps_hbm, mat_ref.at[0]),
+        (sigma_hbm, mat_ref.at[1]),
         (forward_hbm, forward_ref),
     )
     copies = [pltpu.make_async_copy(a, b, sems.at[i]) for i, (a, b) in enumerate(pairs)]
     for copy in copies:
         copy.start()
     place_entries(cap, got_ref, own_ref, sbelow_ref, sabove_ref)
-    for copy in copies[:-1]:
+    for copy in copies[:2]:
         copy.wait()
+    over_rows(e_ref.shape[2], lambda c: magnetic_step(c, e_ref, h_ref, h1_ref))
+    for copy in copies[2:-1]:
+        copy.wait()
+    over_rows(e_ref.shape[2], lambda c: electric_all(c, e_ref, h1_ref, e1_ref, mat_ref))
     slab, width_x = e_ref.shape[1], e_ref.shape[2]
     top = slab - 1
     odd = odd_device()
@@ -520,13 +522,11 @@
     pairs = (
         (h2_ref.at[0:2, 0:top], hout_hbm.at[0:2, 0:top]),
         (h2_ref.at[2], hout_hbm.at[2]),
-        (e2_ref.at[2, 0:top], eout_hbm.at[2, 0:top]),
     )
     done = [pltpu.make_async_copy(a, b, out_sems.at[i]) for i, (a, b) in enumerate(pairs)]
-    done[0].start()
-    done[1].start()
+    for copy in done:
+        copy.start()
     over_rows(width_x, third)
-    done[2].start()
     for copy in done:
         copy.wait()
 
@@ -541,7 +541,6 @@
     far_ref,
     timing_ref,
     bounds_ref,
-    ein_hbm,
     hin_hbm,
     eout_hbm,
     hout_hbm,
@@ -572,10 +571,12 @@
         more[top][2] = -cb_top * (bx + behind_y(high[1]))
         for z in range(slab):
             dot = 0.0
-            for k in range(3 if z == top else 2):
-                delta = more[z][k]
-                dot = dot + delta * c.get(forward_ref, k, z)
-                c.put(e_ref, k, z, c.get(e2_ref, k, z) + delta)
+            for k in range(3):
+                e2 = c.get(e2_ref, k, z)
+                if k < 2 or z == top:
+                    e2 = e2 + more[z][k]
+                    dot = dot + more[z][k] * c.get(forward_ref, k, z)
+                c.put(e_ref, k, z, e2)
             mask = inside(c, bounds_ref, z, slab, cb_low.shape)
             c.put(grad_ref, z, c.get(gradp_ref, z) + (weight1 * mask) * dot)
         c.put(h_ref, 0, c.get(h2_ref, 0, top) + HALF * high[1])
@@ -586,8 +587,7 @@
         over_rows(width_x, body, g * part, (g + 1) * part)
         rows = pl.ds(g * part, part)
         pairs = (
-            (e_ref.at[0:2, :, rows], eout_hbm.at[0:2, :, rows]),
-            (e_ref.at[2, top, rows], eout_hbm.at[2, top, rows]),
+            (e_ref.at[:, :, rows], eout_hbm.at[:, :, rows]),
             (h_ref.at[:, rows], hout_hbm.at[0:2, top, rows]),
             (grad_ref.at[:, rows], grad_hbm.at[:, rows]),
         )
@@ -677,17 +677,15 @@
         in_hbm=(0, 1, 2, 3),
     )
     far1 = lax.ppermute(begun, "gz", far_pairs)
-    packed, chip1, chip2, chip3, far2, h1, e1, mat = call(
+    packed, chip0, chip1, chip2, chip3, far2 = call(
         functools.partial(halves_second, cap),
         (
             sent(peers, 4, lanes),
-            sent(2, *layer),
+            sent(1, *layer),
+            sent(1, *layer),
             sent(1, *layer),
             sent(2, *layer),
             sent(2, *layer),
-            sent(*fields),
-            sent(*fields),
-            sent(2, *slabs),
         ),
         (
             e_field,
@@ -709,15 +707,17 @@
             VMEM((2, *layer), F32),
             VMEM((peers, 4, lanes), F32),
             dma((2,)),
-            dma((4,)),
-            dma((PARTS, 4)),
+            dma((1,)),
+            dma((PARTS, 5)),
         ),
         in_hbm=(2, 3, 7),
     )
     got = lax.all_to_all(packed, "gz", 0, 0, tiled=True)
     far2 = lax.ppermute(far2, "gz", far_pairs)
-    chip1, chip2, chip3 = (lax.ppermute(x, "gz", chip_pairs) for x in (chip1, chip2, chip3))
-    h2, e2, grad, cb, forward, e_part, h_part = call(
+    chip0, chip1, chip2, chip3 = (
+        lax.ppermute(x, "gz", chip_pairs) for x in (chip0, chip1, chip2, chip3)
+    )
+    h2, e2, grad, cb, forward, h_part = call(
         functools.partial(middle, cap),
         (
             kept(*fields),
@@ -726,12 +726,13 @@
             kept(*slabs),
             kept(*fields),
             sent(*fields),
-            sent(*fields),
-        ),
-        (e_field, forward_field, got, h1, e1, mat, chip1, chip2, far1, timing, bounds),
+        ),
+        (e_field, forward_field, got, h_field, permittivity, conductivity, chip0, chip1, chip2, far1, timing, bounds),
         6,
         24,
         scratch=(
+            VMEM(fields, F32),
+            VMEM(fields, F32),
             VMEM(fields, F32),
             VMEM(fields, F32),
             VMEM((2, *slabs), F32),
@@ -743,26 +744,26 @@
             VMEM((2, *layer), F32),
             VMEM((2, *layer), F32),
             VMEM(layer, F32),
-            dma((7,)),
-            dma((3,)),
-        ),
-        in_hbm=(1, 3, 4, 5),
-        anywhere=(6, 7, 8),
+            dma((9,)),
+            dma((2,)),
+        ),
+        in_hbm=(0, 1, 3, 4, 5),
+        anywhere=(6, 7, 8, 9),
     )
     return call(
         last,
         (sent(*fields), sent(*fields), sent(*slabs)),
-        (forward, h2, e2, grad, cb, chip3, far2, timing, bounds, e_part, h_part),
+        (forward, h2, e2, grad, cb, chip3, far2, timing, bounds, h_part),
         2.5,
         16,
         scratch=(
             VMEM(fields, F32),
             VMEM((2, *layer), F32),
             VMEM(slabs, F32),
-            dma((PARTS, 4)),
-        ),
-        in_hbm=(9, 10),
-        aliases={9: 0, 10: 1},
+            dma((PARTS, 3)),
+        ),
+        in_hbm=(9,),
+        aliases={9: 1},
     )
 
 

time: 33 us -> 32.6 us (0.988)
  the two profiles are of different devices: /device:TPU:0 before, /device:TPU:1 now
where the time goes in v6:
time: 32.6 us; the launch traced here: 32 us
  Pallas kernels  14.5 us (44%)
  starting transfers between devices  13.9 us (43%)
  waiting for transfers between devices  2.57 us (8%)
  between operations  0.8 us (2%)
    pallas_call x4, Pallas kernels, call(): pl.pallas_call(body, out_shape=outs, in_specs=[place(i, x) for i, x in en...  14.5 us
    all_to_all x1, starting transfers between devices, local(): got = lax.all_to_all(packed, 'gz', 0, 0, tiled=True)  5.32 us
    ppermute x1, starting transfers between devices, local(): far1 = lax.ppermute(begun, 'gz', far_pairs)  4.29 us
    ppermute x1, starting transfers between devices, local(): far2 = lax.ppermute(far2, 'gz', far_pairs)  3.51 us
    all_to_all x1, waiting for transfers between devices, local(): got = lax.all_to_all(packed, 'gz', 0, 0, tiled=True)  2.13 us
    ppermute x4, starting transfers between devices, local(): lax.ppermute(x, 'gz', chip_pairs)  0.81 us
  transfers between devices with their start and end apart: 7, of which 2 were waited for; matrix products, arithmetic and copies ran while one was open for 0% of the time, Pallas kernels for 31%

profile of v6, /device:TPU:1, one launch (start us, length us, event | category | flops | bytes accessed | tf_op | source)
XLA Modules:
  0.0 32.0 jit_solution(16188325475815950118)
XLA Ops:
  0.6 0.0 copy-start.1
  0.6 0.0 copy-start
  0.7 2.5 %shard_map.121.after_hbm = f32[3,192,256]{2,1,0:T(8,128)} custom-call(f32[3,2,192,256]{3,2,1,0:T(8,128)} %e_hbm.3, f32[3,2,192,256]{3,2,1,0:T(8,128)} %h_hbm.3, f32[2,192,256]{2,1,0:T(8,128)} %eps_hbm.5, f32[2,192,256]{2,1,0:T(8,128)} %sigma_hbm.5), custom_call_target="tpu_custom_call" | custom-call | flops 2300000000 | tf_op jit(solution)/shard_map/pallas_call | solution.py:626
  3.2 4.3 %collective-permute-start.3 = (f32[3,192,256]{2,1,0:T(8,128)}, f32[3,192,256]{2,1,0:T(8,128)S(1)}, u32[]{:S(2)}, u32[]{:S(2)}) collective-permute-start(f32[3,192,256]{2,1,0:T(8,128)} %shard_map.121.after_hbm), channel_id=1, source_target_pairs={{1,2},{2,1},{3,4},{4,3},{5,6},{6,5},{7,8},{8,7},{9,10},{10,9},{11,... | collective-permute-start | bytes 1769480 | tf_op jit(solution)/shard_map/ppermute | solution.py:679
  7.6 0.0 copy-start.6
  7.6 0.0 copy-start.5
  7.6 3.0 %shard_map.122 = (f32[16,4,128]{2,1,0:T(4,128)}, f32[1,192,256]{2,1,0:T(8,128)}, f32[1,192,256]{2,1,0:T(8,128)}, f32[1,192,256]{2,1,0:T(8,128)}, f32[2,192,256]{2,1,0:T(8,128)}, /*index=5*/f32[2,192,256]{2,1,0:T(8,128)}) custom-call(f32[3,2,192,256]{3,2,1,0:T(8,128)S(1)} %copy-done, f32[3,2,192,256]{3,2,1,0:T(8,128)S(1)} %copy-done.1, ...), custom_call_target="tpu_custom_call" | custom-call | flops 3449999872 | tf_op jit(solution)/shard_map/pallas_call | solution.py:626
  10.5 0.1 collective-permute-start
  10.6 0.5 %collective-permute-start.1 = (f32[1,192,256]{2,1,0:T(8,128)}, f32[1,192,256]{2,1,0:T(8,128)S(1)}, u32[]{:S(2)}, u32[]{:S(2)}) collective-permute-start(f32[1,192,256]{2,1,0:T(8,128)} %get-tuple-element.17), channel_id=1, source_target_pairs={{0,1},{1,0},{2,3},{3,2},{4,5},{5,4},{6,7},{7,6},{8,9},{9,8},{10,11... | collective-permute-start | bytes 589832 | tf_op jit(solution)/shard_map/ppermute | solution.py:718
  11.1 0.1 collective-permute-start.2
  11.2 5.3 %all-to-all-start = ((f32[16,4,128]{2,1,0:T(4,128)}), f32[16,4,128]{2,1,0:T(4,128)S(1)}, u32[]{:S(2)}, u32[]{:S(2)}) async-start(f32[16,4,128]{2,1,0:T(4,128)} %get-tuple-element.15), calls=%async_computation | async-start | bytes 65536 | tf_op jit(solution)/shard_map/all_to_all | solution.py:715
  16.5 0.2 collective-permute-start.4
  16.7 0.1 copy.14.bounds_ref
  16.8 0.0 collective-permute-done.chip0_hbm
  16.8 3.5 %collective-permute-start.5 = (f32[2,192,256]{2,1,0:T(8,128)}, f32[2,192,256]{2,1,0:T(8,128)S(1)}, u32[]{:S(2)}, u32[]{:S(2)}) collective-permute-start(f32[2,192,256]{2,1,0:T(8,128)} %get-tuple-element.25), channel_id=1, source_target_pairs={{1,2},{2,1},{3,4},{4,3},{5,6},{6,5},{7,8},{8,7},{9,10},{10,9},{11,... | collective-permute-start | bytes 1179656 | tf_op jit(solution)/shard_map/ppermute | solution.py:716
  20.3 2.1 %all-to-all-done.got_ref = f32[16,4,128]{2,1,0:T(4,128)S(1)} async-done(((f32[16,4,128]{2,1,0:T(4,128)}), f32[16,4,128]{2,1,0:T(4,128)S(1)}, u32[]{:S(2)}, u32[]{:S(2)}) %all-to-all-start) | async-done | bytes 32800 | tf_op jit(solution)/shard_map/all_to_all | solution.py:715
  22.4 0.0 collective-permute-done.1.chip1_hbm
  22.4 0.0 collective-permute-done.2.chip2_hbm
  22.4 0.0 collective-permute-done.3.far_hbm
  22.5 0.0 copy-done.5
  22.5 6.8 %shard_map.123 = (f32[3,2,192,256]{3,2,1,0:T(8,128)S(1)}, f32[3,2,192,256]{3,2,1,0:T(8,128)S(1)}, f32[2,192,256]{2,1,0:T(8,128)S(1)}, f32[2,192,256]{2,1,0:T(8,1...) custom-call(f32[3,2,192,256]{3,2,1,0:T(8,128)} %e_hbm.3, f32[3,2,192,256]{3,2,1,0:T(8,128)} %forward_hbm.1, ...), custom_call_target="tpu_custom_call" | custom-call | flops 6899999744 | tf_op jit(solution)/shard_map/pallas_call | solution.py:626
  29.3 0.0 collective-permute-done.4.chip_ref
  29.3 0.4 %collective-permute-done.5.far_ref = f32[2,192,256]{2,1,0:T(8,128)S(1)} collective-permute-done((f32[2,192,256]{2,1,0:T(8,128)}, f32[2,192,256]{2,1,0:T(8,128)S(1)}, u32[]{:S(2)}, u32[]{:S(2)}) %collective-permute-start.5) | collective-permute-done | bytes 393248 | tf_op jit(solution)/shard_map/ppermute | solution.py:716
  29.7 2.2 %shard_map.124 = (f32[3,2,192,256]{3,2,1,0:T(8,128)}, f32[3,2,192,256]{3,2,1,0:T(8,128)}, f32[2,192,256]{2,1,0:T(8,128)}) custom-call(f32[3,2,192,256]{3,2,1,0:T(8,128)S(1)} %get-tuple-element.19.forward_ref, f32[3,2,192,256]{3,2,1,0:T(8,128)S(1)} %get-tuple-element.20.h2_ref, ...), custom_call_target="tpu_custom_call", output_to_operand_aliasing={{1}: (9, {})} | custom-call | flops 2875000064 | tf_op jit(solution)/shard_map/pallas_call | solution.py:626
  (9 shorter events, 0.0 us)
Async XLA Ops:
  0.6 6.9 %copy-start.1 = (f32[3,2,192,256]{3,2,1,0:T(8,128)S(1)}, f32[3,2,192,256]{3,2,1,0:T(8,128)}, u32[]{:S(2)}) copy-start(f32[3,2,192,256]{3,2,1,0:T(8,128)} %h_hbm.3) | copy-start | bytes 3538948
  0.6 6.9 %copy-start = (f32[3,2,192,256]{3,2,1,0:T(8,128)S(1)}, f32[3,2,192,256]{3,2,1,0:T(8,128)}, u32[]{:S(2)}) copy-start(f32[3,2,192,256]{3,2,1,0:T(8,128)} %e_hbm.3) | copy-start | bytes 3538948
  0.7 6.9 %copy-start.2 = (f32[3,256]{1,0:T(4,128)S(1)}, f32[3,256]{1,0:T(4,128)}, u32[]{:S(2)}) copy-start(f32[3,256]{1,0:T(4,128)} %amplitude_ref.1) | copy-start | bytes 9220
  0.7 6.9 %copy-start.4 = (s32[256,1]{0,1:T(1,128)S(1)}, s32[256,1]{0,1:T(1,128)}, u32[]{:S(2)}) copy-start(s32[256,1]{0,1:T(1,128)} %param.16) | copy-start | bytes 3076
  0.7 6.9 %copy-start.3 = (s32[256,1]{0,1:T(1,128)S(1)}, s32[256,1]{0,1:T(1,128)}, u32[]{:S(2)}) copy-start(s32[256,1]{0,1:T(1,128)} %param.15) | copy-start | bytes 3076
  3.2 19.2 %collective-permute-start.3 = (f32[3,192,256]{2,1,0:T(8,128)}, f32[3,192,256]{2,1,0:T(8,128)S(1)}, u32[]{:S(2)}, u32[]{:S(2)}) collective-permute-start(f32[3,192,256]{2,1,0:T(8,128)} %shard_map.121.after_hbm), channel_id=1, source_target_pairs={{1,2},{2,1},{3,4},{4,3},{5,6},{6,5},{7,8},{8,7},{9,10},{10,9},{11,... | collective-permute-start | bytes 1769480 | tf_op jit(solution)/shard_map/ppermute | solution.py:679
  7.6 9.1 %copy-start.6 = (s32[3,2]{0,1:T(2,128)S(1)}, s32[3,2]{0,1:T(2,128)}, u32[]{:S(2)}) copy-start(s32[3,2]{0,1:T(2,128)} %param.19) | copy-start | bytes 76
  7.6 14.9 %copy-start.5 = (f32[2,2]{1,0:T(2,128)S(1)}, f32[2,2]{1,0:T(2,128)}, u32[]{:S(2)}) copy-start(f32[2,2]{1,0:T(2,128)} %timing_ref.3) | copy-start | bytes 52
  10.5 6.2 %collective-permute-start = (f32[1,192,256]{2,1,0:T(8,128)}, f32[1,192,256]{2,1,0:T(8,128)S(1)}, u32[]{:S(2)}, u32[]{:S(2)}) collective-permute-start(f32[1,192,256]{2,1,0:T(8,128)} %get-tuple-element.16), channel_id=1, source_target_pairs={{0,1},{1,0},{2,3},{3,2},{4,5},{5,4},{6,7},{7,6},{8,9},{9,8},{10,11... | collective-permute-start | bytes 589832 | tf_op jit(solution)/shard_map/ppermute | solution.py:718
  10.6 11.8 %collective-permute-start.1 = (f32[1,192,256]{2,1,0:T(8,128)}, f32[1,192,256]{2,1,0:T(8,128)S(1)}, u32[]{:S(2)}, u32[]{:S(2)}) collective-permute-start(f32[1,192,256]{2,1,0:T(8,128)} %get-tuple-element.17), channel_id=1, source_target_pairs={{0,1},{1,0},{2,3},{3,2},{4,5},{5,4},{6,7},{7,6},{8,9},{9,8},{10,11... | collective-permute-start | bytes 589832 | tf_op jit(solution)/shard_map/ppermute | solution.py:718
  11.1 11.3 %collective-permute-start.2 = (f32[1,192,256]{2,1,0:T(8,128)}, f32[1,192,256]{2,1,0:T(8,128)S(1)}, u32[]{:S(2)}, u32[]{:S(2)}) collective-permute-start(f32[1,192,256]{2,1,0:T(8,128)} %get-tuple-element.18), channel_id=1, source_target_pairs={{0,1},{1,0},{2,3},{3,2},{4,5},{5,4},{6,7},{7,6},{8,9},{9,8},{10,11... | collective-permute-start | bytes 589832 | tf_op jit(solution)/shard_map/ppermute | solution.py:718
  11.2 11.2 %all-to-all-start = ((f32[16,4,128]{2,1,0:T(4,128)}), f32[16,4,128]{2,1,0:T(4,128)S(1)}, u32[]{:S(2)}, u32[]{:S(2)}) async-start(f32[16,4,128]{2,1,0:T(4,128)} %get-tuple-element.15), calls=%async_computation | async-start | bytes 65536 | tf_op jit(solution)/shard_map/all_to_all | solution.py:715
  16.5 12.8 %collective-permute-start.4 = (f32[2,192,256]{2,1,0:T(8,128)}, f32[2,192,256]{2,1,0:T(8,128)S(1)}, u32[]{:S(2)}, u32[]{:S(2)}) collective-permute-start(f32[2,192,256]{2,1,0:T(8,128)} %get-tuple-element.24), channel_id=1, source_target_pairs={{0,1},{1,0},{2,3},{3,2},{4,5},{5,4},{6,7},{7,6},{8,9},{9,8},{10,11... | collective-permute-start | bytes 1179656 | tf_op jit(solution)/shard_map/ppermute | solution.py:718
  16.8 12.9 %collective-permute-start.5 = (f32[2,192,256]{2,1,0:T(8,128)}, f32[2,192,256]{2,1,0:T(8,128)S(1)}, u32[]{:S(2)}, u32[]{:S(2)}) collective-permute-start(f32[2,192,256]{2,1,0:T(8,128)} %get-tuple-element.25), channel_id=1, source_target_pairs={{1,2},{2,1},{3,4},{4,3},{5,6},{6,5},{7,8},{8,7},{9,10},{10,9},{11,... | collective-permute-start | bytes 1179656 | tf_op jit(solution)/shard_map/ppermute | solution.py:716

commit v7 on v6

--- a/solution.py
+++ b/solution.py
@@ -127,6 +127,16 @@
             copy.wait()
 
 
+def start_all(copies):
+    for copy in copies:
+        copy.start()
+
+
+def wait_all(copies):
+    for copy in copies:
+        copy.wait()
+
+
 def by_parity(when_odd, when_even):
     odd = odd_device()
     pl.when(odd)(when_odd)
@@ -237,8 +247,6 @@
     packed_hbm,
     chip0_hbm,
     chip1_hbm,
-    chip2_hbm,
-    chip3_hbm,
     far_hbm,
     h1_ref,
     e1_ref,
@@ -297,10 +305,8 @@
         rows = pl.ds(g * part, part)
         pairs = (
             (far_ref, far_hbm),
-            (chip_ref.at[0:1], chip0_hbm),
-            (chip_ref.at[1:2], chip1_hbm),
-            (chip_ref.at[2:3], chip2_hbm),
-            (chip_ref.at[3:5], chip3_hbm),
+            (chip_ref.at[0:3], chip0_hbm),
+            (chip_ref.at[3:5], chip1_hbm),
         )
         for i, (a, b) in enumerate(pairs):
             out.append(pltpu.make_async_copy(a.at[:, rows], b.at[:, rows], out_sems.at[g, i]))
@@ -374,15 +380,14 @@
 
 def middle(
     cap,
-    e_hbm,
+    e_ref,
     forward_hbm,
     got_ref,
-    h_hbm,
+    h_ref,
     eps_hbm,
     sigma_hbm,
     chip0_hbm,
     chip1_hbm,
-    chip2_hbm,
     far_hbm,
     timing_ref,
     bounds_ref,
@@ -391,9 +396,9 @@
     grad_ref,
     cb_ref,
     forward_ref,
+    eout_hbm,
     hout_hbm,
-    e_ref,
-    h_ref,
+    gout_hbm,
     h1_ref,
     e1_ref,
     mat_ref,
@@ -407,14 +412,13 @@
     dza,
     sems,
     out_sems,
+    odd_sems,
+    even_sems,
 ):
     pairs = (
-        (e_hbm, e_ref),
-        (h_hbm, h_ref),
         (far_hbm, far_ref),
-        (chip0_hbm, chip_ref.at[0:1]),
-        (chip1_hbm, chip_ref.at[1:2]),
-        (chip2_hbm, chip_ref.at[2:3]),
+        (chip0_hbm, chip_ref.at[0:3]),
+        (chip1_hbm, chip_ref.at[3:5]),
         (eps_hbm, mat_ref.at[0]),
         (sigma_hbm, mat_ref.at[1]),
         (forward_hbm, forward_ref),
@@ -423,10 +427,8 @@
     for copy in copies:
         copy.start()
     place_entries(cap, got_ref, own_ref, sbelow_ref, sabove_ref)
-    for copy in copies[:2]:
-        copy.wait()
     over_rows(e_ref.shape[2], lambda c: magnetic_step(c, e_ref, h_ref, h1_ref))
-    for copy in copies[2:-1]:
+    for copy in copies[:-1]:
         copy.wait()
     over_rows(e_ref.shape[2], lambda c: electric_all(c, e_ref, h1_ref, e1_ref, mat_ref))
     slab, width_x = e_ref.shape[1], e_ref.shape[2]
@@ -461,8 +463,10 @@
         e1[top][0] = e1[top][0] + HALF * cb[top] * high[0]
         e1[top][1] = e1[top][1] + HALF * cb[top] * high[1]
         e1[top][2] = e1[top][2] - HALF * cb[top] * (bx + behind_y(high[1]))
-        c.put(fs, 0, cb_b * (hy - wave0 * c.get(sabove_ref, 0)))
-        c.put(fs, 1, -cb_b * (hx + wave0 * c.get(sabove_ref, 1)))
+        from_chip = [c.get(chip_ref, k) for k in (3, 4)]
+        beside = [jnp.where(odd, 0.0, v) for v in from_chip]
+        c.put(fs, 0, beside[0] + cb_b * (hy - wave0 * c.get(sabove_ref, 0)))
+        c.put(fs, 1, beside[1] - cb_b * (hx + wave0 * c.get(sabove_ref, 1)))
         for z in range(slab):
             for k in range(3):
                 c.put(e1_ref, k, z, e1[z][k])
@@ -472,8 +476,9 @@
             HALF * (c.behind_x(e_ref, 0, 0) + behind_y(ey)) + wave0 * c.get(sbelow_ref, 2)
         )
         c.put(dza, dz)
-        c.put(h2a, 0, has_below * HALF * (ey - dy + e1[0][1] - ahead_y(dz)))
-        c.put(h2a, 1, has_below * HALF * (dx - ex - e1[0][0]))
+        beside = [jnp.where(odd, v, 0.0) for v in from_chip]
+        c.put(h2a, 0, beside[0] + has_below * HALF * (ey - dy + e1[0][1] - ahead_y(dz)))
+        c.put(h2a, 1, beside[1] + has_below * HALF * (dx - ex - e1[0][0]))
 
     over_rows(width_x, first)
 
@@ -519,16 +524,44 @@
             c.put(grad_ref, z, mask * (weight0 * dot1 + weight1 * dot2))
 
     copies[-1].wait()
-    pairs = (
-        (h2_ref.at[0:2, 0:top], hout_hbm.at[0:2, 0:top]),
-        (h2_ref.at[2], hout_hbm.at[2]),
-    )
-    done = [pltpu.make_async_copy(a, b, out_sems.at[i]) for i, (a, b) in enumerate(pairs)]
+
+    def copies_of(pairs, sems):
+        return [pltpu.make_async_copy(a, b, sems.at[i]) for i, (a, b) in enumerate(pairs)]
+
+    done = copies_of(
+        (
+            (h2_ref.at[0:2, 0:top], hout_hbm.at[0:2, 0:top]),
+            (h2_ref.at[2], hout_hbm.at[2]),
+        ),
+        out_sems,
+    )
     for copy in done:
         copy.start()
-    over_rows(width_x, third)
-    for copy in done:
-        copy.wait()
+    part = width_x // 2
+    odd_copies, even_copies = [], []
+    for g in range(2):
+        over_rows(width_x, third, g * part, (g + 1) * part)
+        rows = pl.ds(g * part, part)
+        for_odd = copies_of(
+            (
+                (e2_ref.at[:, 0:top, rows], eout_hbm.at[:, 0:top, rows]),
+                (grad_ref.at[0:top, rows], gout_hbm.at[0:top, rows]),
+            ),
+            odd_sems.at[g],
+        )
+        for_even = copies_of(
+            (
+                (e2_ref.at[:, 1:slab, rows], eout_hbm.at[:, 1:slab, rows]),
+                (grad_ref.at[1:slab, rows], gout_hbm.at[1:slab, rows]),
+                (h2_ref.at[0:2, top, rows], hout_hbm.at[0:2, top, rows]),
+                (e2_ref.at[2, 0, rows], eout_hbm.at[2, 0, rows]),
+            ),
+            even_sems.at[g],
+        )
+        by_parity(lambda: start_all(for_odd), lambda: start_all(for_even))
+        odd_copies, even_copies = odd_copies + for_odd, even_copies + for_even
+    by_parity(lambda: wait_all(odd_copies), lambda: wait_all(even_copies))
+    wait_all(done)
 
 
 def last(
@@ -537,11 +570,12 @@
     e2_ref,
     gradp_ref,
     cb_ref,
-    chip_ref,
     far_ref,
     timing_ref,
     bounds_ref,
+    ein_hbm,
     hin_hbm,
+    gin_hbm,
     eout_hbm,
     hout_hbm,
     grad_hbm,
@@ -552,51 +586,52 @@
 ):
     slab, width_x = e2_ref.shape[1], e2_ref.shape[2]
     top = slab - 1
-    odd = odd_device()
     weight1 = timing_ref[1, 1]
     part = width_x // PARTS
 
-    def body(c):
-        chip = [c.get(chip_ref, k) for k in range(2)]
-        far = [c.get(far_ref, k) for k in range(2)]
-        low = [jnp.where(odd, a, b) for a, b in zip(chip, far)]
-        high = [jnp.where(odd, b, a) for a, b in zip(chip, far)]
-        bx = jnp.where(odd, c.behind_x(far_ref, 0), c.behind_x(chip_ref, 0))
-        cb_low, cb_top = c.get(cb_ref, 0), HALF * c.get(cb_ref, top)
-        more = [[0.0] * 3 for _ in range(slab)]
-        more[0][0] = cb_low * low[1]
-        more[0][1] = -cb_low * low[0]
-        more[top][0] = more[top][0] + cb_top * high[0]
-        more[top][1] = more[top][1] + cb_top * high[1]
-        more[top][2] = -cb_top * (bx + behind_y(high[1]))
-        for z in range(slab):
-            dot = 0.0
-            for k in range(3):
-                e2 = c.get(e2_ref, k, z)
-                if k < 2 or z == top:
-                    e2 = e2 + more[z][k]
-                    dot = dot + more[z][k] * c.get(forward_ref, k, z)
-                c.put(e_ref, k, z, e2)
-            mask = inside(c, bounds_ref, z, slab, cb_low.shape)
-            c.put(grad_ref, z, c.get(gradp_ref, z) + (weight1 * mask) * dot)
-        c.put(h_ref, 0, c.get(h2_ref, 0, top) + HALF * high[1])
-        c.put(h_ref, 1, c.get(h2_ref, 1, top) - HALF * high[0])
-
-    copies = []
-    for g in range(PARTS):
-        over_rows(width_x, body, g * part, (g + 1) * part)
-        rows = pl.ds(g * part, part)
-        pairs = (
-            (e_ref.at[:, :, rows], eout_hbm.at[:, :, rows]),
-            (h_ref.at[:, rows], hout_hbm.at[0:2, top, rows]),
-            (grad_ref.at[:, rows], grad_hbm.at[:, rows]),
-        )
-        for i, (a, b) in enumerate(pairs):
-            copy = pltpu.make_async_copy(a, b, sems.at[g, i])
-            copy.start()
-            copies.append(copy)
-    for copy in copies:
-        copy.wait()
+    def finish(c, z, deltas):
+        dot = 0.0
+        for k, delta in enumerate(deltas):
+            dot = dot + delta * c.get(forward_ref, k, z)
+            c.put(e_ref, k, c.get(e2_ref, k, z) + delta)
+        mask = inside(c, bounds_ref, z, slab, dot.shape)
+        c.put(grad_ref, c.get(gradp_ref, z) + (weight1 * mask) * dot)
+
+    def above(c):
+        fx, fy = c.get(far_ref, 0), c.get(far_ref, 1)
+        cb = HALF * c.get(cb_ref, top)
+        finish(c, top, (cb * fx, cb * fy, -cb * (c.behind_x(far_ref, 0) + behind_y(fy))))
+        c.put(h_ref, 0, c.get(h2_ref, 0, top) + HALF * fy)
+        c.put(h_ref, 1, c.get(h2_ref, 1, top) - HALF * fx)
+
+    def below(c):
+        cb = c.get(cb_ref, 0)
+        finish(c, 0, (cb * c.get(far_ref, 1), -cb * c.get(far_ref, 0)))
+
+    def run(z, body, comps, with_h):
+        copies = []
+        for g in range(PARTS):
+            over_rows(width_x, body, g * part, (g + 1) * part)
+            rows = pl.ds(g * part, part)
+            pairs = [
+                (e_ref.at[0:comps, rows], eout_hbm.at[0:comps, z, rows]),
+                (grad_ref.at[rows], grad_hbm.at[z, rows]),
+            ]
+            if with_h:
+                pairs.append((h_ref.at[:, rows], hout_hbm.at[0:2, z, rows]))
+            for i, (a, b) in enumerate(pairs):
+                copies.append(pltpu.make_async_copy(a, b, sems.at[g, i]))
+                copies[-1].start()
+        for copy in copies:
+            copy.wait()
+
+    by_parity(lambda: run(top, above, 3, True), lambda: run(0, below, 2, False))
+
+
+def settle(near_hbm, far_hbm, out_hbm, near_ref, sem):
+    copy = pltpu.make_async_copy(near_hbm.at[0, 0:8], near_ref, sem)
+    copy.start()
+    copy.wait()
 
 
 def shape(*dims):
@@ -677,13 +712,11 @@
         in_hbm=(0, 1, 2, 3),
     )
     far1 = lax.ppermute(begun, "gz", far_pairs)
-    packed, chip0, chip1, chip2, chip3, far2 = call(
+    packed, chip0, chip1, far2 = call(
         functools.partial(halves_second, cap),
         (
             sent(peers, 4, lanes),
-            sent(1, *layer),
-            sent(1, *layer),
-            sent(1, *layer),
+            sent(3, *layer),
             sent(2, *layer),
             sent(2, *layer),
         ),
@@ -708,16 +741,26 @@
             VMEM((peers, 4, lanes), F32),
             dma((2,)),
             dma((1,)),
-            dma((PARTS, 5)),
+            dma((PARTS, 3)),
         ),
         in_hbm=(2, 3, 7),
     )
     got = lax.all_to_all(packed, "gz", 0, 0, tiled=True)
+    far2 = call(
+        settle,
+        sent(2, *layer),
+        (chip1, far2),
+        3,
+        8,
+        scratch=(VMEM((8, wy), F32), dma),
+        in_hbm=(0, 1),
+        aliases={1: 0},
+    )
     far2 = lax.ppermute(far2, "gz", far_pairs)
-    chip0, chip1, chip2, chip3 = (
-        lax.ppermute(x, "gz", chip_pairs) for x in (chip0, chip1, chip2, chip3)
-    )
-    h2, e2, grad, cb, forward, h_part = call(
+    chip0, chip1 = (
+        lax.ppermute(x, "gz", chip_pairs) for x in (chip0, chip1)
+    )
+    h2, e2, grad, cb, forward, e_part, h_part, grad_part = call(
         functools.partial(middle, cap),
         (
             kept(*fields),
@@ -726,17 +769,29 @@
             kept(*slabs),
             kept(*fields),
             sent(*fields),
-        ),
-        (e_field, forward_field, got, h_field, permittivity, conductivity, chip0, chip1, chip2, far1, timing, bounds),
+            sent(*fields),
+            sent(*slabs),
+        ),
+        (
+            e_field,
+            forward_field,
+            got,
+            h_field,
+            permittivity,
+            conductivity,
+            chip0,
+            chip1,
+            far1,
+            timing,
+            bounds,
+        ),
         6,
         24,
         scratch=(
             VMEM(fields, F32),
             VMEM(fields, F32),
-            VMEM(fields, F32),
-            VMEM(fields, F32),
             VMEM((2, *slabs), F32),
-            VMEM((3, *layer), F32),
+            VMEM((5, *layer), F32),
             VMEM((3, *layer), F32),
             VMEM(fields, F32),
             VMEM((3, *layer), F32),
@@ -744,26 +799,28 @@
             VMEM((2, *layer), F32),
             VMEM((2, *layer), F32),
             VMEM(layer, F32),
-            dma((9,)),
+            dma((6,)),
             dma((2,)),
-        ),
-        in_hbm=(0, 1, 3, 4, 5),
-        anywhere=(6, 7, 8, 9),
+            dma((2, 2)),
+            dma((2, 4)),
+        ),
+        in_hbm=(1, 4, 5, 6, 7),
+        anywhere=(8,),
     )
     return call(
         last,
         (sent(*fields), sent(*fields), sent(*slabs)),
-        (forward, h2, e2, grad, cb, chip3, far2, timing, bounds, h_part),
+        (forward, h2, e2, grad, cb, far2, timing, bounds, e_part, h_part, grad_part),
         2.5,
         16,
         scratch=(
-            VMEM(fields, F32),
+            VMEM((3, *layer), F32),
             VMEM((2, *layer), F32),
-            VMEM(slabs, F32),
+            VMEM(layer, F32),
             dma((PARTS, 3)),
         ),
-        in_hbm=(9,),
-        aliases={9: 1},
+        in_hbm=(8, 9, 10),
+        aliases={8: 0, 9: 1, 10: 2},
     )
 
 

time: 32.6 us -> 31.9 us (0.979)
  starting transfers between devices: 13.9 us -> 13.4 us
  Pallas kernels: 14.5 us -> 14.9 us
    all_to_all x1, waiting for transfers between devices: 2.13 us -> 1.62 us  [local(): got = lax.all_to_all(packed, 'gz', 0, 0, tiled=True)]
    pallas_call x4 -> x5, Pallas kernels: 14.5 us -> 14.9 us  [call(): pl.pallas_call(body, out_shape=outs, in_specs=[place(i, x) for i, x in en...]
    ppermute x4 -> x2, starting transfers between devices: 0.81 us -> 0.57 us  [local(): chip0, chip1 = (lax.ppermute(x, 'gz', chip_pairs) for x in (chip0, chip1))]
  transfers between devices with their start and end apart: 7 -> 5, of which waited for: 2 -> 2; matrix products, arithmetic and copies ran while one was open for 0% -> 0% of each run, Pallas kernels for 31% -> 33%
where the time goes in v7:
time: 31.9 us; the launch traced here: 31.6 us
  Pallas kernels  14.9 us (47%)
  starting transfers between devices  13.4 us (42%)
  waiting for transfers between devices  2.32 us (7%)
  between operations  0.8 us (3%)
    pallas_call x5, Pallas kernels, call(): pl.pallas_call(body, out_shape=outs, in_specs=[place(i, x) for i, x in en...  14.9 us
    all_to_all x1, starting transfers between devices, local(): got = lax.all_to_all(packed, 'gz', 0, 0, tiled=True)  5.02 us
    ppermute x1, starting transfers between devices, local(): far1 = lax.ppermute(begun, 'gz', far_pairs)  4.29 us
    ppermute x1, starting transfers between devices, local(): far2 = lax.ppermute(far2, 'gz', far_pairs)  3.54 us
    all_to_all x1, waiting for transfers between devices, local(): got = lax.all_to_all(packed, 'gz', 0, 0, tiled=True)  1.62 us
    ppermute x1, waiting for transfers between devices, local(): far2 = lax.ppermute(far2, 'gz', far_pairs)  0.69 us
  transfers between devices with their start and end apart: 5, of which 2 were waited for; matrix products, arithmetic and copies ran while one was open for 0% of the time, Pallas kernels for 33%

profile of v7, /device:TPU:1, one launch (start us, length us, event | category | flops | bytes accessed | tf_op | source)
XLA Modules:
  0.0 31.6 jit_solution(10748271903714413242)
XLA Ops:
  0.6 0.0 copy-start.1
  0.6 0.0 copy-start
  0.7 0.0 copy-start.2
  0.7 0.0 copy-start.4
  0.7 0.0 copy-start.3
  0.7 2.5 %shard_map.121.after_hbm = f32[3,192,256]{2,1,0:T(8,128)} custom-call(f32[3,2,192,256]{3,2,1,0:T(8,128)} %e_ref.3, f32[3,2,192,256]{3,2,1,0:T(8,128)} %h_ref.3, f32[2,192,256]{2,1,0:T(8,128)} %eps_hbm.5, f32[2,192,256]{2,1,0:T(8,128)} %sigma_hbm.5), custom_call_target="tpu_custom_call" | custom-call | flops 2300000000 | tf_op jit(solution)/shard_map/pallas_call | solution.py:661
  3.2 4.3 %collective-permute-start.2 = (f32[3,192,256]{2,1,0:T(8,128)}, f32[3,192,256]{2,1,0:T(8,128)S(1)}, u32[]{:S(2)}, u32[]{:S(2)}) collective-permute-start(f32[3,192,256]{2,1,0:T(8,128)} %shard_map.121.after_hbm), channel_id=1, source_target_pairs={{1,2},{2,1},{3,4},{4,3},{5,6},{6,5},{7,8},{8,7},{9,10},{10,9},{11,... | collective-permute-start | bytes 1769480 | tf_op jit(solution)/shard_map/ppermute | solution.py:714
  7.5 0.0 copy-done.1
  7.5 0.0 copy-done
  7.6 2.8 %shard_map.122 = (f32[16,4,128]{2,1,0:T(4,128)}, f32[3,192,256]{2,1,0:T(8,128)}, f32[2,192,256]{2,1,0:T(8,128)}, f32[2,192,256]{2,1,0:T(8,128)}) custom-call(f32[3,2,192,256]{3,2,1,0:T(8,128)S(1)} %copy-done, f32[3,2,192,256]{3,2,1,0:T(8,128)S(1)} %copy-done.1, f32[2,192,256]{2,1,0:T(8,128)} %eps_hbm.5, f32[2,192,256]{2,1,0:T(8,128)} %sigma_hbm.5, ...), custom_call_target="tpu_custom_call" | custom-call | flops 3449999872 | tf_op jit(solution)/shard_map/pallas_call | solution.py:661
  10.4 0.1 collective-permute-start
  10.5 0.5 %collective-permute-start.1 = (f32[2,192,256]{2,1,0:T(8,128)}, f32[2,192,256]{2,1,0:T(8,128)}, u32[]{:S(2)}, u32[]{:S(2)}) collective-permute-start(f32[2,192,256]{2,1,0:T(8,128)} %get-tuple-element.17.near_hbm), channel_id=1, source_target_pairs={{0,1},{1,0},{2,3},{3,2},{4,5},{5,4},{6,7},{7,6},{8,9},{9,8},{10,11... | collective-permute-start | bytes 1179656 | tf_op jit(solution)/shard_map/ppermute | solution.py:761
  11.0 5.0 %all-to-all-start = ((f32[16,4,128]{2,1,0:T(4,128)}), f32[16,4,128]{2,1,0:T(4,128)S(1)}, u32[]{:S(2)}, u32[]{:S(2)}) async-start(f32[16,4,128]{2,1,0:T(4,128)} %get-tuple-element.15), calls=%async_computation | async-start | bytes 65536 | tf_op jit(solution)/shard_map/all_to_all | solution.py:748
  16.0 0.0 copy-start.5
  16.0 0.7 %shard_map.124 = f32[2,192,256]{2,1,0:T(8,128)} custom-call(f32[2,192,256]{2,1,0:T(8,128)} %get-tuple-element.17.near_hbm, f32[2,192,256]{2,1,0:T(8,128)} %get-tuple-element.23.far_hbm), custom_call_target="tpu_custom_call", output_to_operand_aliasing={{}: (1, {})} | custom-call | flops 3449999872 | tf_op jit(solution)/shard_map/pallas_call | solution.py:661
  16.7 3.5 %collective-permute-start.3 = (f32[2,192,256]{2,1,0:T(8,128)}, f32[2,192,256]{2,1,0:T(8,128)S(1)}, u32[]{:S(2)}, u32[]{:S(2)}) collective-permute-start(f32[2,192,256]{2,1,0:T(8,128)} %shard_map.124), channel_id=1, source_target_pairs={{1,2},{2,1},{3,4},{4,3},{5,6},{6,5},{7,8},{8,7},{9,10},{10,9},{11,... | collective-permute-start | bytes 1179656 | tf_op jit(solution)/shard_map/ppermute | solution.py:759
  20.3 0.1 copy.17.bounds_ref
  20.4 1.6 %all-to-all-done.got_ref = f32[16,4,128]{2,1,0:T(4,128)S(1)} async-done(((f32[16,4,128]{2,1,0:T(4,128)}), f32[16,4,128]{2,1,0:T(4,128)S(1)}, u32[]{:S(2)}, u32[]{:S(2)}) %all-to-all-start) | async-done | bytes 32800 | tf_op jit(solution)/shard_map/all_to_all | solution.py:748
  22.0 0.0 collective-permute-done.1.chip1_hbm
  22.0 0.0 collective-permute-done.2.far_hbm
  22.0 0.0 collective-permute-done.chip0_hbm
  22.0 7.0 %shard_map.123 = (f32[3,2,192,256]{3,2,1,0:T(8,128)S(1)}, f32[3,2,192,256]{3,2,1,0:T(8,128)S(1)}, f32[2,192,256]{2,1,0:T(8,128)S(1)}, f32[2,192,256]{2,1,0:T(8,1...) custom-call(f32[3,2,192,256]{3,2,1,0:T(8,128)S(1)} %copy-done, ...), custom_call_target="tpu_custom_call" | custom-call | flops 6899999744 | tf_op jit(solution)/shard_map/pallas_call | solution.py:661
  29.0 0.7 %collective-permute-done.3.far_ref = f32[2,192,256]{2,1,0:T(8,128)S(1)} collective-permute-done((f32[2,192,256]{2,1,0:T(8,128)}, f32[2,192,256]{2,1,0:T(8,128)S(1)}, u32[]{:S(2)}, u32[]{:S(2)}) %collective-permute-start.3) | collective-permute-done | bytes 393248 | tf_op jit(solution)/shard_map/ppermute | solution.py:759
  29.7 1.8 %shard_map.125 = (f32[3,2,192,256]{3,2,1,0:T(8,128)}, f32[3,2,192,256]{3,2,1,0:T(8,128)}, f32[2,192,256]{2,1,0:T(8,128)}) custom-call(f32[3,2,192,256]{3,2,1,0:T(8,128)S(1)} %get-tuple-element.18.forward_ref, f32[3,2,192,256]{3,2,1,0:T(8,128)S(1)} %get-tuple-element.19.h2_ref, ...), custom_call_target="tpu_custom_call", output_to_operand_aliasing={{0}: (8, {}), {1}: (9, {}), {2}: (10, {})} | custom-call | flops 2875000064 | tf_op jit(solution)/shard_map/pallas_call | solution.py:661
  (6 shorter events, 0.0 us)
Async XLA Ops:
  0.6 6.9 %copy-start.1 = (f32[3,2,192,256]{3,2,1,0:T(8,128)S(1)}, f32[3,2,192,256]{3,2,1,0:T(8,128)}, u32[]{:S(2)}) copy-start(f32[3,2,192,256]{3,2,1,0:T(8,128)} %h_ref.3) | copy-start | bytes 3538948
  0.6 6.9 %copy-start = (f32[3,2,192,256]{3,2,1,0:T(8,128)S(1)}, f32[3,2,192,256]{3,2,1,0:T(8,128)}, u32[]{:S(2)}) copy-start(f32[3,2,192,256]{3,2,1,0:T(8,128)} %e_ref.3) | copy-start | bytes 3538948
  0.7 6.9 %copy-start.2 = (f32[3,256]{1,0:T(4,128)S(1)}, f32[3,256]{1,0:T(4,128)}, u32[]{:S(2)}) copy-start(f32[3,256]{1,0:T(4,128)} %amplitude_ref.1) | copy-start | bytes 9220
  0.7 6.9 %copy-start.4 = (s32[256,1]{0,1:T(1,128)S(1)}, s32[256,1]{0,1:T(1,128)}, u32[]{:S(2)}) copy-start(s32[256,1]{0,1:T(1,128)} %param.16) | copy-start | bytes 3076
  0.7 6.9 %copy-start.3 = (s32[256,1]{0,1:T(1,128)S(1)}, s32[256,1]{0,1:T(1,128)}, u32[]{:S(2)}) copy-start(s32[256,1]{0,1:T(1,128)} %param.15) | copy-start | bytes 3076
  3.2 18.8 %collective-permute-start.2 = (f32[3,192,256]{2,1,0:T(8,128)}, f32[3,192,256]{2,1,0:T(8,128)S(1)}, u32[]{:S(2)}, u32[]{:S(2)}) collective-permute-start(f32[3,192,256]{2,1,0:T(8,128)} %shard_map.121.after_hbm), channel_id=1, source_target_pairs={{1,2},{2,1},{3,4},{4,3},{5,6},{6,5},{7,8},{8,7},{9,10},{10,9},{11,... | collective-permute-start | bytes 1769480 | tf_op jit(solution)/shard_map/ppermute | solution.py:714
  10.4 11.6 %collective-permute-start = (f32[3,192,256]{2,1,0:T(8,128)}, f32[3,192,256]{2,1,0:T(8,128)}, u32[]{:S(2)}, u32[]{:S(2)}) collective-permute-start(f32[3,192,256]{2,1,0:T(8,128)} %get-tuple-element.16), channel_id=1, source_target_pairs={{0,1},{1,0},{2,3},{3,2},{4,5},{5,4},{6,7},{7,6},{8,9},{9,8},{10,11... | collective-permute-start | bytes 1769480 | tf_op jit(solution)/shard_map/ppermute | solution.py:761
  10.5 11.5 %collective-permute-start.1 = (f32[2,192,256]{2,1,0:T(8,128)}, f32[2,192,256]{2,1,0:T(8,128)}, u32[]{:S(2)}, u32[]{:S(2)}) collective-permute-start(f32[2,192,256]{2,1,0:T(8,128)} %get-tuple-element.17.near_hbm), channel_id=1, source_target_pairs={{0,1},{1,0},{2,3},{3,2},{4,5},{5,4},{6,7},{7,6},{8,9},{9,8},{10,11... | collective-permute-start | bytes 1179656 | tf_op jit(solution)/shard_map/ppermute | solution.py:761
  11.0 11.0 %all-to-all-start = ((f32[16,4,128]{2,1,0:T(4,128)}), f32[16,4,128]{2,1,0:T(4,128)S(1)}, u32[]{:S(2)}, u32[]{:S(2)}) async-start(f32[16,4,128]{2,1,0:T(4,128)} %get-tuple-element.15), calls=%async_computation | async-start | bytes 65536 | tf_op jit(solution)/shard_map/all_to_all | solution.py:748
  16.0 4.3 %copy-start.6 = (s32[3,2]{0,1:T(2,128)S(1)}, s32[3,2]{0,1:T(2,128)}, u32[]{:S(2)}) copy-start(s32[3,2]{0,1:T(2,128)} %param.19) | copy-start | bytes 76
  16.0 6.0 %copy-start.5 = (f32[2,2]{1,0:T(2,128)S(1)}, f32[2,2]{1,0:T(2,128)}, u32[]{:S(2)}) copy-start(f32[2,2]{1,0:T(2,128)} %timing_ref.3) | copy-start | bytes 52
  16.7 13.0 %collective-permute-start.3 = (f32[2,192,256]{2,1,0:T(8,128)}, f32[2,192,256]{2,1,0:T(8,128)S(1)}, u32[]{:S(2)}, u32[]{:S(2)}) collective-permute-start(f32[2,192,256]{2,1,0:T(8,128)} %shard_map.124), channel_id=1, source_target_pairs={{1,2},{2,1},{3,4},{4,3},{5,6},{6,5},{7,8},{8,7},{9,10},{10,9},{11,... | collective-permute-start | bytes 1179656 | tf_op jit(solution)/shard_map/ppermute | solution.py:759

commit v8 on v7

--- a/solution.py
+++ b/solution.py
@@ -395,6 +395,7 @@
     e2_ref,
     grad_ref,
     cb_ref,
+    share_ref,
     forward_ref,
     eout_hbm,
     hout_hbm,
@@ -521,6 +522,7 @@
                 dot1 = dot1 + e1 * fwd
                 dot2 = dot2 + e2 * fwd
             mask = inside(c, bounds_ref, z, slab, ca.shape)
+            c.put(share_ref, z, weight1 * mask)
             c.put(grad_ref, z, mask * (weight0 * dot1 + weight1 * dot2))
 
     copies[-1].wait()
@@ -570,9 +572,8 @@
     e2_ref,
     gradp_ref,
     cb_ref,
+    share_ref,
     far_ref,
-    timing_ref,
-    bounds_ref,
     ein_hbm,
     hin_hbm,
     gin_hbm,
@@ -586,7 +587,6 @@
 ):
     slab, width_x = e2_ref.shape[1], e2_ref.shape[2]
     top = slab - 1
-    weight1 = timing_ref[1, 1]
     part = width_x // PARTS
 
     def finish(c, z, deltas):
@@ -594,8 +594,7 @@
         for k, delta in enumerate(deltas):
             dot = dot + delta * c.get(forward_ref, k, z)
             c.put(e_ref, k, c.get(e2_ref, k, z) + delta)
-        mask = inside(c, bounds_ref, z, slab, dot.shape)
-        c.put(grad_ref, c.get(gradp_ref, z) + (weight1 * mask) * dot)
+        c.put(grad_ref, c.get(gradp_ref, z) + c.get(share_ref, z) * dot)
 
     def above(c):
         fx, fy = c.get(far_ref, 0), c.get(far_ref, 1)
@@ -760,11 +759,12 @@
     chip0, chip1 = (
         lax.ppermute(x, "gz", chip_pairs) for x in (chip0, chip1)
     )
-    h2, e2, grad, cb, forward, e_part, h_part, grad_part = call(
+    h2, e2, grad, cb, share, forward, e_part, h_part, grad_part = call(
         functools.partial(middle, cap),
         (
             kept(*fields),
             kept(*fields),
+            kept(*slabs),
             kept(*slabs),
             kept(*slabs),
             kept(*fields),
@@ -810,7 +810,7 @@
     return call(
         last,
         (sent(*fields), sent(*fields), sent(*slabs)),
-        (forward, h2, e2, grad, cb, far2, timing, bounds, e_part, h_part, grad_part),
+        (forward, h2, e2, grad, cb, share, far2, e_part, h_part, grad_part),
         2.5,
         16,
         scratch=(
@@ -819,8 +819,8 @@
             VMEM(layer, F32),
             dma((PARTS, 3)),
         ),
-        in_hbm=(8, 9, 10),
-        aliases={8: 0, 9: 1, 10: 2},
+        in_hbm=(7, 8, 9),
+        aliases={7: 0, 8: 1, 9: 2},
     )
 
 

time: 31.9 us -> 31.3 us (0.981)
  Pallas kernels: 14.9 us -> 14.3 us
    pallas_call x5, Pallas kernels: 14.9 us -> 14.3 us  [call(): pl.pallas_call(body, out_shape=outs, in_specs=[place(i, x) for i, x in en...]
  transfers between devices with their start and end apart: 5 -> 5, of which waited for: 2 -> 2; matrix products, arithmetic and copies ran while one was open for 0% -> 0% of each run, Pallas kernels for 33% -> 34%
where the time goes in v8:
time: 31.3 us; the launch traced here: 31 us
  Pallas kernels  14.3 us (46%)
  starting transfers between devices  13.4 us (43%)
  waiting for transfers between devices  2.29 us (7%)
  between operations  0.8 us (3%)
    pallas_call x5, Pallas kernels, call(): pl.pallas_call(body, out_shape=outs, in_specs=[place(i, x) for i, x in en...  14.3 us
    all_to_all x1, starting transfers between devices, local(): got = lax.all_to_all(packed, 'gz', 0, 0, tiled=True)  5.02 us
    ppermute x1, starting transfers between devices, local(): far1 = lax.ppermute(begun, 'gz', far_pairs)  4.29 us
    ppermute x1, starting transfers between devices, local(): far2 = lax.ppermute(far2, 'gz', far_pairs)  3.54 us
    all_to_all x1, waiting for transfers between devices, local(): got = lax.all_to_all(packed, 'gz', 0, 0, tiled=True)  1.62 us
    ppermute x1, waiting for transfers between devices, local(): far2 = lax.ppermute(far2, 'gz', far_pairs)  0.67 us
  transfers between devices with their start and end apart: 5, of which 2 were waited for; matrix products, arithmetic and copies ran while one was open for 0% of the time, Pallas kernels for 34%

profile of v8, /device:TPU:1, one launch (start us, length us, event | category | flops | bytes accessed | tf_op | source)
XLA Modules:
  0.0 31.0 jit_solution(18230276271419856909)
XLA Ops:
  0.6 0.0 copy-start.1
  0.6 0.0 copy-start
  0.7 0.0 copy-start.2
  0.7 0.0 copy-start.4
  0.7 0.0 copy-start.3
  0.7 2.5 %shard_map.121.after_hbm = f32[3,192,256]{2,1,0:T(8,128)} custom-call(f32[3,2,192,256]{3,2,1,0:T(8,128)} %e_ref.3, f32[3,2,192,256]{3,2,1,0:T(8,128)} %h_ref.3, f32[2,192,256]{2,1,0:T(8,128)} %eps_hbm.5, f32[2,192,256]{2,1,0:T(8,128)} %sigma_hbm.5), custom_call_target="tpu_custom_call" | custom-call | flops 2300000000 | tf_op jit(solution)/shard_map/pallas_call | solution.py:660
  3.2 4.3 %collective-permute-start.2 = (f32[3,192,256]{2,1,0:T(8,128)}, f32[3,192,256]{2,1,0:T(8,128)S(1)}, u32[]{:S(2)}, u32[]{:S(2)}) collective-permute-start(f32[3,192,256]{2,1,0:T(8,128)} %shard_map.121.after_hbm), channel_id=1, source_target_pairs={{1,2},{2,1},{3,4},{4,3},{5,6},{6,5},{7,8},{8,7},{9,10},{10,9},{11,... | collective-permute-start | bytes 1769480 | tf_op jit(solution)/shard_map/ppermute | solution.py:713
  7.5 0.0 copy-done.1
  7.5 0.0 copy-done
  7.6 2.8 %shard_map.122 = (f32[16,4,128]{2,1,0:T(4,128)}, f32[3,192,256]{2,1,0:T(8,128)}, f32[2,192,256]{2,1,0:T(8,128)}, f32[2,192,256]{2,1,0:T(8,128)}) custom-call(f32[3,2,192,256]{3,2,1,0:T(8,128)S(1)} %copy-done, f32[3,2,192,256]{3,2,1,0:T(8,128)S(1)} %copy-done.1, f32[2,192,256]{2,1,0:T(8,128)} %eps_hbm.5, f32[2,192,256]{2,1,0:T(8,128)} %sigma_hbm.5, ...), custom_call_target="tpu_custom_call" | custom-call | flops 3449999872 | tf_op jit(solution)/shard_map/pallas_call | solution.py:660
  10.4 0.1 collective-permute-start
  10.5 0.5 %collective-permute-start.1 = (f32[2,192,256]{2,1,0:T(8,128)}, f32[2,192,256]{2,1,0:T(8,128)}, u32[]{:S(2)}, u32[]{:S(2)}) collective-permute-start(f32[2,192,256]{2,1,0:T(8,128)} %get-tuple-element.18.near_hbm), channel_id=1, source_target_pairs={{0,1},{1,0},{2,3},{3,2},{4,5},{5,4},{6,7},{7,6},{8,9},{9,8},{10,11... | collective-permute-start | bytes 1179656 | tf_op jit(solution)/shard_map/ppermute | solution.py:760
  11.0 5.0 %all-to-all-start = ((f32[16,4,128]{2,1,0:T(4,128)}), f32[16,4,128]{2,1,0:T(4,128)S(1)}, u32[]{:S(2)}, u32[]{:S(2)}) async-start(f32[16,4,128]{2,1,0:T(4,128)} %get-tuple-element.16), calls=%async_computation | async-start | bytes 65536 | tf_op jit(solution)/shard_map/all_to_all | solution.py:747
  16.0 0.0 copy-start.5
  16.0 0.7 %shard_map.124 = f32[2,192,256]{2,1,0:T(8,128)} custom-call(f32[2,192,256]{2,1,0:T(8,128)} %get-tuple-element.18.near_hbm, f32[2,192,256]{2,1,0:T(8,128)} %get-tuple-element.25.far_hbm), custom_call_target="tpu_custom_call", output_to_operand_aliasing={{}: (1, {})} | custom-call | flops 3449999872 | tf_op jit(solution)/shard_map/pallas_call | solution.py:660
  16.7 3.5 %collective-permute-start.3 = (f32[2,192,256]{2,1,0:T(8,128)}, f32[2,192,256]{2,1,0:T(8,128)S(1)}, u32[]{:S(2)}, u32[]{:S(2)}) collective-permute-start(f32[2,192,256]{2,1,0:T(8,128)} %shard_map.124), channel_id=1, source_target_pairs={{1,2},{2,1},{3,4},{4,3},{5,6},{6,5},{7,8},{8,7},{9,10},{10,9},{11,... | collective-permute-start | bytes 1179656 | tf_op jit(solution)/shard_map/ppermute | solution.py:758
  20.3 0.1 copy.17.bounds_ref
  20.4 1.6 %all-to-all-done.got_ref = f32[16,4,128]{2,1,0:T(4,128)S(1)} async-done(((f32[16,4,128]{2,1,0:T(4,128)}), f32[16,4,128]{2,1,0:T(4,128)S(1)}, u32[]{:S(2)}, u32[]{:S(2)}) %all-to-all-start) | async-done | bytes 32800 | tf_op jit(solution)/shard_map/all_to_all | solution.py:747
  22.0 0.0 collective-permute-done.1.chip1_hbm
  22.0 0.0 collective-permute-done.2.far_hbm
  22.0 0.0 collective-permute-done.chip0_hbm
  22.0 7.0 %shard_map.123 = (f32[3,2,192,256]{3,2,1,0:T(8,128)S(1)}, f32[3,2,192,256]{3,2,1,0:T(8,128)S(1)}, f32[2,192,256]{2,1,0:T(8,128)S(1)}, f32[2,192,256]{2,1,0:T(8,1...) custom-call(f32[3,2,192,256]{3,2,1,0:T(8,128)S(1)} %copy-done, ...), custom_call_target="tpu_custom_call" | custom-call | flops 6899999744 | tf_op jit(solution)/shard_map/pallas_call | solution.py:660
  29.1 0.7 %collective-permute-done.3.far_ref = f32[2,192,256]{2,1,0:T(8,128)S(1)} collective-permute-done((f32[2,192,256]{2,1,0:T(8,128)}, f32[2,192,256]{2,1,0:T(8,128)S(1)}, u32[]{:S(2)}, u32[]{:S(2)}) %collective-permute-start.3) | collective-permute-done | bytes 393248 | tf_op jit(solution)/shard_map/ppermute | solution.py:758
  29.7 1.2 %shard_map.125 = (f32[3,2,192,256]{3,2,1,0:T(8,128)}, f32[3,2,192,256]{3,2,1,0:T(8,128)}, f32[2,192,256]{2,1,0:T(8,128)}) custom-call(f32[3,2,192,256]{3,2,1,0:T(8,128)S(1)} %get-tuple-element.19.forward_ref, f32[3,2,192,256]{3,2,1,0:T(8,128)S(1)} %get-tuple-element.20.h2_ref, ...), custom_call_target="tpu_custom_call", output_to_operand_aliasing={{0}: (7, {}), {1}: (8, {}), {2}: (9, {})} | custom-call | flops 2875000064 | tf_op jit(solution)/shard_map/pallas_call | solution.py:660
  (6 shorter events, 0.0 us)
Async XLA Ops:
  0.6 6.9 %copy-start.1 = (f32[3,2,192,256]{3,2,1,0:T(8,128)S(1)}, f32[3,2,192,256]{3,2,1,0:T(8,128)}, u32[]{:S(2)}) copy-start(f32[3,2,192,256]{3,2,1,0:T(8,128)} %h_ref.3) | copy-start | bytes 3538948
  0.6 6.9 %copy-start = (f32[3,2,192,256]{3,2,1,0:T(8,128)S(1)}, f32[3,2,192,256]{3,2,1,0:T(8,128)}, u32[]{:S(2)}) copy-start(f32[3,2,192,256]{3,2,1,0:T(8,128)} %e_ref.3) | copy-start | bytes 3538948
  0.7 6.9 %copy-start.2 = (f32[3,256]{1,0:T(4,128)S(1)}, f32[3,256]{1,0:T(4,128)}, u32[]{:S(2)}) copy-start(f32[3,256]{1,0:T(4,128)} %amplitude_ref.1) | copy-start | bytes 9220
  0.7 6.9 %copy-start.4 = (s32[256,1]{0,1:T(1,128)S(1)}, s32[256,1]{0,1:T(1,128)}, u32[]{:S(2)}) copy-start(s32[256,1]{0,1:T(1,128)} %param.16) | copy-start | bytes 3076
  0.7 6.9 %copy-start.3 = (s32[256,1]{0,1:T(1,128)S(1)}, s32[256,1]{0,1:T(1,128)}, u32[]{:S(2)}) copy-start(s32[256,1]{0,1:T(1,128)} %param.15) | copy-start | bytes 3076
  3.2 18.8 %collective-permute-start.2 = (f32[3,192,256]{2,1,0:T(8,128)}, f32[3,192,256]{2,1,0:T(8,128)S(1)}, u32[]{:S(2)}, u32[]{:S(2)}) collective-permute-start(f32[3,192,256]{2,1,0:T(8,128)} %shard_map.121.after_hbm), channel_id=1, source_target_pairs={{1,2},{2,1},{3,4},{4,3},{5,6},{6,5},{7,8},{8,7},{9,10},{10,9},{11,... | collective-permute-start | bytes 1769480 | tf_op jit(solution)/shard_map/ppermute | solution.py:713
  10.4 11.6 %collective-permute-start = (f32[3,192,256]{2,1,0:T(8,128)}, f32[3,192,256]{2,1,0:T(8,128)}, u32[]{:S(2)}, u32[]{:S(2)}) collective-permute-start(f32[3,192,256]{2,1,0:T(8,128)} %get-tuple-element.17), channel_id=1, source_target_pairs={{0,1},{1,0},{2,3},{3,2},{4,5},{5,4},{6,7},{7,6},{8,9},{9,8},{10,11... | collective-permute-start | bytes 1769480 | tf_op jit(solution)/shard_map/ppermute | solution.py:760
  10.5 11.5 %collective-permute-start.1 = (f32[2,192,256]{2,1,0:T(8,128)}, f32[2,192,256]{2,1,0:T(8,128)}, u32[]{:S(2)}, u32[]{:S(2)}) collective-permute-start(f32[2,192,256]{2,1,0:T(8,128)} %get-tuple-element.18.near_hbm), channel_id=1, source_target_pairs={{0,1},{1,0},{2,3},{3,2},{4,5},{5,4},{6,7},{7,6},{8,9},{9,8},{10,11... | collective-permute-start | bytes 1179656 | tf_op jit(solution)/shard_map/ppermute | solution.py:760
  11.0 11.0 %all-to-all-start = ((f32[16,4,128]{2,1,0:T(4,128)}), f32[16,4,128]{2,1,0:T(4,128)S(1)}, u32[]{:S(2)}, u32[]{:S(2)}) async-start(f32[16,4,128]{2,1,0:T(4,128)} %get-tuple-element.16), calls=%async_computation | async-start | bytes 65536 | tf_op jit(solution)/shard_map/all_to_all | solution.py:747
  16.0 4.3 %copy-start.6 = (s32[3,2]{0,1:T(2,128)S(1)}, s32[3,2]{0,1:T(2,128)}, u32[]{:S(2)}) copy-start(s32[3,2]{0,1:T(2,128)} %param.19) | copy-start | bytes 76
  16.0 6.0 %copy-start.5 = (f32[2,2]{1,0:T(2,128)S(1)}, f32[2,2]{1,0:T(2,128)}, u32[]{:S(2)}) copy-start(f32[2,2]{1,0:T(2,128)} %timing_ref.1) | copy-start | bytes 52
  16.7 13.0 %collective-permute-start.3 = (f32[2,192,256]{2,1,0:T(8,128)}, f32[2,192,256]{2,1,0:T(8,128)S(1)}, u32[]{:S(2)}, u32[]{:S(2)}) collective-permute-start(f32[2,192,256]{2,1,0:T(8,128)} %shard_map.124), channel_id=1, source_target_pairs={{1,2},{2,1},{3,4},{4,3},{5,6},{6,5},{7,8},{8,7},{9,10},{10,9},{11,... | collective-permute-start | bytes 1179656 | tf_op jit(solution)/shard_map/ppermute | solution.py:758

commit v9 on v8

--- a/solution.py
+++ b/solution.py
@@ -369,13 +369,13 @@
 
 
 def inside(c, bounds_ref, z, slab, shape):
-    deep = lax.axis_index("gz") * slab + z
-    in_z = (deep >= bounds_ref[0, 0]) & (deep < bounds_ref[0, 1])
-    line = lax.broadcasted_iota(jnp.int32, shape, 0) + c.at
-    column = lax.broadcasted_iota(jnp.int32, shape, 1)
-    keep = (line >= bounds_ref[1, 0]) & (line < bounds_ref[1, 1])
-    keep = keep & (column >= bounds_ref[2, 0]) & (column < bounds_ref[2, 1])
-    return jnp.where(keep & in_z, 1.0, 0.0)
+    def between(k, at):
+        return jnp.where((at >= bounds_ref[k : k + 1, 0:1]) & (at < bounds_ref[k : k + 1, 1:2]), 1.0, 0.0)
+
+    deep = jnp.full((1, shape[1]), lax.axis_index("gz") * slab + z, jnp.int32)
+    line = lax.broadcasted_iota(jnp.int32, (shape[0], 1), 0) + c.at
+    column = lax.broadcasted_iota(jnp.int32, (1, shape[1]), 1)
+    return between(1, line) * (between(0, deep) * between(2, column))
 
 
 def middle(
@@ -436,8 +436,8 @@
     top = slab - 1
     odd = odd_device()
     has_below = jnp.where(lax.axis_index("gz") > 0, 1.0, 0.0).astype(F32)
-    wave0, wave1 = timing_ref[0, 0], timing_ref[0, 1]
-    weight0, weight1 = timing_ref[1, 0], timing_ref[1, 1]
+    wave0, wave1 = timing_ref[0:1, 0:1], timing_ref[0:1, 1:2]
+    weight0, weight1 = timing_ref[1:2, 0:1], timing_ref[1:2, 1:2]
 
     def first(c):
         chip = [c.get(chip_ref, k) for k in range(3)]
@@ -651,7 +651,7 @@
             return pl.BlockSpec(memory_space=pltpu.HBM)
         if i in anywhere:
             return pl.BlockSpec(memory_space=pl.ANY)
-        return pl.BlockSpec(memory_space=SMEM if x.size < 16 else VMEM)
+        return pl.BlockSpec(memory_space=VMEM)
 
     ins = [
         pltpu.with_memory_space_constraint(x, pltpu.HBM) if i in in_hbm else x

time: 31.3 us -> 31.3 us (level)
  waiting for transfers between devices: 2.29 us -> 2.64 us
    pallas_call x5, Pallas kernels: 14.3 us -> 14 us  [call(): pl.pallas_call(body, out_shape=outs, in_specs=[place(i, x) for i, x in en...]
    ppermute x1, waiting for transfers between devices: 0.67 us -> 1.02 us  [local(): far2 = lax.ppermute(far2, 'gz', far_pairs)]
  transfers between devices with their start and end apart: 5 -> 5, of which waited for: 2 -> 2; matrix products, arithmetic and copies ran while one was open for 0% -> 0% of each run, Pallas kernels for 34% -> 33%
where the time goes in v9:
time: 31.3 us; the launch traced here: 31 us
  Pallas kernels  14 us (45%)
  starting transfers between devices  13.4 us (43%)
  waiting for transfers between devices  2.64 us (8%)
  between operations  0.8 us (3%)
    pallas_call x5, Pallas kernels, call(): pl.pallas_call(body, out_shape=outs, in_specs=[place(i, x) for i, x in en...  14 us
    all_to_all x1, starting transfers between devices, local(): got = lax.all_to_all(packed, 'gz', 0, 0, tiled=True)  5.02 us
    ppermute x1, starting transfers between devices, local(): far1 = lax.ppermute(begun, 'gz', far_pairs)  4.29 us
    ppermute x1, starting transfers between devices, local(): far2 = lax.ppermute(far2, 'gz', far_pairs)  3.54 us
    all_to_all x1, waiting for transfers between devices, local(): got = lax.all_to_all(packed, 'gz', 0, 0, tiled=True)  1.62 us
    ppermute x1, waiting for transfers between devices, local(): far2 = lax.ppermute(far2, 'gz', far_pairs)  1.02 us
  transfers between devices with their start and end apart: 5, of which 2 were waited for; matrix products, arithmetic and copies ran while one was open for 0% of the time, Pallas kernels for 33%

profile of v9, /device:TPU:1, one launch (start us, length us, event | category | flops | bytes accessed | tf_op | source)
XLA Modules:
  0.0 31.0 jit_solution(9716195896599719399)
XLA Ops:
  0.6 0.0 copy-start.1
  0.6 0.0 copy-start
  0.7 0.0 copy-start.2
  0.7 0.0 copy-start.4
  0.7 0.0 copy-start.3
  0.7 2.5 %shard_map.121.after_hbm = f32[3,192,256]{2,1,0:T(8,128)} custom-call(f32[3,2,192,256]{3,2,1,0:T(8,128)} %e_ref.3, f32[3,2,192,256]{3,2,1,0:T(8,128)} %h_ref.3, f32[2,192,256]{2,1,0:T(8,128)} %eps_hbm.5, f32[2,192,256]{2,1,0:T(8,128)} %sigma_hbm.5), custom_call_target="tpu_custom_call" | custom-call | flops 2300000000 | tf_op jit(solution)/shard_map/pallas_call | solution.py:660
  3.2 4.3 %collective-permute-start.2 = (f32[3,192,256]{2,1,0:T(8,128)}, f32[3,192,256]{2,1,0:T(8,128)S(1)}, u32[]{:S(2)}, u32[]{:S(2)}) collective-permute-start(f32[3,192,256]{2,1,0:T(8,128)} %shard_map.121.after_hbm), channel_id=1, source_target_pairs={{1,2},{2,1},{3,4},{4,3},{5,6},{6,5},{7,8},{8,7},{9,10},{10,9},{11,... | collective-permute-start | bytes 1769480 | tf_op jit(solution)/shard_map/ppermute | solution.py:713
  7.5 0.0 copy-done.1
  7.5 0.0 copy-done
  7.6 2.8 %shard_map.122 = (f32[16,4,128]{2,1,0:T(4,128)}, f32[3,192,256]{2,1,0:T(8,128)}, f32[2,192,256]{2,1,0:T(8,128)}, f32[2,192,256]{2,1,0:T(8,128)}) custom-call(f32[3,2,192,256]{3,2,1,0:T(8,128)S(1)} %copy-done, f32[3,2,192,256]{3,2,1,0:T(8,128)S(1)} %copy-done.1, f32[2,192,256]{2,1,0:T(8,128)} %eps_hbm.5, f32[2,192,256]{2,1,0:T(8,128)} %sigma_hbm.5, ...), custom_call_target="tpu_custom_call" | custom-call | flops 3449999872 | tf_op jit(solution)/shard_map/pallas_call | solution.py:660
  10.4 0.1 collective-permute-start
  10.5 0.5 %collective-permute-start.1 = (f32[2,192,256]{2,1,0:T(8,128)}, f32[2,192,256]{2,1,0:T(8,128)}, u32[]{:S(2)}, u32[]{:S(2)}) collective-permute-start(f32[2,192,256]{2,1,0:T(8,128)} %get-tuple-element.18.near_hbm), channel_id=1, source_target_pairs={{0,1},{1,0},{2,3},{3,2},{4,5},{5,4},{6,7},{7,6},{8,9},{9,8},{10,11... | collective-permute-start | bytes 1179656 | tf_op jit(solution)/shard_map/ppermute | solution.py:760
  11.0 5.0 %all-to-all-start = ((f32[16,4,128]{2,1,0:T(4,128)}), f32[16,4,128]{2,1,0:T(4,128)S(1)}, u32[]{:S(2)}, u32[]{:S(2)}) async-start(f32[16,4,128]{2,1,0:T(4,128)} %get-tuple-element.16), calls=%async_computation | async-start | bytes 65536 | tf_op jit(solution)/shard_map/all_to_all | solution.py:747
  16.0 0.0 copy-start.5
  16.0 0.7 %shard_map.124 = f32[2,192,256]{2,1,0:T(8,128)} custom-call(f32[2,192,256]{2,1,0:T(8,128)} %get-tuple-element.18.near_hbm, f32[2,192,256]{2,1,0:T(8,128)} %get-tuple-element.25.far_hbm), custom_call_target="tpu_custom_call", output_to_operand_aliasing={{}: (1, {})} | custom-call | flops 3449999872 | tf_op jit(solution)/shard_map/pallas_call | solution.py:660
  16.7 3.5 %collective-permute-start.3 = (f32[2,192,256]{2,1,0:T(8,128)}, f32[2,192,256]{2,1,0:T(8,128)S(1)}, u32[]{:S(2)}, u32[]{:S(2)}) collective-permute-start(f32[2,192,256]{2,1,0:T(8,128)} %shard_map.124), channel_id=1, source_target_pairs={{1,2},{2,1},{3,4},{4,3},{5,6},{6,5},{7,8},{8,7},{9,10},{10,9},{11,... | collective-permute-start | bytes 1179656 | tf_op jit(solution)/shard_map/ppermute | solution.py:758
  20.3 0.1 copy.17.bounds_ref
  20.4 1.6 %all-to-all-done.got_ref = f32[16,4,128]{2,1,0:T(4,128)S(1)} async-done(((f32[16,4,128]{2,1,0:T(4,128)}), f32[16,4,128]{2,1,0:T(4,128)S(1)}, u32[]{:S(2)}, u32[]{:S(2)}) %all-to-all-start) | async-done | bytes 32800 | tf_op jit(solution)/shard_map/all_to_all | solution.py:747
  22.0 0.0 collective-permute-done.1.chip1_hbm
  22.0 0.0 collective-permute-done.2.far_hbm
  22.0 0.0 collective-permute-done.chip0_hbm
  22.0 6.7 %shard_map.123 = (f32[3,2,192,256]{3,2,1,0:T(8,128)S(1)}, f32[3,2,192,256]{3,2,1,0:T(8,128)S(1)}, f32[2,192,256]{2,1,0:T(8,128)S(1)}, f32[2,192,256]{2,1,0:T(8,1...) custom-call(f32[3,2,192,256]{3,2,1,0:T(8,128)S(1)} %copy-done, ...), custom_call_target="tpu_custom_call" | custom-call | flops 6899999744 | tf_op jit(solution)/shard_map/pallas_call | solution.py:660
  28.7 1.0 %collective-permute-done.3.far_ref = f32[2,192,256]{2,1,0:T(8,128)S(1)} collective-permute-done((f32[2,192,256]{2,1,0:T(8,128)}, f32[2,192,256]{2,1,0:T(8,128)S(1)}, u32[]{:S(2)}, u32[]{:S(2)}) %collective-permute-start.3) | collective-permute-done | bytes 393248 | tf_op jit(solution)/shard_map/ppermute | solution.py:758
  29.7 1.2 %shard_map.125 = (f32[3,2,192,256]{3,2,1,0:T(8,128)}, f32[3,2,192,256]{3,2,1,0:T(8,128)}, f32[2,192,256]{2,1,0:T(8,128)}) custom-call(f32[3,2,192,256]{3,2,1,0:T(8,128)S(1)} %get-tuple-element.19.forward_ref, f32[3,2,192,256]{3,2,1,0:T(8,128)S(1)} %get-tuple-element.20.h2_ref, ...), custom_call_target="tpu_custom_call", output_to_operand_aliasing={{0}: (7, {}), {1}: (8, {}), {2}: (9, {})} | custom-call | flops 2875000064 | tf_op jit(solution)/shard_map/pallas_call | solution.py:660
  (6 shorter events, 0.0 us)
Async XLA Ops:
  0.6 6.9 %copy-start.1 = (f32[3,2,192,256]{3,2,1,0:T(8,128)S(1)}, f32[3,2,192,256]{3,2,1,0:T(8,128)}, u32[]{:S(2)}) copy-start(f32[3,2,192,256]{3,2,1,0:T(8,128)} %h_ref.3) | copy-start | bytes 3538948
  0.6 6.9 %copy-start = (f32[3,2,192,256]{3,2,1,0:T(8,128)S(1)}, f32[3,2,192,256]{3,2,1,0:T(8,128)}, u32[]{:S(2)}) copy-start(f32[3,2,192,256]{3,2,1,0:T(8,128)} %e_ref.3) | copy-start | bytes 3538948
  0.7 6.9 %copy-start.2 = (f32[3,256]{1,0:T(4,128)S(1)}, f32[3,256]{1,0:T(4,128)}, u32[]{:S(2)}) copy-start(f32[3,256]{1,0:T(4,128)} %amplitude_ref.1) | copy-start | bytes 9220
  0.7 6.9 %copy-start.4 = (s32[256,1]{0,1:T(1,128)S(1)}, s32[256,1]{0,1:T(1,128)}, u32[]{:S(2)}) copy-start(s32[256,1]{0,1:T(1,128)} %param.16) | copy-start | bytes 3076
  0.7 6.9 %copy-start.3 = (s32[256,1]{0,1:T(1,128)S(1)}, s32[256,1]{0,1:T(1,128)}, u32[]{:S(2)}) copy-start(s32[256,1]{0,1:T(1,128)} %param.15) | copy-start | bytes 3076
  3.2 18.8 %collective-permute-start.2 = (f32[3,192,256]{2,1,0:T(8,128)}, f32[3,192,256]{2,1,0:T(8,128)S(1)}, u32[]{:S(2)}, u32[]{:S(2)}) collective-permute-start(f32[3,192,256]{2,1,0:T(8,128)} %shard_map.121.after_hbm), channel_id=1, source_target_pairs={{1,2},{2,1},{3,4},{4,3},{5,6},{6,5},{7,8},{8,7},{9,10},{10,9},{11,... | collective-permute-start | bytes 1769480 | tf_op jit(solution)/shard_map/ppermute | solution.py:713
  10.4 11.6 %collective-permute-start = (f32[3,192,256]{2,1,0:T(8,128)}, f32[3,192,256]{2,1,0:T(8,128)}, u32[]{:S(2)}, u32[]{:S(2)}) collective-permute-start(f32[3,192,256]{2,1,0:T(8,128)} %get-tuple-element.17), channel_id=1, source_target_pairs={{0,1},{1,0},{2,3},{3,2},{4,5},{5,4},{6,7},{7,6},{8,9},{9,8},{10,11... | collective-permute-start | bytes 1769480 | tf_op jit(solution)/shard_map/ppermute | solution.py:760
  10.5 11.5 %collective-permute-start.1 = (f32[2,192,256]{2,1,0:T(8,128)}, f32[2,192,256]{2,1,0:T(8,128)}, u32[]{:S(2)}, u32[]{:S(2)}) collective-permute-start(f32[2,192,256]{2,1,0:T(8,128)} %get-tuple-element.18.near_hbm), channel_id=1, source_target_pairs={{0,1},{1,0},{2,3},{3,2},{4,5},{5,4},{6,7},{7,6},{8,9},{9,8},{10,11... | collective-permute-start | bytes 1179656 | tf_op jit(solution)/shard_map/ppermute | solution.py:760
  11.0 11.0 %all-to-all-start = ((f32[16,4,128]{2,1,0:T(4,128)}), f32[16,4,128]{2,1,0:T(4,128)S(1)}, u32[]{:S(2)}, u32[]{:S(2)}) async-start(f32[16,4,128]{2,1,0:T(4,128)} %get-tuple-element.16), calls=%async_computation | async-start | bytes 65536 | tf_op jit(solution)/shard_map/all_to_all | solution.py:747
  16.0 4.3 %copy-start.6 = (s32[3,2]{0,1:T(2,128)S(1)}, s32[3,2]{0,1:T(2,128)}, u32[]{:S(2)}) copy-start(s32[3,2]{0,1:T(2,128)} %param.19) | copy-start | bytes 76
  16.0 6.0 %copy-start.5 = (f32[2,2]{1,0:T(2,128)S(1)}, f32[2,2]{1,0:T(2,128)}, u32[]{:S(2)}) copy-start(f32[2,2]{1,0:T(2,128)} %timing_ref.1) | copy-start | bytes 52
  16.7 13.0 %collective-permute-start.3 = (f32[2,192,256]{2,1,0:T(8,128)}, f32[2,192,256]{2,1,0:T(8,128)S(1)}, u32[]{:S(2)}, u32[]{:S(2)}) collective-permute-start(f32[2,192,256]{2,1,0:T(8,128)} %shard_map.124), channel_id=1, source_target_pairs={{1,2},{2,1},{3,4},{4,3},{5,6},{6,5},{7,8},{8,7},{9,10},{10,9},{11,... | collective-permute-start | bytes 1179656 | tf_op jit(solution)/shard_map/ppermute | solution.py:758
